TPU v7x, 32 devices: a whole 2x2x4 slice. The times are simulated.
32 devices in a mesh: shard: 2 (over core), tensor: 4 (over y, x), section: 4 (over z).
Axes of the slice: x: 2, y: 2, z: 4, core: 2. Of those that a mesh axis runs over, the one named last changes fastest.
Arguments:
- gradient: bfloat16 [6, 2048, 8192], P(None, ('tensor', 'section'), 'shard'), may hold values from -6 to 6
- basis: bfloat16 [6, 2048, 256], P(None, ('tensor', 'section')), may hold values from -6 to 6
- moment_m: float32 [6, 8192, 256], P(None, ('shard', 'tensor', 'section')), may hold values from -4 to 4
- moment_v: float32 [6, 8192, 256], P(None, ('shard', 'tensor', 'section')), may hold values from 0.002 to 0.02
Outputs:
- delta: bfloat16 [6, 2048, 8192], P(None, ('tensor', 'section'), 'shard')
- basis_new: bfloat16 [6, 2048, 256], P(None, ('tensor', 'section'))
- moment_m_new: float32 [6, 8192, 256], P(None, ('shard', 'tensor', 'section'))
- moment_v_new: float32 [6, 8192, 256], P(None, ('shard', 'tensor', 'section'))
All inputs are finite; a program needn't handle non-finite values. Where the computation divides by a largest or mean magnitude, that divisor is 1e-20 or more.
Results may differ from a plain program's by a relative error of at most 0.0049.
Values may be sent and summed in bfloat16 or wider, within the bound.
No kernel may reach another device: no remote copies, remote signals or barrier semaphores. Data moves between devices by JAX's collectives and lax.ppermute only.
A program may use at most 128 MiB of HBM per device.

v0:
```python
import math

import jax
import jax.numpy as jnp
from jax import lax
from jax.sharding import PartitionSpec as P

D = 2048
NS_ITERS = 4


beta_one = 0.9
beta_two = 0.999
bias_one = 1.0 - 0.9**10
bias_two = 1.0 - 0.999**10
eps_adam = 1e-08
galore_gain = 4.0


def gram_total(iterate):
    local_gram = jnp.einsum("kmr,kms->krs", iterate, iterate, precision=lax.Precision.HIGHEST)
    return lax.psum(local_gram, ("tensor", "section"))


def orthogonal(subspace):
    gram_mat = gram_total(subspace)
    row_bound = jnp.max(jnp.sum(jnp.abs(gram_mat), axis=2), axis=1)[:, None, None] + 1e-06
    iterate = subspace / jnp.sqrt(row_bound)
    gram_mat = gram_mat / row_bound
    identity = jnp.eye(gram_mat.shape[1], dtype=jnp.float32)
    for turn_index in range(NS_ITERS):
        factor = 1.5 * identity - 0.5 * gram_mat
        iterate = jnp.einsum("kmr,krs->kms", iterate, factor, precision=lax.Precision.HIGHEST)
        if turn_index + 1 < NS_ITERS:
            gram_mat = gram_total(iterate)
    return iterate


def per_device(gradient, basis, moment_m, moment_v):
    width_root = math.sqrt(D)
    partial_low = jnp.einsum("kmn,kmr->knr", gradient, basis, preferred_element_type=jnp.float32)
    low_rank = (
        lax.psum_scatter(partial_low, ("tensor", "section"), scatter_dimension=1, tiled=True)
        / width_root
    )
    moment_m_new = beta_one * moment_m + (1.0 - beta_one) * low_rank
    moment_v_new = beta_two * moment_v + (1.0 - beta_two) * low_rank * low_rank
    step_low = (moment_m_new / bias_one / (jnp.sqrt(moment_v_new / bias_two) + eps_adam)).astype(
        jnp.bfloat16
    )
    rough_low = low_rank.astype(jnp.bfloat16)
    step_block, rough_block = (
        lax.all_gather(step_low, ("tensor", "section"), axis=1, tiled=True),
        lax.all_gather(rough_low, ("tensor", "section"), axis=1, tiled=True),
    )
    delta = (
        -galore_gain
        / width_root
        * jnp.einsum("kmr,knr->kmn", basis, step_block, preferred_element_type=jnp.float32)
    ).astype(jnp.bfloat16)
    subspace = jnp.einsum("kmn,knr->kmr", gradient, rough_block, preferred_element_type=jnp.float32)
    whole_sum = lax.psum(subspace, "shard")
    basis_new = (width_root * orthogonal(whole_sum)).astype(jnp.bfloat16)
    return (delta, basis_new, moment_m_new, moment_v_new)


def solution(mesh):
    placed = (
        P(None, ("tensor", "section"), "shard"),
        P(None, ("tensor", "section"), None),
        P(None, ("shard", "tensor", "section"), None),
        P(None, ("shard", "tensor", "section"), None),
    )
    return jax.shard_map(
        per_device,
        mesh=mesh,
        in_specs=placed,
        out_specs=(
            P(None, ("tensor", "section"), "shard"),
            P(None, ("tensor", "section"), None),
            P(None, ("shard", "tensor", "section"), None),
            P(None, ("shard", "tensor", "section"), None),
        ),
        check_vma=False,
    )
```

profile of v0, /device:TPU:0, one launch (start us, length us, event | category | flops | bytes accessed | tf_op | source)
XLA Modules:
  0.0 1229.2 jit_solution(9681382425586528637)
XLA Ops:
  7.2 0.9 copy-done
  8.2 14.5 %fusion.37 = f32[6,4096,256]{2,1,0:T(8,128)} fusion(bf16[6,128,4096]{2,1,0:T(8,128)(2,1)} %param.4, bf16[6,128,256]{2,1,0:T(8,128)(2,1)S(1)} %copy-done), kind=kOutput, calls=%fused_computation.42 | convolution fusion | flops 1610612736 | bytes 31850496 | tf_op jit(solution)/shard_map/kmn,kmr->knr/dot_general | solution.py:41
  22.8 364.5 %reduce-scatter.2.cloned.1.call-done = f32[6,256,256]{2,1,0:T(8,128)} async-done(((f32[6,4096,256]{2,1,0:T(8,128)}), f32[6,256,256]{2,1,0:T(8,128)}) %reduce-scatter.2.cloned.1.call-update) | async-done | bytes 1572880 | tf_op jit(solution)/shard_map/reduce_scatter | solution.py:43
  387.3 5.1 divide_convert_fusion
  392.5 151.1 %all-gather.5.cloned.1.call-done = bf16[6,4096,256]{2,1,0:T(8,128)(2,1)} async-done(((bf16[6,256,256]{2,1,0:T(8,128)(2,1)}), bf16[6,4096,256]{2,1,0:T(8,128)(2,1)}) %all-gather.5.cloned.1.call-update) | async-done | bytes 12582928 | tf_op jit(solution)/shard_map/all_gather | solution.py:54
  543.7 9.5 convolution_bitcast_fusion
  553.3 17.5 %all-reduce.6.cloned.1.call-done = f32[6,128,256]{1,2,0:T(8,128)} async-done(((f32[6,128,256]{1,2,0:T(8,128)}), f32[6,128,256]{1,2,0:T(8,128)}) %all-reduce.6.cloned.1.call-update) | async-done | bytes 786448 | tf_op jit(solution)/shard_map/psum | solution.py:62
  570.8 3.9 fusion.38
  575.0 121.0 %all-reduce.8.cloned.1.call-done = f32[6,256,256]{2,1,0:T(8,128)} async-done(((f32[6,256,256]{2,1,0:T(8,128)}), f32[6,256,256]{2,1,0:T(8,128)}) %all-reduce.8.cloned.1.call-update) | async-done | bytes 1572880 | tf_op jit(solution)/shard_map/psum | solution.py:22
  696.0 1.7 abs_reduce_fusion
  697.8 3.1 fusion.10
  701.0 2.6 fusion.39
  703.6 116.8 %all-reduce.10.cloned.1.call-done = f32[6,256,256]{2,1,0:T(8,128)} async-done(((f32[6,256,256]{2,1,0:T(8,128)}), f32[6,256,256]{2,1,0:T(8,128)}) %all-reduce.10.cloned.1.call-update) | async-done | bytes 1572880 | tf_op jit(solution)/shard_map/psum | solution.py:22
  820.4 2.6 fusion.7
  823.0 2.6 fusion.40
  825.7 0.7 all-gather.3.cloned.1.call-update
  826.7 117.2 %all-reduce.12.cloned.1.call-done = f32[6,256,256]{2,1,0:T(8,128)} async-done(((f32[6,256,256]{2,1,0:T(8,128)}), f32[6,256,256]{2,1,0:T(8,128)}) %all-reduce.12.cloned.1.call-update) | async-done | bytes 1572880 | tf_op jit(solution)/shard_map/psum | solution.py:22
  943.8 2.6 fusion.4
  946.4 2.6 fusion.41
  949.1 149.0 %all-gather.3.cloned.1.call-done = bf16[6,4096,256]{2,1,0:T(8,128)(2,1)} async-done(((bf16[6,256,256]{2,1,0:T(8,128)(2,1)}), bf16[6,4096,256]{2,1,0:T(8,128)(2,1)}) %all-gather.3.cloned.1.call-update) | async-done | bytes 12582928 | tf_op jit(solution)/shard_map/all_gather | solution.py:53
  1098.1 10.6 fusion
  1108.7 8.6 copy.17
  1117.3 101.7 %all-reduce.14.cloned.1.call-done = f32[6,256,256]{2,1,0:T(8,128)} async-done(((f32[6,256,256]{2,1,0:T(8,128)}), f32[6,256,256]{2,1,0:T(8,128)}) %all-reduce.14.cloned.1.call-update) | async-done | bytes 1572880 | tf_op jit(solution)/shard_map/psum | solution.py:22
  1219.1 3.3 fusion.17
  (23 shorter events, 1.0 us)
Async XLA Ops:
  7.2 1.0 copy-start
  7.2 380.2 %reduce-scatter.2.cloned.1.call-start = ((), (), s32[]{:S(2)}) async-start(), calls=%async_computation.1 | async-start | bytes 26738688 | tf_op jit(solution)/shard_map/reduce_scatter | solution.py:43
  22.7 364.6 %copy-start.2 = (f32[6,256,256]{2,1,0:T(8,128)S(1)}, f32[6,256,256]{2,1,0:T(8,128)}, u32[]{:S(2)}) copy-start(f32[6,256,256]{2,1,0:T(8,128)} %param.6) | copy-start | bytes 4718596
  22.7 520.9 %all-gather.5.cloned.1.call-start = ((), (), s32[]{:S(2)}) async-start(), calls=%async_computation.3 | async-start | bytes 13369344 | tf_op jit(solution)/shard_map/all_gather | solution.py:54
  392.5 178.3 %all-reduce.6.cloned.1.call-start = ((), (), s32[]{:S(2)}) async-start(), calls=%async_computation.4 | async-start | bytes 1572864 | tf_op jit(solution)/shard_map/psum | solution.py:62
  553.2 142.8 %all-reduce.8.cloned.1.call-start = ((), (), s32[]{:S(2)}) async-start(), calls=%async_computation.5 | async-start | bytes 3145728 | tf_op jit(solution)/shard_map/psum | solution.py:22
  574.7 123.1 %copy-start.1 = (f32[6,128,256]{1,2,0:T(8,128)S(1)}, f32[6,128,256]{1,2,0:T(8,128)}, u32[]{:S(2)}) copy-start(f32[6,128,256]{1,2,0:T(8,128)} %all-reduce.6.cloned.1.call-done) | copy-start | bytes 2359300
  574.7 245.7 %all-reduce.10.cloned.1.call-start = ((), (), s32[]{:S(2)}) async-start(), calls=%async_computation.6 | async-start | bytes 3145728 | tf_op jit(solution)/shard_map/psum | solution.py:22
  703.6 240.2 %all-reduce.12.cloned.1.call-start = ((), (), s32[]{:S(2)}) async-start(), calls=%async_computation.7 | async-start | bytes 3145728 | tf_op jit(solution)/shard_map/psum | solution.py:22
  825.7 272.4 %all-gather.3.cloned.1.call-start = ((), (), s32[]{:S(2)}) async-start(), calls=%async_computation.2 | async-start | bytes 13369344 | tf_op jit(solution)/shard_map/all_gather | solution.py:53
  826.4 392.6 %all-reduce.14.cloned.1.call-start = ((), (), s32[]{:S(2)}) async-start(), calls=%async_computation.8 | async-start | bytes 3145728 | tf_op jit(solution)/shard_map/psum | solution.py:22
Sparse Core Ops, SparseCore 0:
  22.9 364.4 reduce-scatter.1
  392.6 151.0 all-gather.4
  553.3 17.3 all-reduce.5
  577.5 118.4 all-reduce.7
  703.7 116.6 all-reduce.9
  827.2 116.6 all-reduce.11
  946.6 151.4 all-gather.2
  1103.5 115.5 all-reduce.13
where the time goes:
time: 1230 us
  waiting for transfers between devices  1140 us (93%)
  matrix products  58 us (5%)
  between operations  14.2 us (1%)
    psum x4, waiting for transfers between devices, gram_total(): return lax.psum(local_gram, ('tensor', 'section'))  457 us
    reduce_scatter x1, waiting for transfers between devices, per_device(): lax.psum_scatter(partial_low, ('tensor', 'section'), scatter_dimension=1,...  365 us
    all_gather x1, waiting for transfers between devices, per_device(): lax.all_gather(rough_low, ('tensor', 'section'), axis=1, tiled=True)  151 us
    all_gather x1, waiting for transfers between devices, per_device(): lax.all_gather(step_low, ('tensor', 'section'), axis=1, tiled=True)  149 us
  transfers between devices with their start and end apart: 8, of which 8 were waited for; matrix products, arithmetic and copies ran while one was open for 2% of the time, Pallas kernels for 0%

commit v1 on v0

v1 whole, which is shorter than its diff:
```python
import functools
import math

import jax
import jax.numpy as jnp
from jax import lax
from jax.experimental import pallas as pl
from jax.experimental.pallas import tpu as pltpu
from jax.sharding import PartitionSpec as P

D = 2048
NS_ITERS = 4
CHUNKS = (2, 2, 2)
VMEM_LIMIT = 40 * 1024 * 1024

beta_one = 0.9
beta_two = 0.999
bias_one = 1.0 - 0.9**10
bias_two = 1.0 - 0.999**10
eps_adam = 1e-08
galore_gain = 4.0
width_root = math.sqrt(D)

F32 = jnp.float32
BF16 = jnp.bfloat16


def dot_tn(a, b):
    return lax.dot_general(a, b, (((0,), (0,)), ((), ())), preferred_element_type=F32)


def dot_nn(a, b):
    return lax.dot_general(a, b, (((1,), (0,)), ((), ())), preferred_element_type=F32)


def dot_nt(a, b):
    return lax.dot_general(a, b, (((1,), (1,)), ((), ())), preferred_element_type=F32)


def split(a):
    high = a.astype(BF16)
    return high, (a - high.astype(F32)).astype(BF16)


def fine(dot, a, b):
    (ah, al), (bh, bl) = a, b
    return dot(ah, bh) + (dot(ah, bl) + dot(al, bh))


def call(body, grid, prefetch, ins, outs, scratch, flops, aliases=None):
    moved = sum(math.prod(s) * jnp.dtype(d).itemsize for s, d, _, _ in outs)
    moved += sum(a.size * a.dtype.itemsize for a, b, _ in ins if b is not None)
    return pl.pallas_call(
        body,
        grid_spec=pltpu.PrefetchScalarGridSpec(
            num_scalar_prefetch=1,
            grid=grid,
            in_specs=[
                pl.BlockSpec(memory_space=pl.ANY) if b is None else pl.BlockSpec(b, m)
                for _, b, m in ins
            ],
            out_specs=[pl.BlockSpec(b, m) for _, _, b, m in outs],
            scratch_shapes=scratch,
        ),
        out_shape=[jax.ShapeDtypeStruct(s, d) for s, d, _, _ in outs],
        input_output_aliases=aliases or {},
        compiler_params=pltpu.CompilerParams(vmem_limit_bytes=VMEM_LIMIT),
        cost_estimate=pl.CostEstimate(flops=flops, bytes_accessed=moved, transcendentals=0),
    )(prefetch, *[a for a, _, _ in ins])


def low_partial(place, grads, bases, k0, kc, sections):
    rows, width = grads[0].shape[1:]
    rank = bases[0].shape[2]
    part = width // sections
    n = len(grads)

    def body(place_ref, *refs):
        g, b, out, total = refs[:n], refs[n : 2 * n], refs[2 * n : -1], refs[-1]
        acc = dot_tn(g[0][0], b[0][0])
        for m in range(1, n):
            acc += dot_tn(g[m][0], b[m][0])
        total[...] = acc
        for j in range(sections):
            at = pl.multiple_of(jnp.bitwise_xor(place_ref[1], j) * part, part)
            out[j][0] = total[pl.ds(at, part), :].astype(BF16)

    return call(
        body,
        (kc,),
        place,
        [(g, (1, rows, width), lambda i, p: (i, 0, 0)) for g in grads]
        + [(b, (1, rows, rank), lambda i, p: (k0 + i, 0, 0)) for b in bases],
        [((kc, part, rank), BF16, (1, part, rank), lambda i, p: (i, 0, 0))] * sections,
        [pltpu.VMEM((width, rank), F32)],
        2 * kc * n * rows * width * rank,
    )


def subspace_partial(place, grads, roughs, split_cores):
    kc, rows, width = grads[0].shape
    part, rank = roughs[0].shape[1:]
    n, s = len(grads), len(roughs)
    half = kc // 2

    def pick(i, p):
        if not split_cores:
            return (i, 0, 0)
        core = p[2]
        return (jnp.where(i < half, 2 * i + core, 2 * (i - half) + 1 - core), 0, 0)

    def body(place_ref, *refs):
        g, r, out, whole = refs[:n], refs[n : n + s], refs[n + s], refs[-1]
        for j in range(s):
            at = pl.multiple_of(jnp.bitwise_xor(place_ref[1], j) * part, part)
            whole[pl.ds(at, part), :] = r[j][0]
        for m in range(n):
            out[0, m] = dot_nn(g[m][0], whole[...])

    return call(
        body,
        (kc,),
        place,
        [(g, (1, rows, width), pick) for g in grads]
        + [(r, (1, part, rank), pick) for r in roughs],
        [((kc, n, rows, rank), F32, (1, n, rows, rank), lambda i, p: (i, 0, 0, 0))],
        [pltpu.VMEM((width, rank), BF16)],
        2 * kc * n * rows * width * rank,
    )[0]


def delta_parts(place, bases, steps, k0):
    kc, part, rank = steps[0].shape
    rows = bases[0].shape[1]
    n, s = len(bases), len(steps)
    width = part * s

    def body(place_ref, *refs):
        b, r, out, whole = refs[:n], refs[n : n + s], refs[n + s : -1], refs[-1]
        for j in range(s):
            at = pl.multiple_of(jnp.bitwise_xor(place_ref[1], j) * part, part)
            whole[pl.ds(at, part), :] = r[j][0]
        for m in range(n):
            out[m][0] = (-galore_gain / width_root * dot_nt(b[m][0], whole[...])).astype(BF16)

    return call(
        body,
        (kc,),
        place,
        [(b, (1, rows, rank), lambda i, p: (k0 + i, 0, 0)) for b in bases]
        + [(r, (1, part, rank), lambda i, p: (i, 0, 0)) for r in steps],
        [((kc, rows, width), BF16, (1, rows, width), lambda i, p: (i, 0, 0))] * n,
        [pltpu.VMEM((width, rank), BF16)],
        2 * kc * n * rows * width * rank,
    )


def place_delta(place, parts, before, k0, matrices):
    kc, rows, width = parts[0].shape
    n = len(parts)

    def body(place_ref, *refs):
        out = refs[-1]
        for m in range(n):
            at = pl.multiple_of(jnp.bitwise_xor(place_ref[0], m) * width, width)
            out[0, :, pl.ds(at, width)] = refs[m][0]

    ins = [(p, (1, rows, width), lambda i, p: (i, 0, 0)) for p in parts]
    aliases = {}
    if before is not None:
        ins.append((before, None, None))
        aliases = {n + 1: 0}
    return call(
        body,
        (kc,),
        place,
        ins,
        [
            (
                (matrices, rows, n * width),
                BF16,
                (1, rows, n * width),
                lambda i, p: (k0 + i, 0, 0),
            )
        ],
        [],
        0,
        aliases,
    )[0]


def gram_parts(place, groups):
    n = len(groups[0])
    rows, rank = groups[0][0].shape[1:]
    counts = [g[0].shape[0] for g in groups]
    total = sum(counts)
    part = rank // n
    flat = [p for g in groups for p in g]

    def body(place_ref, *refs):
        pieces, sub, out, whole = refs[: len(flat)], refs[len(flat)], refs[len(flat) + 1 : -1], refs[-1]
        at = 0
        for j, count in enumerate(counts):
            for i in range(count):
                acc = pieces[j * n][i]
                for m in range(1, n):
                    acc += pieces[j * n + m][i]
                sub[at] = acc
                high = split(acc)
                whole[at] = fine(dot_tn, high, high)
                at += 1
        for m in range(n):
            start = pl.multiple_of(jnp.bitwise_xor(place_ref[0], m) * part, part)
            for i in range(total):
                out[m][i] = whole[i, pl.ds(start, part), :]

    zero3 = lambda i, p: (0, 0, 0)
    res = call(
        body,
        (1,),
        place,
        [(p, p.shape, zero3) for p in flat],
        [((total, rows, rank), F32, (total, rows, rank), zero3)]
        + [((total, part, rank), F32, (total, part, rank), zero3)] * n,
        [pltpu.VMEM((total, rank, rank), F32)],
        6 * total * rows * rank * rank,
    )
    return res[0], res[1:]


def newton_schulz(place, pieces, sub):
    n = len(pieces)
    total, rows, rank = sub.shape
    part = rank // n

    def body(place_ref, *refs):
        p, s, out, whole = refs[:n], refs[n], refs[n + 1], refs[-1]
        for m in range(n):
            start = pl.multiple_of(jnp.bitwise_xor(place_ref[0], m) * part, part)
            for i in range(total):
                whole[i, pl.ds(start, part), :] = p[m][i]
        row = lax.broadcasted_iota(jnp.int32, (rank, rank), 0)
        col = lax.broadcasted_iota(jnp.int32, (rank, rank), 1)
        eye = jnp.where(row == col, 1.0, 0.0).astype(F32)
        iters, grams, prods = [], [], []
        for i in range(total):
            gram = whole[i]
            bound = jnp.max(jnp.sum(jnp.abs(gram), axis=1, keepdims=True), axis=0, keepdims=True) + 1e-06
            iters.append(s[i] / jnp.sqrt(bound))
            grams.append(gram / bound)
            prods.append(None)
        for turn in range(NS_ITERS):
            for i in range(total):
                factor = 1.5 * eye - 0.5 * grams[i]
                f = split(factor)
                prods[i] = factor if turn == 0 else fine(dot_nn, split(prods[i]), f)
                if turn + 1 < NS_ITERS:
                    half = fine(dot_nn, split(grams[i]), f)
                    grams[i] = fine(dot_nn, split(half), f)
        for i in range(total):
            res = fine(dot_nn, split(iters[i]), split(prods[i]))
            out[i] = (width_root * res).astype(BF16)

    zero3 = lambda i, p: (0, 0, 0)
    return call(
        body,
        (1,),
        place,
        [(p, p.shape, zero3) for p in pieces] + [(sub, sub.shape, zero3)],
        [((total, rows, rank), BF16, (total, rows, rank), zero3)],
        [pltpu.VMEM((total, rank, rank), F32)],
        60 * total * rank * rank * rank,
    )[0]


def per_device(shape, gradient, basis, moment_m, moment_v):
    tensors, sections, cores = shape["tensor"], shape["section"], shape["shard"]
    t, z, c = (lax.axis_index(a) for a in ("tensor", "section", "shard"))
    place = jnp.stack([t, z, c]).astype(jnp.int32)
    matrices, rows, columns = gradient.shape
    width = columns // tensors
    split_cores = cores == 2

    def swap(x, axis, m):
        return lax.ppermute(x, axis, [(i, i ^ m) for i in range(shape[axis])])

    def other_core(x):
        return lax.ppermute(x, "shard", [(0, 1), (1, 0)])

    if split_cores:
        mine = lax.dynamic_slice_in_dim(basis, c * (matrices // 2), matrices // 2, 0)
        got = jnp.stack([swap(mine, "tensor", m) for m in range(1, tensors)])
        theirs = other_core(got)
        first = jnp.where(c == 0, got, theirs)
        second = jnp.where(c == 0, theirs, got)
        bases = [basis] + [
            jnp.concatenate([first[m], second[m]], 0) for m in range(tensors - 1)
        ]
    else:
        bases = [basis] + [swap(basis, "tensor", m) for m in range(1, tensors)]

    starts = [sum(CHUNKS[:j]) for j in range(len(CHUNKS))]
    grads, lows = [], []
    for k0, kc in zip(starts, CHUNKS):
        cut = [
            lax.dynamic_slice(gradient, (k0, 0, (t ^ m) * width), (kc, rows, width))
            for m in range(tensors)
        ]
        grads.append([cut[0]] + [swap(cut[m], "tensor", m) for m in range(1, tensors)])

    m_news, v_news, steps, groups = [], [], [], []
    for j, (k0, kc) in enumerate(zip(starts, CHUNKS)):
        parts = low_partial(place, grads[j], bases, k0, kc, sections)
        total = parts[0].astype(F32)
        for m in range(1, sections):
            total += swap(parts[m], "section", m).astype(F32)
        low_rank = total / width_root
        m_new = beta_one * moment_m[k0 : k0 + kc] + (1.0 - beta_one) * low_rank
        v_new = beta_two * moment_v[k0 : k0 + kc] + (1.0 - beta_two) * low_rank * low_rank
        step_low = (m_new / bias_one / (jnp.sqrt(v_new / bias_two) + eps_adam)).astype(BF16)
        rough_low = low_rank.astype(BF16)
        m_news.append(m_new)
        v_news.append(v_new)
        roughs = [rough_low] + [swap(rough_low, "section", m) for m in range(1, sections)]
        steps.append([step_low] + [swap(step_low, "section", m) for m in range(1, sections)])
        sub = subspace_partial(place, grads[j], roughs, split_cores)
        if split_cores:
            half = kc // 2
            sub = sub[:half] + other_core(sub[half:])
        else:
            sub = lax.psum(sub, "shard")
        groups.append([sub[:, 0]] + [swap(sub[:, m], "tensor", m) for m in range(1, tensors)])

    sub, cut = gram_parts(place, groups)
    gram = cut[0]
    for m in range(1, tensors):
        gram = gram + swap(cut[m], "tensor", m)
    pieces = [gram] + [swap(gram, "section", m) for m in range(1, sections)]
    gram = functools.reduce(jnp.add, pieces)
    pieces = [gram] + [swap(gram, "tensor", m) for m in range(1, tensors)]
    done = newton_schulz(place, pieces, sub)
    if split_cores:
        theirs = other_core(done)
        even = jnp.where(c == 0, done, theirs)
        odd = jnp.where(c == 0, theirs, done)
        basis_new = jnp.stack([even, odd], 1).reshape(basis.shape)
    else:
        basis_new = done

    delta = None
    for j, k0 in enumerate(starts):
        cut = delta_parts(place, bases, steps[j], k0)
        parts = [cut[0]] + [swap(cut[m], "tensor", m) for m in range(1, tensors)]
        delta = place_delta(place, parts, delta, k0, matrices)

    return (delta, basis_new, jnp.concatenate(m_news, 0), jnp.concatenate(v_news, 0))


def solution(mesh):
    placed = (
        P(None, ("tensor", "section"), "shard"),
        P(None, ("tensor", "section"), None),
        P(None, ("shard", "tensor", "section"), None),
        P(None, ("shard", "tensor", "section"), None),
    )
    return jax.shard_map(
        functools.partial(per_device, dict(mesh.shape)),
        mesh=mesh,
        in_specs=placed,
        out_specs=placed,
        check_vma=False,
    )
```

time: 1230 us -> 373 us (0.30)
  waiting for transfers between devices: 1140 us -> 193 us
  starting transfers between devices: 0.73 us -> 132 us
  matrix products: 58 us -> 0 us
  Pallas kernels: 0 us -> 32.3 us
  between operations: 14.2 us -> 1 us
    psum x5 -> x0, waiting for transfers between devices: 474 us -> none  [the longest x4 457 us: gram_total(): return lax.psum(local_gram, ('tensor', 'section'))]
    reduce_scatter x1 -> x0, waiting for transfers between devices: 365 us -> none  [per_device(): lax.psum_scatter(partial_low, ('tensor', 'section'), scatter_dimension=1,...]
    all_gather x2 -> x0, waiting for transfers between devices: 300 us -> none  [the longest x1 151 us: per_device(): lax.all_gather(rough_low, ('tensor', 'section'), axis=1, tiled=True)]
    ppermute x0 -> x71, waiting for transfers between devices: none -> 193 us  [the longest x66 193 us: swap(): return lax.ppermute(x, axis, [(i, i ^ m) for i in range(shape[axis])])]
    ppermute x0 -> x71, starting transfers between devices: none -> 132 us  [the longest x66 131 us: swap(): return lax.ppermute(x, axis, [(i, i ^ m) for i in range(shape[axis])])]
    dot_general x11 -> x0, matrix products: 58 us -> none  [the longest x1 14.5 us: per_device(): jnp.einsum('kmn,kmr->knr', gradient, basis, preferred_element_type=jnp.fl...]
    pallas_call x0 -> x14, Pallas kernels: none -> 32.3 us  [call(): pl.pallas_call(body, grid_spec=pltpu.PrefetchScalarGridSpec(num_scalar_pr...]
  transfers between devices with their start and end apart: 8 -> 71, of which waited for: 8 -> 29; matrix products, arithmetic and copies ran while one was open for 2% -> 3% of each run, Pallas kernels for 0% -> 9%
where the time goes in v1:
time: 373 us; the launch traced here: 372 us
  waiting for transfers between devices  193 us (52%)
  starting transfers between devices  132 us (35%)
  Pallas kernels  32.3 us (9%)
  other arithmetic  7.81 us (2%)
  local copies, waits for them, and re-layouts  7.11 us (2%)
    ppermute x66, waiting for transfers between devices, swap(): return lax.ppermute(x, axis, [(i, i ^ m) for i in range(shape[axis])])  193 us
    ppermute x66, starting transfers between devices, swap(): return lax.ppermute(x, axis, [(i, i ^ m) for i in range(shape[axis])])  131 us
    pallas_call x14, Pallas kernels, call(): pl.pallas_call(body, grid_spec=pltpu.PrefetchScalarGridSpec(num_scalar_pr...  32.3 us
  transfers between devices with their start and end apart: 71, of which 29 were waited for; matrix products, arithmetic and copies ran while one was open for 3% of the time, Pallas kernels for 9%

profile of v1, /device:TPU:0, one launch (start us, length us, event | category | flops | bytes accessed | tf_op | source)
XLA Modules:
  0.0 372.4 jit_solution(6944285194510511890)
XLA Ops:
  10.3 4.8 %collective-permute-done.1 = bf16[3,128,256]{2,1,0:T(8,128)(2,1)S(1)} collective-permute-done((bf16[3,128,256]{2,1,0:T(8,128)(2,1)S(1)}, bf16[3,128,256]{2,1,0:T(8,128)(2,1)S(1)}, u32[]{:S(2)}, u32[]{:S(2)}) %collective-permute-start.1) | collective-permute-done | bytes 196640 | tf_op jit(solution)/shard_map/ppermute | solution.py:285
  17.0 5.1 %constant_dynamic-slice_fusion = (bf16[2,128,1024]{2,1,0:T(8,128)(2,1)}, bf16[2,128,1024]{2,1,0:T(8,128)(2,1)}, bf16[2,128,1024]{2,1,0:T(8,128)(2,1)S(1)}, bf16[...) fusion(bf16[6,128,4096]{2,1,0:T(8,128)(2,1)} %param.4, ...), kind=kLoop, calls=%fused_computation.49 | loop fusion | bytes 12582928 | tf_op jit(solution)/shard_map/dynamic_slice | solution.py:306
  28.9 8.1 %collective-permute-done.16.refs_1_ = bf16[2,128,1024]{2,1,0:T(8,128)(2,1)S(1)} collective-permute-done((bf16[2,128,1024]{2,1,0:T(8,128)(2,1)}, bf16[2,128,1024]{2,1,0:T(8,128)(2,1)S(1)}, u32[]{:S(2)}, u32[]{:S(2)}) %collective-permute-start.16) | collective-permute-done | bytes 524320 | tf_op jit(solution)/shard_map/ppermute | solution.py:285
  38.5 11.1 %collective-permute-done.17.refs_2_ = bf16[2,128,1024]{2,1,0:T(8,128)(2,1)S(1)} collective-permute-done((bf16[2,128,1024]{2,1,0:T(8,128)(2,1)}, bf16[2,128,1024]{2,1,0:T(8,128)(2,1)S(1)}, u32[]{:S(2)}, u32[]{:S(2)}) %collective-permute-start.17) | collective-permute-done | bytes 524320 | tf_op jit(solution)/shard_map/ppermute | solution.py:285
  52.0 7.6 %collective-permute-done.4.refs_1_ = bf16[2,128,1024]{2,1,0:T(8,128)(2,1)} collective-permute-done((bf16[2,128,1024]{2,1,0:T(8,128)(2,1)}, bf16[2,128,1024]{2,1,0:T(8,128)(2,1)}, u32[]{:S(2)}, u32[]{:S(2)}) %collective-permute-start.4) | collective-permute-done | bytes 524320 | tf_op jit(solution)/shard_map/ppermute | solution.py:285
  63.4 8.7 %collective-permute-done.5.refs_2_ = bf16[2,128,1024]{2,1,0:T(8,128)(2,1)S(1)} collective-permute-done((bf16[2,128,1024]{2,1,0:T(8,128)(2,1)}, bf16[2,128,1024]{2,1,0:T(8,128)(2,1)S(1)}, u32[]{:S(2)}, u32[]{:S(2)}) %collective-permute-start.5) | collective-permute-done | bytes 524320 | tf_op jit(solution)/shard_map/ppermute | solution.py:285
  85.6 8.2 %collective-permute-done.30.refs_3_ = bf16[2,128,1024]{2,1,0:T(8,128)(2,1)S(1)} collective-permute-done((bf16[2,128,1024]{2,1,0:T(8,128)(2,1)S(1)}, bf16[2,128,1024]{2,1,0:T(8,128)(2,1)S(1)}, u32[]{:S(2)}, u32[]{:S(2)}) %collective-permute-start.30) | collective-permute-done | bytes 524320 | tf_op jit(solution)/shard_map/ppermute | solution.py:285
  104.4 11.8 %collective-permute-done.8 = bf16[2,256,256]{2,1,0:T(8,128)(2,1)S(1)} collective-permute-done((bf16[2,256,256]{2,1,0:T(8,128)(2,1)S(1)}, bf16[2,256,256]{2,1,0:T(8,128)(2,1)S(1)}, u32[]{:S(2)}, u32[]{:S(2)}) %collective-permute-start.8) | collective-permute-done | bytes 262176 | tf_op jit(solution)/shard_map/ppermute | solution.py:285
  117.5 20.0 %collective-permute-done.32 = bf16[2,256,256]{2,1,0:T(8,128)(2,1)S(1)} collective-permute-done((bf16[2,256,256]{2,1,0:T(8,128)(2,1)S(1)}, bf16[2,256,256]{2,1,0:T(8,128)(2,1)S(1)}, u32[]{:S(2)}, u32[]{:S(2)}) %collective-permute-start.32) | collective-permute-done | bytes 262176 | tf_op jit(solution)/shard_map/ppermute | solution.py:285
  139.1 5.3 %collective-permute-start.54 = (bf16[2,256,256]{2,1,0:T(8,128)(2,1)S(1)}, bf16[2,256,256]{2,1,0:T(8,128)(2,1)S(1)}, u32[]{:S(2)}, u32[]{:S(2)}) collective-permute-start(bf16[2,256,256]{2,1,0:T(8,128)(2,1)S(1)} %get-tuple-element.92.refs_4_), channel_id=1, source_target_pairs={{0,1},{1,0},{2,3},{3,2},{4,5},{5,4},{6,7},{7,6},{8,9},{9,8},{10,11... | collective-permute-start | bytes 786440 | tf_op jit(solution)/shard_map/ppermute | solution.py:285
  150.8 6.1 %collective-permute-done.54.refs_5_ = bf16[2,256,256]{2,1,0:T(8,128)(2,1)S(1)} collective-permute-done((bf16[2,256,256]{2,1,0:T(8,128)(2,1)S(1)}, bf16[2,256,256]{2,1,0:T(8,128)(2,1)S(1)}, u32[]{:S(2)}, u32[]{:S(2)}) %collective-permute-start.54) | collective-permute-done | bytes 262176 | tf_op jit(solution)/shard_map/ppermute | solution.py:285
  156.9 8.4 %collective-permute-done.55.refs_6_ = bf16[2,256,256]{2,1,0:T(8,128)(2,1)S(1)} collective-permute-done((bf16[2,256,256]{2,1,0:T(8,128)(2,1)S(1)}, bf16[2,256,256]{2,1,0:T(8,128)(2,1)S(1)}, u32[]{:S(2)}, u32[]{:S(2)}) %collective-permute-start.55) | collective-permute-done | bytes 262176 | tf_op jit(solution)/shard_map/ppermute | solution.py:285
  171.9 16.5 %collective-permute-start.40 = (bf16[2,256,256]{2,1,0:T(8,128)(2,1)S(1)}, bf16[2,256,256]{2,1,0:T(8,128)(2,1)S(1)}, u32[]{:S(2)}, u32[]{:S(2)}) collective-permute-start(bf16[2,256,256]{2,1,0:T(8,128)(2,1)S(1)} %get-tuple-element.93.refs_4_), channel_id=1, source_target_pairs={{0,1},{1,0},{2,3},{3,2},{4,5},{5,4},{6,7},{7,6},{8,9},{9,8},{10,11... | collective-permute-start | bytes 786440 | tf_op jit(solution)/shard_map/ppermute | solution.py:285
  190.8 4.8 %collective-permute-start.34 = (bf16[2,256,256]{2,1,0:T(8,128)(2,1)S(1)}, bf16[2,256,256]{2,1,0:T(8,128)(2,1)S(1)}, u32[]{:S(2)}, u32[]{:S(2)}) collective-permute-start(bf16[2,256,256]{2,1,0:T(8,128)(2,1)S(1)} %get-tuple-element.62.refs_4_), channel_id=1, source_target_pairs={{0,1},{1,0},{2,3},{3,2},{4,5},{5,4},{6,7},{7,6},{8,9},{9,8},{10,11... | collective-permute-start | bytes 786440 | tf_op jit(solution)/shard_map/ppermute | solution.py:285
  198.7 13.2 %collective-permute-done.41.refs_6_ = bf16[2,256,256]{2,1,0:T(8,128)(2,1)S(1)} collective-permute-done((bf16[2,256,256]{2,1,0:T(8,128)(2,1)S(1)}, bf16[2,256,256]{2,1,0:T(8,128)(2,1)S(1)}, u32[]{:S(2)}, u32[]{:S(2)}) %collective-permute-start.41) | collective-permute-done | bytes 262176 | tf_op jit(solution)/shard_map/ppermute | solution.py:285
  237.3 10.5 %collective-permute-start.22 = (bf16[2,256,256]{2,1,0:T(8,128)(2,1)S(1)}, bf16[2,256,256]{2,1,0:T(8,128)(2,1)S(1)}, u32[]{:S(2)}, u32[]{:S(2)}) collective-permute-start(bf16[2,256,256]{2,1,0:T(8,128)(2,1)S(1)} %get-tuple-element.86.refs_4_), channel_id=1, source_target_pairs={{0,1},{1,0},{2,3},{3,2},{4,5},{5,4},{6,7},{7,6},{8,9},{9,8},{10,11... | collective-permute-start | bytes 786440 | tf_op jit(solution)/shard_map/ppermute | solution.py:285
  262.9 13.9 %collective-permute-done.23.refs_6_ = bf16[2,256,256]{2,1,0:T(8,128)(2,1)S(1)} collective-permute-done((bf16[2,256,256]{2,1,0:T(8,128)(2,1)S(1)}, bf16[2,256,256]{2,1,0:T(8,128)(2,1)S(1)}, u32[]{:S(2)}, u32[]{:S(2)}) %collective-permute-start.23) | collective-permute-done | bytes 262176 | tf_op jit(solution)/shard_map/ppermute | solution.py:285
  276.8 12.4 %collective-permute-start.65 = (f32[3,64,256]{2,1,0:T(8,128)S(1)}, f32[3,64,256]{2,1,0:T(8,128)S(1)}, u32[]{:S(2)}, u32[]{:S(2)}) collective-permute-start(f32[3,64,256]{2,1,0:T(8,128)S(1)} %add_add_fusion.1), channel_id=1, source_target_pairs={{0,2},{1,3},{2,0},{3,1},{4,6},{5,7},{6,4},{7,5},{8,10},{9,11},{10,... | collective-permute-start | bytes 589832 | tf_op jit(solution)/shard_map/ppermute | solution.py:285
  305.3 6.2 %collective-permute-done.65 = f32[3,64,256]{2,1,0:T(8,128)S(1)} collective-permute-done((f32[3,64,256]{2,1,0:T(8,128)S(1)}, f32[3,64,256]{2,1,0:T(8,128)S(1)}, u32[]{:S(2)}, u32[]{:S(2)}) %collective-permute-start.65) | collective-permute-done | bytes 196640 | tf_op jit(solution)/shard_map/ppermute | solution.py:285
  314.0 5.5 %collective-permute-done.38.refs_2_ = bf16[2,128,1024]{2,1,0:T(8,128)(2,1)S(1)} collective-permute-done((bf16[2,128,1024]{2,1,0:T(8,128)(2,1)S(1)}, bf16[2,128,1024]{2,1,0:T(8,128)(2,1)S(1)}, u32[]{:S(2)}, u32[]{:S(2)}) %collective-permute-start.38) | collective-permute-done | bytes 524320 | tf_op jit(solution)/shard_map/ppermute | solution.py:285
  323.5 6.4 %collective-permute-done.25.refs_1_ = bf16[2,128,1024]{2,1,0:T(8,128)(2,1)S(1)} collective-permute-done((bf16[2,128,1024]{2,1,0:T(8,128)(2,1)S(1)}, bf16[2,128,1024]{2,1,0:T(8,128)(2,1)S(1)}, u32[]{:S(2)}, u32[]{:S(2)}) %collective-permute-start.25) | collective-permute-done | bytes 524320 | tf_op jit(solution)/shard_map/ppermute | solution.py:285
  334.5 14.2 %collective-permute-done.68.refs_2_ = f32[3,64,256]{2,1,0:T(8,128)S(1)} collective-permute-done((f32[3,64,256]{2,1,0:T(8,128)S(1)}, f32[3,64,256]{2,1,0:T(8,128)S(1)}, u32[]{:S(2)}, u32[]{:S(2)}) %collective-permute-start.68) | collective-permute-done | bytes 196640 | tf_op jit(solution)/shard_map/ppermute | solution.py:285
  349.4 5.1 %shard_map.88 = bf16[3,128,256]{2,1,0:T(8,128)(2,1)S(1)} custom-call(s32[3]{0:T(128)S(1)} %pad_add_fusion.place_ref, f32[3,64,256]{2,1,0:T(8,128)S(1)} %add_add_fusion.refs_0_, f32[3,64,256]{2,1,0:T(8,128)S(1)} %collective-permute-done.67.refs_1_, f32[3,64,256]{2,1,0:T(8,128)S(1)} %collective-permute-done.68.refs_2_, ...), custom_call_target="tpu_custom_call" | custom-call | flops 3019898880 | bytes 1376256 | tf_op jit(solution)/shard_map/pallas_call | solution.py:53
  361.2 8.4 %collective-permute-done.14.refs_2_ = bf16[2,128,1024]{2,1,0:T(8,128)(2,1)S(1)} collective-permute-done((bf16[2,128,1024]{2,1,0:T(8,128)(2,1)S(1)}, bf16[2,128,1024]{2,1,0:T(8,128)(2,1)S(1)}, u32[]{:S(2)}, u32[]{:S(2)}) %collective-permute-start.14) | collective-permute-done | bytes 524320 | tf_op jit(solution)/shard_map/ppermute | solution.py:285
  (172 shorter events, 148.9 us)
Async XLA Ops:
  25.5 34.1 %collective-permute-start.4 = (bf16[2,128,1024]{2,1,0:T(8,128)(2,1)}, bf16[2,128,1024]{2,1,0:T(8,128)(2,1)}, u32[]{:S(2)}, u32[]{:S(2)}) collective-permute-start(bf16[2,128,1024]{2,1,0:T(8,128)(2,1)} %get-tuple-element.80), channel_id=1, source_target_pairs={{0,4},{4,0},{8,12},{12,8},{1,5},{5,1},{9,13},{13,9},{2,6},{6,2},{1... | collective-permute-start | bytes 1572872 | tf_op jit(solution)/shard_map/ppermute | solution.py:285
  26.9 45.1 %collective-permute-start.5 = (bf16[2,128,1024]{2,1,0:T(8,128)(2,1)}, bf16[2,128,1024]{2,1,0:T(8,128)(2,1)S(1)}, u32[]{:S(2)}, u32[]{:S(2)}) collective-permute-start(bf16[2,128,1024]{2,1,0:T(8,128)(2,1)} %get-tuple-element.79), channel_id=1, source_target_pairs={{0,8},{4,12},{8,0},{12,4},{1,9},{5,13},{9,1},{13,5},{2,10},{6,14},... | collective-permute-start | bytes 1572872 | tf_op jit(solution)/shard_map/ppermute | solution.py:285
  37.0 36.7 %collective-permute-start.6 = (bf16[2,128,1024]{2,1,0:T(8,128)(2,1)S(1)}, bf16[2,128,1024]{2,1,0:T(8,128)(2,1)S(1)}, u32[]{:S(2)}, u32[]{:S(2)}) collective-permute-start(bf16[2,128,1024]{2,1,0:T(8,128)(2,1)S(1)} %copy-done.6), channel_id=1, source_target_pairs={{0,12},{4,8},{8,4},{12,0},{1,13},{5,9},{9,5},{13,1},{2,14},{6,10},... | collective-permute-start | bytes 1572872 | tf_op jit(solution)/shard_map/ppermute | solution.py:285
  49.6 32.4 %collective-permute-start.28 = (bf16[2,128,1024]{2,1,0:T(8,128)(2,1)S(1)}, bf16[2,128,1024]{2,1,0:T(8,128)(2,1)S(1)}, u32[]{:S(2)}, u32[]{:S(2)}) collective-permute-start(bf16[2,128,1024]{2,1,0:T(8,128)(2,1)S(1)} %copy-done.5), channel_id=1, source_target_pairs={{0,4},{4,0},{8,12},{12,8},{1,5},{5,1},{9,13},{13,9},{2,6},{6,2},{1... | collective-permute-start | bytes 1572872 | tf_op jit(solution)/shard_map/ppermute | solution.py:285
  50.3 35.3 %collective-permute-start.29 = (bf16[2,128,1024]{2,1,0:T(8,128)(2,1)S(1)}, bf16[2,128,1024]{2,1,0:T(8,128)(2,1)S(1)}, u32[]{:S(2)}, u32[]{:S(2)}) collective-permute-start(bf16[2,128,1024]{2,1,0:T(8,128)(2,1)S(1)} %copy-done.4), channel_id=1, source_target_pairs={{0,8},{4,12},{8,0},{12,4},{1,9},{5,13},{9,1},{13,5},{2,10},{6,14},... | collective-permute-start | bytes 1572872 | tf_op jit(solution)/shard_map/ppermute | solution.py:285
  59.6 34.2 %collective-permute-start.30 = (bf16[2,128,1024]{2,1,0:T(8,128)(2,1)S(1)}, bf16[2,128,1024]{2,1,0:T(8,128)(2,1)S(1)}, u32[]{:S(2)}, u32[]{:S(2)}) collective-permute-start(bf16[2,128,1024]{2,1,0:T(8,128)(2,1)S(1)} %copy-done.3), channel_id=1, source_target_pairs={{0,12},{4,8},{8,4},{12,0},{1,13},{5,9},{9,5},{13,1},{2,14},{6,10},... | collective-permute-start | bytes 1572872 | tf_op jit(solution)/shard_map/ppermute | solution.py:285
  72.0 26.5 %collective-permute-start.19 = (bf16[2,256,256]{2,1,0:T(8,128)(2,1)S(1)}, bf16[2,256,256]{2,1,0:T(8,128)(2,1)S(1)}, u32[]{:S(2)}, u32[]{:S(2)}) collective-permute-start(bf16[2,256,256]{2,1,0:T(8,128)(2,1)S(1)} %get-tuple-element.42), channel_id=1, source_target_pairs={{0,1},{1,0},{2,3},{3,2},{4,5},{5,4},{6,7},{7,6},{8,9},{9,8},{10,11... | collective-permute-start | bytes 786440 | tf_op jit(solution)/shard_map/ppermute | solution.py:285
  73.6 26.4 %collective-permute-start.20 = (bf16[2,256,256]{2,1,0:T(8,128)(2,1)S(1)}, bf16[2,256,256]{2,1,0:T(8,128)(2,1)S(1)}, u32[]{:S(2)}, u32[]{:S(2)}) collective-permute-start(bf16[2,256,256]{2,1,0:T(8,128)(2,1)S(1)} %get-tuple-element.43), channel_id=1, source_target_pairs={{0,2},{1,3},{2,0},{3,1},{4,6},{5,7},{6,4},{7,5},{8,10},{9,11},{10,... | collective-permute-start | bytes 786440 | tf_op jit(solution)/shard_map/ppermute | solution.py:285
  100.3 37.2 %collective-permute-start.32 = (bf16[2,256,256]{2,1,0:T(8,128)(2,1)S(1)}, bf16[2,256,256]{2,1,0:T(8,128)(2,1)S(1)}, u32[]{:S(2)}, u32[]{:S(2)}) collective-permute-start(bf16[2,256,256]{2,1,0:T(8,128)(2,1)S(1)} %get-tuple-element.51), channel_id=1, source_target_pairs={{0,2},{1,3},{2,0},{3,1},{4,6},{5,7},{6,4},{7,5},{8,10},{9,11},{10,... | collective-permute-start | bytes 786440 | tf_op jit(solution)/shard_map/ppermute | solution.py:285
  103.1 34.5 %collective-permute-start.33 = (bf16[2,256,256]{2,1,0:T(8,128)(2,1)S(1)}, bf16[2,256,256]{2,1,0:T(8,128)(2,1)S(1)}, u32[]{:S(2)}, u32[]{:S(2)}) collective-permute-start(bf16[2,256,256]{2,1,0:T(8,128)(2,1)S(1)} %get-tuple-element.52), channel_id=1, source_target_pairs={{0,3},{1,2},{2,1},{3,0},{4,7},{5,6},{6,5},{7,4},{8,11},{9,10},{10,... | collective-permute-start | bytes 786440 | tf_op jit(solution)/shard_map/ppermute | solution.py:285
  147.8 40.6 %collective-permute-start.47 = (bf16[2,256,256]{2,1,0:T(8,128)(2,1)S(1)}, bf16[2,256,256]{2,1,0:T(8,128)(2,1)S(1)}, u32[]{:S(2)}, u32[]{:S(2)}) collective-permute-start(bf16[2,256,256]{2,1,0:T(8,128)(2,1)S(1)} %get-tuple-element.91.refs_4_), channel_id=1, source_target_pairs={{0,1},{1,0},{2,3},{3,2},{4,5},{5,4},{6,7},{7,6},{8,9},{9,8},{10,11... | collective-permute-start | bytes 786440 | tf_op jit(solution)/shard_map/ppermute | solution.py:285
  148.4 40.1 %collective-permute-start.48 = (bf16[2,256,256]{2,1,0:T(8,128)(2,1)S(1)}, bf16[2,256,256]{2,1,0:T(8,128)(2,1)S(1)}, u32[]{:S(2)}, u32[]{:S(2)}) collective-permute-start(bf16[2,256,256]{2,1,0:T(8,128)(2,1)S(1)} %get-tuple-element.91.refs_4_), channel_id=1, source_target_pairs={{0,2},{1,3},{2,0},{3,1},{4,6},{5,7},{6,4},{7,5},{8,10},{9,11},{10,... | collective-permute-start | bytes 786440 | tf_op jit(solution)/shard_map/ppermute | solution.py:285
  168.8 45.3 %collective-permute-start.57 = (f32[1,4,128,256]{3,2,1,0:T(8,128)S(1)}, f32[1,4,128,256]{3,2,1,0:T(8,128)S(1)}, u32[]{:S(2)}, u32[]{:S(2)}) collective-permute-start(f32[1,4,128,256]{3,2,1,0:T(8,128)S(1)} %slice.139), channel_id=1, source_target_pairs={{0,16},{16,0},{1,17},{17,1},{2,18},{18,2},{3,19},{19,3},{4,20},{20... | collective-permute-start | bytes 1572872 | tf_op jit(solution)/shard_map/ppermute | solution.py:288
  190.8 61.4 %collective-permute-start.34 = (bf16[2,256,256]{2,1,0:T(8,128)(2,1)S(1)}, bf16[2,256,256]{2,1,0:T(8,128)(2,1)S(1)}, u32[]{:S(2)}, u32[]{:S(2)}) collective-permute-start(bf16[2,256,256]{2,1,0:T(8,128)(2,1)S(1)} %get-tuple-element.62.refs_4_), channel_id=1, source_target_pairs={{0,1},{1,0},{2,3},{3,2},{4,5},{5,4},{6,7},{7,6},{8,9},{9,8},{10,11... | collective-permute-start | bytes 786440 | tf_op jit(solution)/shard_map/ppermute | solution.py:285
  197.2 55.0 %collective-permute-start.35 = (bf16[2,256,256]{2,1,0:T(8,128)(2,1)S(1)}, bf16[2,256,256]{2,1,0:T(8,128)(2,1)S(1)}, u32[]{:S(2)}, u32[]{:S(2)}) collective-permute-start(bf16[2,256,256]{2,1,0:T(8,128)(2,1)S(1)} %get-tuple-element.62.refs_4_), channel_id=1, source_target_pairs={{0,2},{1,3},{2,0},{3,1},{4,6},{5,7},{6,4},{7,5},{8,10},{9,11},{10,... | collective-permute-start | bytes 786440 | tf_op jit(solution)/shard_map/ppermute | solution.py:285
  257.6 33.9 %collective-permute-start.10 = (bf16[2,256,256]{2,1,0:T(8,128)(2,1)S(1)}, bf16[2,256,256]{2,1,0:T(8,128)(2,1)S(1)}, u32[]{:S(2)}, u32[]{:S(2)}) collective-permute-start(bf16[2,256,256]{2,1,0:T(8,128)(2,1)S(1)} %get-tuple-element.83.refs_4_), channel_id=1, source_target_pairs={{0,1},{1,0},{2,3},{3,2},{4,5},{5,4},{6,7},{7,6},{8,9},{9,8},{10,11... | collective-permute-start | bytes 786440 | tf_op jit(solution)/shard_map/ppermute | solution.py:285
  260.0 39.7 %collective-permute-start.11 = (bf16[2,256,256]{2,1,0:T(8,128)(2,1)S(1)}, bf16[2,256,256]{2,1,0:T(8,128)(2,1)S(1)}, u32[]{:S(2)}, u32[]{:S(2)}) collective-permute-start(bf16[2,256,256]{2,1,0:T(8,128)(2,1)S(1)} %get-tuple-element.83.refs_4_), channel_id=1, source_target_pairs={{0,2},{1,3},{2,0},{3,1},{4,6},{5,7},{6,4},{7,5},{8,10},{9,11},{10,... | collective-permute-start | bytes 786440 | tf_op jit(solution)/shard_map/ppermute | solution.py:285
  261.6 38.8 %collective-permute-start.12 = (bf16[2,256,256]{2,1,0:T(8,128)(2,1)S(1)}, bf16[2,256,256]{2,1,0:T(8,128)(2,1)S(1)}, u32[]{:S(2)}, u32[]{:S(2)}) collective-permute-start(bf16[2,256,256]{2,1,0:T(8,128)(2,1)S(1)} %get-tuple-element.83.refs_4_), channel_id=1, source_target_pairs={{0,3},{1,2},{2,1},{3,0},{4,7},{5,6},{6,5},{7,4},{8,11},{9,10},{10,... | collective-permute-start | bytes 786440 | tf_op jit(solution)/shard_map/ppermute | solution.py:285
  276.8 34.7 %collective-permute-start.65 = (f32[3,64,256]{2,1,0:T(8,128)S(1)}, f32[3,64,256]{2,1,0:T(8,128)S(1)}, u32[]{:S(2)}, u32[]{:S(2)}) collective-permute-start(f32[3,64,256]{2,1,0:T(8,128)S(1)} %add_add_fusion.1), channel_id=1, source_target_pairs={{0,2},{1,3},{2,0},{3,1},{4,6},{5,7},{6,4},{7,5},{8,10},{9,11},{10,... | collective-permute-start | bytes 589832 | tf_op jit(solution)/shard_map/ppermute | solution.py:285
  312.0 42.5 %collective-permute-start.26 = (bf16[2,128,1024]{2,1,0:T(8,128)(2,1)S(1)}, bf16[2,128,1024]{2,1,0:T(8,128)(2,1)S(1)}, u32[]{:S(2)}, u32[]{:S(2)}) collective-permute-start(bf16[2,128,1024]{2,1,0:T(8,128)(2,1)S(1)} %get-tuple-element.47), channel_id=1, source_target_pairs={{0,8},{4,12},{8,0},{12,4},{1,9},{5,13},{9,1},{13,5},{2,10},{6,14},... | collective-permute-start | bytes 1572872 | tf_op jit(solution)/shard_map/ppermute | solution.py:285
  319.5 29.2 %collective-permute-start.68 = (f32[3,64,256]{2,1,0:T(8,128)S(1)}, f32[3,64,256]{2,1,0:T(8,128)S(1)}, u32[]{:S(2)}, u32[]{:S(2)}) collective-permute-start(f32[3,64,256]{2,1,0:T(8,128)S(1)} %add_add_fusion.refs_0_), channel_id=1, source_target_pairs={{0,8},{4,12},{8,0},{12,4},{1,9},{5,13},{9,1},{13,5},{2,10},{6,14},... | collective-permute-start | bytes 589832 | tf_op jit(solution)/shard_map/ppermute | solution.py:285
  321.0 28.3 %collective-permute-start.69 = (f32[3,64,256]{2,1,0:T(8,128)S(1)}, f32[3,64,256]{2,1,0:T(8,128)S(1)}, u32[]{:S(2)}, u32[]{:S(2)}) collective-permute-start(f32[3,64,256]{2,1,0:T(8,128)S(1)} %add_add_fusion.refs_0_), channel_id=1, source_target_pairs={{0,12},{4,8},{8,4},{12,0},{1,13},{5,9},{9,5},{13,1},{2,14},{6,10},... | collective-permute-start | bytes 589832 | tf_op jit(solution)/shard_map/ppermute | solution.py:285
  329.9 29.3 %collective-permute-start.27 = (bf16[2,128,1024]{2,1,0:T(8,128)(2,1)S(1)}, bf16[2,128,1024]{2,1,0:T(8,128)(2,1)S(1)}, u32[]{:S(2)}, u32[]{:S(2)}) collective-permute-start(bf16[2,128,1024]{2,1,0:T(8,128)(2,1)S(1)} %get-tuple-element.48), channel_id=1, source_target_pairs={{0,12},{4,8},{8,4},{12,0},{1,13},{5,9},{9,5},{13,1},{2,14},{6,10},... | collective-permute-start | bytes 1572872 | tf_op jit(solution)/shard_map/ppermute | solution.py:285
  334.1 27.0 %collective-permute-start.13 = (bf16[2,128,1024]{2,1,0:T(8,128)(2,1)S(1)}, bf16[2,128,1024]{2,1,0:T(8,128)(2,1)S(1)}, u32[]{:S(2)}, u32[]{:S(2)}) collective-permute-start(bf16[2,128,1024]{2,1,0:T(8,128)(2,1)S(1)} %get-tuple-element.38), channel_id=1, source_target_pairs={{0,4},{4,0},{8,12},{12,8},{1,5},{5,1},{9,13},{13,9},{2,6},{6,2},{1... | collective-permute-start | bytes 1572872 | tf_op jit(solution)/shard_map/ppermute | solution.py:285
  (54 other events, 889.7 us)

commit v2 on v1

v2 whole, which is shorter than its diff:
```python
import functools
import math

import jax
import jax.numpy as jnp
from jax import lax
from jax.experimental import pallas as pl
from jax.experimental.pallas import tpu as pltpu
from jax.sharding import PartitionSpec as P

D = 2048
NS_ITERS = 4
CHUNKS = (2, 2, 2)
VMEM_LIMIT = 40 * 1024 * 1024

beta_one = 0.9
beta_two = 0.999
bias_one = 1.0 - 0.9**10
bias_two = 1.0 - 0.999**10
eps_adam = 1e-08
galore_gain = 4.0
width_root = math.sqrt(D)

F32 = jnp.float32
BF16 = jnp.bfloat16


def dot_tn(a, b):
    return lax.dot_general(a, b, (((0,), (0,)), ((), ())), preferred_element_type=F32)


def dot_nn(a, b):
    return lax.dot_general(a, b, (((1,), (0,)), ((), ())), preferred_element_type=F32)


def dot_nt(a, b):
    return lax.dot_general(a, b, (((1,), (1,)), ((), ())), preferred_element_type=F32)


def split(a):
    high = a.astype(BF16)
    return high, (a - high.astype(F32)).astype(BF16)


def fine(dot, a, b):
    (ah, al), (bh, bl) = a, b
    return dot(ah, bh) + (dot(ah, bl) + dot(al, bh))


def call(body, grid, prefetch, ins, outs, scratch, flops, aliases=None):
    moved = sum(math.prod(s) * jnp.dtype(d).itemsize for s, d, _, _ in outs)
    moved += sum(a.size * a.dtype.itemsize for a, b, _ in ins if b is not None)
    return pl.pallas_call(
        body,
        grid_spec=pltpu.PrefetchScalarGridSpec(
            num_scalar_prefetch=1,
            grid=grid,
            in_specs=[
                pl.BlockSpec(memory_space=pl.ANY) if b is None else pl.BlockSpec(b, m)
                for _, b, m in ins
            ],
            out_specs=[pl.BlockSpec(b, m) for _, _, b, m in outs],
            scratch_shapes=scratch,
        ),
        out_shape=[jax.ShapeDtypeStruct(s, d) for s, d, _, _ in outs],
        input_output_aliases=aliases or {},
        compiler_params=pltpu.CompilerParams(vmem_limit_bytes=VMEM_LIMIT),
        cost_estimate=pl.CostEstimate(flops=1, bytes_accessed=1, transcendentals=0),
    )(prefetch, *[a for a, _, _ in ins])


def outgoing(place, gradient, basis, k0, kc, tensors, after):
    rows, columns = gradient.shape[1:]
    rank = basis.shape[2]
    width = columns // tensors
    n = tensors - 1

    def body(place_ref, *refs):
        g, b, out = refs[:n], refs[n], refs[-n:]
        for m in range(n):
            out[m][0, :, :width] = g[m][0]
            out[m][0, :, width:] = b[0]

    return call(
        body,
        (kc,),
        place,
        [
            (gradient, (1, rows, width), lambda i, p, m=m: (k0 + i, 0, jnp.bitwise_xor(p[0], m)))
            for m in range(1, tensors)
        ]
        + [(basis, (1, rows, rank), lambda i, p: (k0 + i, 0, 0))]
        + [(a, None, None) for a in after],
        [((kc, rows, width + rank), BF16, (1, rows, width + rank), lambda i, p: (i, 0, 0))] * n,
        [],
        0,
    )


def sources(gradient, basis, got, k0, pick=lambda i, p: i):
    rows, rank = basis.shape[1:]
    kc, _, wide = got[0].shape
    return [
        (gradient, (1, rows, wide - rank), lambda i, p: (k0 + pick(i, p), 0, p[0])),
        (basis, (1, rows, rank), lambda i, p: (k0 + pick(i, p), 0, 0)),
    ] + [(g, (1, rows, wide), lambda i, p: (pick(i, p), 0, 0)) for g in got]


def low_partial(place, gradient, basis, got, k0, sections):
    rows, rank = basis.shape[1:]
    kc, _, wide = got[0].shape
    width = wide - rank
    part = width // sections
    n = len(got)
    chosen = blocks_sent(sections)

    def body(place_ref, *refs):
        out, total = refs[2 + n : -1], refs[-1]
        acc = dot_tn(refs[0][0], refs[1][0])
        for m in range(n):
            acc += dot_tn(refs[2 + m][0, :, :width], refs[2 + m][0, :, width:])
        total[...] = acc
        z = place_ref[1]
        for j, block in enumerate(chosen):
            at = pl.multiple_of(block(z) * part, part)
            out[j][0] = total[pl.ds(at, part), :].astype(out[j].dtype)

    return call(
        body,
        (kc,),
        place,
        sources(gradient, basis, got, k0),
        [
            ((kc, part, rank), BF16 if j else F32, (1, part, rank), lambda i, p: (i, 0, 0))
            for j in range(len(chosen))
        ],
        [pltpu.VMEM((width, rank), F32)],
        2 * kc * (n + 1) * rows * width * rank,
    )


def blocks_sent(sections):
    return [lambda z, m=m: jnp.bitwise_xor(z, m) for m in range(sections)]


def section_sum(parts, swap):
    if len(parts) != 4:
        return [parts[0]] + [swap(parts[m], "section", m) for m in range(1, len(parts))]
    own, near, two, far = parts
    far = swap(far, "section", 1)
    near = swap(near, "section", 1)
    two = (two.astype(F32) + far.astype(F32)).astype(BF16)
    return [own, near, swap(two, "section", 2)]


def section_gather(x, sections, swap):
    if sections != 4:
        return [x] + [swap(x, "section", m) for m in range(1, sections)]
    two = swap(x, "section", 2)
    near = swap(x, "section", 1)
    return [x, near, two, swap(two, "section", 1)]


def gather_into(whole, refs, z):
    part = refs[0].shape[-2]
    for j, ref in enumerate(refs):
        at = pl.multiple_of(jnp.bitwise_xor(z, j) * part, part)
        whole[pl.ds(at, part), :] = ref[0]


def update(place, terms, moment_m, moment_v, before, k0):
    kc, part, rank = terms[0].shape
    n = len(terms)

    def body(place_ref, *refs):
        m_ref, v_ref = refs[n], refs[n + 1]
        rough, step_out, m_out, v_out = refs[-4:]
        total = refs[0][0]
        for j in range(1, n):
            total += refs[j][0].astype(F32)
        low_rank = total / width_root
        m_new = beta_one * m_ref[0] + (1.0 - beta_one) * low_rank
        v_new = beta_two * v_ref[0] + (1.0 - beta_two) * low_rank * low_rank
        step = m_new / bias_one / (jnp.sqrt(v_new / bias_two) + eps_adam)
        rough[0] = low_rank.astype(BF16)
        step_out[0] = step.astype(BF16)
        m_out[0] = m_new
        v_out[0] = v_new

    here = lambda i, p: (k0 + i, 0, 0)
    block = (1, part, rank)
    ins = [(a, block, lambda i, p: (i, 0, 0)) for a in terms]
    ins += [(moment_m, block, here), (moment_v, block, here)]
    aliases = {}
    if before is not None:
        ins += [(b, None, None) for b in before]
        aliases = {n + 3: 2, n + 4: 3}
    return call(
        body,
        (kc,),
        place,
        ins,
        [
            ((kc, part, rank), BF16, block, lambda i, p: (i, 0, 0)),
            ((kc, part, rank), BF16, block, lambda i, p: (i, 0, 0)),
            (moment_m.shape, F32, block, here),
            (moment_v.shape, F32, block, here),
        ],
        [],
        0,
        aliases,
    )


def subspace_partial(place, gradient, basis, got, gathered, k0, split_cores):
    rows, rank = basis.shape[1:]
    kc, _, wide = got[0].shape
    width = wide - rank
    part = gathered[0].shape[1]
    n, s = len(got), len(gathered)
    half = kc // 2

    def pick(i, p):
        if not split_cores:
            return i
        return jnp.where(i < half, 2 * i + p[2], 2 * (i - half) + 1 - p[2])

    def body(place_ref, *refs):
        out, whole = refs[-2:]
        gather_into(whole, refs[2 + n : 2 + n + s], place_ref[1])
        out[0, 0] = dot_nn(refs[0][0], whole[...])
        for m in range(n):
            out[0, m + 1] = dot_nn(refs[2 + m][0, :, :width], whole[...])

    return call(
        body,
        (kc,),
        place,
        sources(gradient, basis, got, k0, pick)
        + [(r, (1, part, rank), lambda i, p: (pick(i, p), 0, 0)) for r in gathered],
        [((kc, n + 1, rows, rank), F32, (1, n + 1, rows, rank), lambda i, p: (i, 0, 0, 0))],
        [pltpu.VMEM((width, rank), BF16)],
        2 * kc * (n + 1) * rows * width * rank,
    )[0]


def delta_parts(place, basis, got, gathered, k0):
    rows, rank = basis.shape[1:]
    kc, _, wide = got[0].shape
    width = wide - rank
    part = gathered[0].shape[1]
    n, s = len(got), len(gathered)

    def body(place_ref, *refs):
        out, whole = refs[1 + n + s : -1], refs[-1]
        gather_into(whole, refs[1 + n : 1 + n + s], place_ref[1])
        for m in range(n + 1):
            b = refs[m][0, :, width:] if m else refs[0][0]
            out[m][0] = (-galore_gain / width_root * dot_nt(b, whole[...])).astype(BF16)

    return call(
        body,
        (kc,),
        place,
        [(basis, (1, rows, rank), lambda i, p: (k0 + i, 0, 0))]
        + [(g, (1, rows, wide), lambda i, p: (i, 0, 0)) for g in got]
        + [(r, (1, part, rank), lambda i, p: (i, 0, 0)) for r in gathered],
        [((kc, rows, width), BF16, (1, rows, width), lambda i, p: (i, 0, 0))] * (n + 1),
        [pltpu.VMEM((width, rank), BF16)],
        2 * kc * (n + 1) * rows * width * rank,
    )


def place_delta(place, parts, before, k0, matrices):
    kc, rows, width = parts[0].shape
    n = len(parts)

    def body(place_ref, *refs):
        out = refs[-1]
        for m in range(n):
            at = pl.multiple_of(jnp.bitwise_xor(place_ref[0], m) * width, width)
            out[0, :, pl.ds(at, width)] = refs[m][0]

    ins = [(p, (1, rows, width), lambda i, p: (i, 0, 0)) for p in parts]
    aliases = {}
    if before is not None:
        ins.append((before, None, None))
        aliases = {n + 1: 0}
    shape = (matrices, rows, n * width)
    return call(
        body,
        (kc,),
        place,
        ins,
        [(shape, BF16, (1, rows, n * width), lambda i, p: (k0 + i, 0, 0))],
        [],
        0,
        aliases,
    )[0]


def gram_parts(place, groups):
    n = len(groups[0])
    rows, rank = groups[0][0].shape[1:]
    counts = [g[0].shape[0] for g in groups]
    total = sum(counts)
    part = rank // n
    flat = [p for g in groups for p in g]

    def body(place_ref, *refs):
        pieces, sub, out, whole = refs[: len(flat)], refs[len(flat)], refs[len(flat) + 1 : -1], refs[-1]
        at = 0
        for j, count in enumerate(counts):
            for i in range(count):
                acc = pieces[j * n][i]
                for m in range(1, n):
                    acc += pieces[j * n + m][i]
                sub[at] = acc
                high = split(acc)
                whole[at] = fine(dot_tn, high, high)
                at += 1
        for m in range(n):
            start = pl.multiple_of(jnp.bitwise_xor(place_ref[0], m) * part, part)
            for i in range(total):
                out[m][i] = whole[i, pl.ds(start, part), :]

    zero3 = lambda i, p: (0, 0, 0)
    res = call(
        body,
        (1,),
        place,
        [(p, p.shape, zero3) for p in flat],
        [((total, rows, rank), F32, (total, rows, rank), zero3)]
        + [((total, part, rank), F32, (total, part, rank), zero3)] * n,
        [pltpu.VMEM((total, rank, rank), F32)],
        6 * total * rows * rank * rank,
    )
    return res[0], res[1:]


def newton_schulz(place, pieces, sub):
    n = len(pieces)
    total, rows, rank = sub.shape
    part = rank // n

    def body(place_ref, *refs):
        p, s, out, whole = refs[:n], refs[n], refs[n + 1], refs[-1]
        for m in range(n):
            start = pl.multiple_of(jnp.bitwise_xor(place_ref[0], m) * part, part)
            for i in range(total):
                whole[i, pl.ds(start, part), :] = p[m][i]
        row = lax.broadcasted_iota(jnp.int32, (rank, rank), 0)
        col = lax.broadcasted_iota(jnp.int32, (rank, rank), 1)
        eye = jnp.where(row == col, 1.0, 0.0).astype(F32)
        iters, grams, prods = [], [], []
        for i in range(total):
            gram = whole[i]
            bound = jnp.max(jnp.sum(jnp.abs(gram), axis=1, keepdims=True), axis=0, keepdims=True) + 1e-06
            iters.append(s[i] / jnp.sqrt(bound))
            grams.append(gram / bound)
            prods.append(None)
        for turn in range(NS_ITERS):
            for i in range(total):
                factor = 1.5 * eye - 0.5 * grams[i]
                f = split(factor)
                prods[i] = factor if turn == 0 else fine(dot_nn, split(prods[i]), f)
                if turn + 1 < NS_ITERS:
                    half = fine(dot_nn, split(grams[i]), f)
                    grams[i] = fine(dot_nn, split(half), f)
        for i in range(total):
            res = fine(dot_nn, split(iters[i]), split(prods[i]))
            out[i] = (width_root * res).astype(BF16)

    zero3 = lambda i, p: (0, 0, 0)
    return call(
        body,
        (1,),
        place,
        [(p, p.shape, zero3) for p in pieces] + [(sub, sub.shape, zero3)],
        [((total, rows, rank), BF16, (total, rows, rank), zero3)],
        [pltpu.VMEM((total, rank, rank), F32)],
        60 * total * rank * rank * rank,
    )[0]


def after(x, *others):
    return lax.optimization_barrier((x, others))[0]


def per_device(shape, gradient, basis, moment_m, moment_v):
    tensors, sections, cores = shape["tensor"], shape["section"], shape["shard"]
    t, z, c = (lax.axis_index(a) for a in ("tensor", "section", "shard"))
    place = jnp.stack([t, z, c]).astype(jnp.int32)
    matrices = gradient.shape[0]
    split_cores = cores == 2
    n = len(CHUNKS)
    starts = [sum(CHUNKS[:j]) for j in range(n)]

    def swap(x, axis, m):
        return lax.ppermute(x, axis, [(i, i ^ m) for i in range(shape[axis])])

    def other_core(x):
        return lax.ppermute(x, "shard", [(0, 1), (1, 0)])

    def swap_all(cut):
        return [swap(cut[m - 1], "tensor", m) for m in range(1, tensors)]

    def then(*values):
        nonlocal place
        place = after(place, *values)

    grads, roughs, steps, cuts, groups = {}, {}, {}, {}, {}
    rough_own, step_own, state = {}, {}, {"news": None, "delta": None}

    def send(j, *waits):
        cut = outgoing(place, gradient, basis, starts[j], CHUNKS[j], tensors, waits)
        grads[j] = swap_all(cut)
        then(cut)

    def low(j):
        parts = low_partial(place, gradient, basis, grads[j], starts[j], sections)
        then(parts)
        return section_sum(parts, swap)

    def step(j, terms):
        rough, new, *state["news"] = update(place, terms, moment_m, moment_v, state["news"], starts[j])
        rough_own[j], step_own[j] = rough, new
        then(rough)

    def subspace(j):
        sub = subspace_partial(place, gradient, basis, grads[j], roughs[j], starts[j], split_cores)
        then(sub)
        if split_cores:
            half = CHUNKS[j] // 2
            sub = sub[:half] + other_core(sub[half:])
        else:
            sub = lax.psum(sub, "shard")
        groups[j] = [sub[:, 0]] + [swap(sub[:, m], "tensor", m) for m in range(1, tensors)]

    def delta(j):
        cut = delta_parts(place, basis, grads[j], steps[j], starts[j])
        then(cut)
        cuts[j] = [cut[0]] + swap_all(cut[1:])

    def put(j):
        state["delta"] = place_delta(place, cuts[j], state["delta"], starts[j], matrices)
        then(state["delta"])

    def gather(x):
        return section_gather(x, sections, swap)

    send(0)
    send(1, *grads[0])
    terms = low(0)
    step(0, terms)
    roughs[0] = gather(rough_own[0])
    steps[0] = gather(step_own[0])
    send(2, *grads[1])
    terms = low(1)
    step(1, terms)
    subspace(0)
    delta(0)
    roughs[1] = gather(rough_own[1])
    steps[1] = gather(step_own[1])
    terms = low(2)
    step(2, terms)
    subspace(1)
    delta(1)
    put(0)
    roughs[2] = gather(rough_own[2])
    steps[2] = gather(after(step_own[2], roughs[2][2]))
    subspace(2)
    put(1)
    delta(2)
    sub, cut = gram_parts(place, [groups[j] for j in range(n)])
    then(sub)
    gram = cut[0]
    for m in range(1, tensors):
        gram = gram + swap(cut[m], "tensor", m)
    reach = 1
    while reach < sections:
        gram = gram + swap(gram, "section", reach)
        reach *= 2
    pieces = [gram] + [swap(gram, "tensor", m) for m in range(1, tensors)]
    done = newton_schulz(place, pieces, sub)
    then(done)
    if split_cores:
        theirs = other_core(done)
        even = jnp.where(c == 0, done, theirs)
        odd = jnp.where(c == 0, theirs, done)
        basis_new = jnp.stack([even, odd], 1).reshape(basis.shape)
    else:
        basis_new = done
    put(2)
    return (state["delta"], basis_new, *state["news"])


def solution(mesh):
    placed = (
        P(None, ("tensor", "section"), "shard"),
        P(None, ("tensor", "section"), None),
        P(None, ("shard", "tensor", "section"), None),
        P(None, ("shard", "tensor", "section"), None),
    )
    return jax.shard_map(
        functools.partial(per_device, dict(mesh.shape)),
        mesh=mesh,
        in_specs=placed,
        out_specs=placed,
        check_vma=False,
    )
```

time: 373 us -> 320 us (0.86)
  starting transfers between devices: 132 us -> 95.9 us
  waiting for transfers between devices: 193 us -> 177 us
  Pallas kernels: 32.3 us -> 40.9 us
  other arithmetic: 7.81 us -> 0.64 us
    ppermute x66 -> x62, starting transfers between devices: 131 us -> 95.7 us  [swap(): return lax.ppermute(x, axis, [(i, i ^ m) for i in range(shape[axis])])]
    ppermute x66 -> x62, waiting for transfers between devices: 193 us -> 177 us  [swap(): return lax.ppermute(x, axis, [(i, i ^ m) for i in range(shape[axis])])]
    pallas_call x14 -> x20, Pallas kernels: 32.3 us -> 40.9 us  [call(): pl.pallas_call(body, grid_spec=pltpu.PrefetchScalarGridSpec(num_scalar_pr...]
    dynamic_slice x2 -> x0, local copies, waits for them, and re-layouts: 6 us -> none  [the longest x1 5.05 us: per_device(): lax.dynamic_slice(gradient, (k0, 0, (t ^ m) * width), (kc, rows, width))]
    unnamed x14 -> x12, local copies, waits for them, and re-layouts: 0.03 us -> 3.8 us
  transfers between devices with their start and end apart: 71 -> 66, of which waited for: 29 -> 32; matrix products, arithmetic and copies ran while one was open for 3% -> 0% of each run, Pallas kernels for 9% -> 10%
where the time goes in v2:
time: 320 us
  waiting for transfers between devices  177 us (55%)
  starting transfers between devices  95.9 us (30%)
  Pallas kernels  40.9 us (13%)
  local copies, waits for them, and re-layouts  4.79 us (1%)
    ppermute x62, waiting for transfers between devices, swap(): return lax.ppermute(x, axis, [(i, i ^ m) for i in range(shape[axis])])  177 us
    ppermute x62, starting transfers between devices, swap(): return lax.ppermute(x, axis, [(i, i ^ m) for i in range(shape[axis])])  95.7 us
    pallas_call x20, Pallas kernels, call(): pl.pallas_call(body, grid_spec=pltpu.PrefetchScalarGridSpec(num_scalar_pr...  40.9 us
  transfers between devices with their start and end apart: 66, of which 32 were waited for; matrix products, arithmetic and copies ran while one was open for 0% of the time, Pallas kernels for 10%

profile of v2, /device:TPU:0, one launch (start us, length us, event | category | flops | bytes accessed | tf_op | source)
XLA Modules:
  0.0 320.1 jit_solution(8347426358343026389)
XLA Ops:
  9.9 14.0 %collective-permute-done.refs_4_.refs_2_.refs_1_ = bf16[2,128,1280]{2,1,0:T(8,128)(2,1)S(1)} collective-permute-done((bf16[2,128,1280]{2,1,0:T(8,128)(2,1)S(1)}, bf16[2,128,1280]{2,1,0:T(8,128)(2,1)S(1)}, u32[]{:S(2)}, u32[]{:S(2)}) %collective-permute-start) | collective-permute-done | bytes 655392 | tf_op jit(solution)/shard_map/ppermute | solution.py:400
  24.0 14.7 %collective-permute-done.1.refs_5_.refs_3_.refs_2_ = bf16[2,128,1280]{2,1,0:T(8,128)(2,1)S(1)} collective-permute-done((bf16[2,128,1280]{2,1,0:T(8,128)(2,1)S(1)}, bf16[2,128,1280]{2,1,0:T(8,128)(2,1)S(1)}, u32[]{:S(2)}, u32[]{:S(2)}) %collective-permute-start.1) | collective-permute-done | bytes 655392 | tf_op jit(solution)/shard_map/ppermute | solution.py:400
  47.4 5.9 %collective-permute-done.4 = bf16[2,256,256]{2,1,0:T(8,128)(2,1)S(1)} collective-permute-done((bf16[2,256,256]{2,1,0:T(8,128)(2,1)S(1)}, bf16[2,256,256]{2,1,0:T(8,128)(2,1)S(1)}, u32[]{:S(2)}, u32[]{:S(2)}) %collective-permute-start.4) | collective-permute-done | bytes 262176 | tf_op jit(solution)/shard_map/ppermute | solution.py:400
  57.3 14.8 %collective-permute-done.5.refs_2_ = bf16[2,256,256]{2,1,0:T(8,128)(2,1)S(1)} collective-permute-done((bf16[2,256,256]{2,1,0:T(8,128)(2,1)S(1)}, bf16[2,256,256]{2,1,0:T(8,128)(2,1)S(1)}, u32[]{:S(2)}, u32[]{:S(2)}) %collective-permute-start.5) | collective-permute-done | bytes 262176 | tf_op jit(solution)/shard_map/ppermute | solution.py:400
  82.9 4.6 %collective-permute-done.16.refs_6_ = bf16[2,256,256]{2,1,0:T(8,128)(2,1)S(1)} collective-permute-done((bf16[2,256,256]{2,1,0:T(8,128)(2,1)S(1)}, bf16[2,256,256]{2,1,0:T(8,128)(2,1)S(1)}, u32[]{:S(2)}, u32[]{:S(2)}) %collective-permute-start.16) | collective-permute-done | bytes 262176 | tf_op jit(solution)/shard_map/ppermute | solution.py:400
  94.6 6.5 %collective-permute-done.12.refs_6_ = bf16[2,256,256]{2,1,0:T(8,128)(2,1)S(1)} collective-permute-done((bf16[2,256,256]{2,1,0:T(8,128)(2,1)S(1)}, bf16[2,256,256]{2,1,0:T(8,128)(2,1)S(1)}, u32[]{:S(2)}, u32[]{:S(2)}) %collective-permute-start.12) | collective-permute-done | bytes 262176 | tf_op jit(solution)/shard_map/ppermute | solution.py:400
  104.1 7.8 %collective-permute-done.14.refs_8_ = bf16[2,256,256]{2,1,0:T(8,128)(2,1)S(1)} collective-permute-done((bf16[2,256,256]{2,1,0:T(8,128)(2,1)S(1)}, bf16[2,256,256]{2,1,0:T(8,128)(2,1)S(1)}, u32[]{:S(2)}, u32[]{:S(2)}) %collective-permute-start.14) | collective-permute-done | bytes 262176 | tf_op jit(solution)/shard_map/ppermute | solution.py:400
  131.4 9.7 %collective-permute-done.22 = bf16[2,256,256]{2,1,0:T(8,128)(2,1)S(1)} collective-permute-done((bf16[2,256,256]{2,1,0:T(8,128)(2,1)S(1)}, bf16[2,256,256]{2,1,0:T(8,128)(2,1)S(1)}, u32[]{:S(2)}, u32[]{:S(2)}) %collective-permute-start.22) | collective-permute-done | bytes 262176 | tf_op jit(solution)/shard_map/ppermute | solution.py:400
  142.7 9.6 %collective-permute-done.27.refs_5_ = bf16[2,256,256]{2,1,0:T(8,128)(2,1)S(1)} collective-permute-done((bf16[2,256,256]{2,1,0:T(8,128)(2,1)S(1)}, bf16[2,256,256]{2,1,0:T(8,128)(2,1)S(1)}, u32[]{:S(2)}, u32[]{:S(2)}) %collective-permute-start.27) | collective-permute-done | bytes 262176 | tf_op jit(solution)/shard_map/ppermute | solution.py:400
  154.0 7.8 %collective-permute-start.30 = (bf16[2,128,1024]{2,1,0:T(8,128)(2,1)S(1)}, bf16[2,128,1024]{2,1,0:T(8,128)(2,1)S(1)}, u32[]{:S(2)}, u32[]{:S(2)}) collective-permute-start(bf16[2,128,1024]{2,1,0:T(8,128)(2,1)S(1)} %get-tuple-element.105), channel_id=1, source_target_pairs={{0,4},{4,0},{8,12},{12,8},{1,5},{5,1},{9,13},{13,9},{2,6},{6,2},{1... | collective-permute-start | bytes 1572872 | tf_op jit(solution)/shard_map/ppermute | solution.py:400
  171.1 5.3 %collective-permute-done.29.refs_7_ = bf16[2,256,256]{2,1,0:T(8,128)(2,1)S(1)} collective-permute-done((bf16[2,256,256]{2,1,0:T(8,128)(2,1)S(1)}, bf16[2,256,256]{2,1,0:T(8,128)(2,1)S(1)}, u32[]{:S(2)}, u32[]{:S(2)}) %collective-permute-start.29) | collective-permute-done | bytes 262176 | tf_op jit(solution)/shard_map/ppermute | solution.py:400
  180.2 8.6 %collective-permute-start.32 = (bf16[2,128,1024]{2,1,0:T(8,128)(2,1)S(1)}, bf16[2,128,1024]{2,1,0:T(8,128)(2,1)S(1)}, u32[]{:S(2)}, u32[]{:S(2)}) collective-permute-start(bf16[2,128,1024]{2,1,0:T(8,128)(2,1)S(1)} %get-tuple-element.107), channel_id=1, source_target_pairs={{0,12},{4,8},{8,4},{12,0},{1,13},{5,9},{9,5},{13,1},{2,14},{6,10},... | collective-permute-start | bytes 1572872 | tf_op jit(solution)/shard_map/ppermute | solution.py:400
  199.8 5.2 %collective-permute-done.35.refs_8_ = bf16[2,256,256]{2,1,0:T(8,128)(2,1)S(1)} collective-permute-done((bf16[2,256,256]{2,1,0:T(8,128)(2,1)S(1)}, bf16[2,256,256]{2,1,0:T(8,128)(2,1)S(1)}, u32[]{:S(2)}, u32[]{:S(2)}) %collective-permute-start.35) | collective-permute-done | bytes 262176 | tf_op jit(solution)/shard_map/ppermute | solution.py:400
  206.8 4.2 %collective-permute-start.45 = (f32[1,128,256]{2,1,0:T(8,128)S(1)}, f32[1,128,256]{2,1,0:T(8,128)S(1)}, u32[]{:S(2)}, u32[]{:S(2)}) collective-permute-start(f32[1,128,256]{2,1,0:T(8,128)S(1)} %get-tuple-element.152), channel_id=1, source_target_pairs={{0,12},{4,8},{8,4},{12,0},{1,13},{5,9},{9,5},{13,1},{2,14},{6,10},... | collective-permute-start | bytes 393224 | tf_op jit(solution)/shard_map/ppermute | solution.py:400
  213.3 4.5 %collective-permute-start.40 = (bf16[2,256,256]{2,1,0:T(8,128)(2,1)S(1)}, bf16[2,256,256]{2,1,0:T(8,128)(2,1)S(1)}, u32[]{:S(2)}, u32[]{:S(2)}) collective-permute-start(bf16[2,256,256]{2,1,0:T(8,128)(2,1)S(1)} %get-tuple-element.129.refs_4_), channel_id=1, source_target_pairs={{0,2},{1,3},{2,0},{3,1},{4,6},{5,7},{6,4},{7,5},{8,10},{9,11},{10,... | collective-permute-start | bytes 786440 | tf_op jit(solution)/shard_map/ppermute | solution.py:400
  222.2 7.7 %collective-permute-done.40.refs_6_ = bf16[2,256,256]{2,1,0:T(8,128)(2,1)S(1)} collective-permute-done((bf16[2,256,256]{2,1,0:T(8,128)(2,1)S(1)}, bf16[2,256,256]{2,1,0:T(8,128)(2,1)S(1)}, u32[]{:S(2)}, u32[]{:S(2)}) %collective-permute-start.40) | collective-permute-done | bytes 262176 | tf_op jit(solution)/shard_map/ppermute | solution.py:400
  232.0 7.1 %collective-permute-done.39.refs_5_ = bf16[2,256,256]{2,1,0:T(8,128)(2,1)S(1)} collective-permute-done((bf16[2,256,256]{2,1,0:T(8,128)(2,1)S(1)}, bf16[2,256,256]{2,1,0:T(8,128)(2,1)S(1)}, u32[]{:S(2)}, u32[]{:S(2)}) %collective-permute-start.39) | collective-permute-done | bytes 262176 | tf_op jit(solution)/shard_map/ppermute | solution.py:400
  242.5 5.8 %collective-permute-done.37.refs_2_ = bf16[2,128,1024]{2,1,0:T(8,128)(2,1)S(1)} collective-permute-done((bf16[2,128,1024]{2,1,0:T(8,128)(2,1)S(1)}, bf16[2,128,1024]{2,1,0:T(8,128)(2,1)S(1)}, u32[]{:S(2)}, u32[]{:S(2)}) %collective-permute-start.37) | collective-permute-done | bytes 524320 | tf_op jit(solution)/shard_map/ppermute | solution.py:400
  267.8 3.9 %collective-permute-start.57 = (f32[3,64,256]{2,1,0:T(8,128)S(1)}, f32[3,64,256]{2,1,0:T(8,128)S(1)}, u32[]{:S(2)}, u32[]{:S(2)}) collective-permute-start(f32[3,64,256]{2,1,0:T(8,128)S(1)} %add_add_fusion), channel_id=1, source_target_pairs={{0,1},{1,0},{2,3},{3,2},{4,5},{5,4},{6,7},{7,6},{8,9},{9,8},{10,11... | collective-permute-start | bytes 589832 | tf_op jit(solution)/shard_map/ppermute | solution.py:400
  271.7 5.5 %collective-permute-done.57 = f32[3,64,256]{2,1,0:T(8,128)S(1)} collective-permute-done((f32[3,64,256]{2,1,0:T(8,128)S(1)}, f32[3,64,256]{2,1,0:T(8,128)S(1)}, u32[]{:S(2)}, u32[]{:S(2)}) %collective-permute-start.57) | collective-permute-done | bytes 196640 | tf_op jit(solution)/shard_map/ppermute | solution.py:400
  277.3 3.2 collective-permute-start.58
  280.4 5.8 %collective-permute-done.58 = f32[3,64,256]{2,1,0:T(8,128)S(1)} collective-permute-done((f32[3,64,256]{2,1,0:T(8,128)S(1)}, f32[3,64,256]{2,1,0:T(8,128)S(1)}, u32[]{:S(2)}, u32[]{:S(2)}) %collective-permute-start.58) | collective-permute-done | bytes 196640 | tf_op jit(solution)/shard_map/ppermute | solution.py:400
  296.3 15.7 %collective-permute-done.60.refs_2_ = f32[3,64,256]{2,1,0:T(8,128)S(1)} collective-permute-done((f32[3,64,256]{2,1,0:T(8,128)S(1)}, f32[3,64,256]{2,1,0:T(8,128)S(1)}, u32[]{:S(2)}, u32[]{:S(2)}) %collective-permute-start.60) | collective-permute-done | bytes 196640 | tf_op jit(solution)/shard_map/ppermute | solution.py:400
  312.0 5.1 %shard_map.93 = bf16[3,128,256]{2,1,0:T(8,128)(2,1)S(1)} custom-call(s32[3]{0:T(128)S(1)} %pad_add_fusion.place_ref, f32[3,64,256]{2,1,0:T(8,128)S(1)} %add.43.refs_0_, f32[3,64,256]{2,1,0:T(8,128)S(1)} %collective-permute-done.59.refs_1_, f32[3,64,256]{2,1,0:T(8,128)S(1)} %collective-permute-done.60.refs_2_, ...), custom_call_target="tpu_custom_call" | custom-call | flops 1 | bytes 1 | tf_op jit(solution)/shard_map/pallas_call | solution.py:53
  (160 shorter events, 136.1 us)
Async XLA Ops:
  8.4 30.2 %collective-permute-start.1 = (bf16[2,128,1280]{2,1,0:T(8,128)(2,1)S(1)}, bf16[2,128,1280]{2,1,0:T(8,128)(2,1)S(1)}, u32[]{:S(2)}, u32[]{:S(2)}) collective-permute-start(bf16[2,128,1280]{2,1,0:T(8,128)(2,1)S(1)} %get-tuple-element.75), channel_id=1, source_target_pairs={{0,8},{4,12},{8,0},{12,4},{1,9},{5,13},{9,1},{13,5},{2,10},{6,14},... | collective-permute-start | bytes 1966088 | tf_op jit(solution)/shard_map/ppermute | solution.py:400
  9.9 28.7 %collective-permute-start.2 = (bf16[2,128,1280]{2,1,0:T(8,128)(2,1)S(1)}, bf16[2,128,1280]{2,1,0:T(8,128)(2,1)S(1)}, u32[]{:S(2)}, u32[]{:S(2)}) collective-permute-start(bf16[2,128,1280]{2,1,0:T(8,128)(2,1)S(1)} %get-tuple-element.76), channel_id=1, source_target_pairs={{0,12},{4,8},{8,4},{12,0},{1,13},{5,9},{9,5},{13,1},{2,14},{6,10},... | collective-permute-start | bytes 1966088 | tf_op jit(solution)/shard_map/ppermute | solution.py:400
  43.5 33.4 %collective-permute-start.6 = (bf16[2,128,1280]{2,1,0:T(8,128)(2,1)S(1)}, bf16[2,128,1280]{2,1,0:T(8,128)(2,1)S(1)}, u32[]{:S(2)}, u32[]{:S(2)}) collective-permute-start(bf16[2,128,1280]{2,1,0:T(8,128)(2,1)S(1)} %get-tuple-element.78), channel_id=1, source_target_pairs={{0,4},{4,0},{8,12},{12,8},{1,5},{5,1},{9,13},{13,9},{2,6},{6,2},{1... | collective-permute-start | bytes 1966088 | tf_op jit(solution)/shard_map/ppermute | solution.py:400
  44.7 32.2 %collective-permute-start.7 = (bf16[2,128,1280]{2,1,0:T(8,128)(2,1)S(1)}, bf16[2,128,1280]{2,1,0:T(8,128)(2,1)S(1)}, u32[]{:S(2)}, u32[]{:S(2)}) collective-permute-start(bf16[2,128,1280]{2,1,0:T(8,128)(2,1)S(1)} %get-tuple-element.79), channel_id=1, source_target_pairs={{0,8},{4,12},{8,0},{12,4},{1,9},{5,13},{9,1},{13,5},{2,10},{6,14},... | collective-permute-start | bytes 1966088 | tf_op jit(solution)/shard_map/ppermute | solution.py:400
  45.5 31.3 %collective-permute-start.8 = (bf16[2,128,1280]{2,1,0:T(8,128)(2,1)S(1)}, bf16[2,128,1280]{2,1,0:T(8,128)(2,1)S(1)}, u32[]{:S(2)}, u32[]{:S(2)}) collective-permute-start(bf16[2,128,1280]{2,1,0:T(8,128)(2,1)S(1)} %get-tuple-element.80), channel_id=1, source_target_pairs={{0,12},{4,8},{8,4},{12,0},{1,13},{5,9},{9,5},{13,1},{2,14},{6,10},... | collective-permute-start | bytes 1966088 | tf_op jit(solution)/shard_map/ppermute | solution.py:400
  82.8 21.2 %collective-permute-start.9 = (bf16[2,256,256]{2,1,0:T(8,128)(2,1)S(1)}, bf16[2,256,256]{2,1,0:T(8,128)(2,1)S(1)}, u32[]{:S(2)}, u32[]{:S(2)}) collective-permute-start(bf16[2,256,256]{2,1,0:T(8,128)(2,1)S(1)} %get-tuple-element.94), channel_id=1, source_target_pairs={{0,1},{1,0},{2,3},{3,2},{4,5},{5,4},{6,7},{7,6},{8,9},{9,8},{10,11... | collective-permute-start | bytes 786440 | tf_op jit(solution)/shard_map/ppermute | solution.py:400
  87.5 36.4 %collective-permute-start.18 = (bf16[2,128,1280]{2,1,0:T(8,128)(2,1)}, bf16[2,128,1280]{2,1,0:T(8,128)(2,1)S(1)}, u32[]{:S(2)}, u32[]{:S(2)}) collective-permute-start(bf16[2,128,1280]{2,1,0:T(8,128)(2,1)} %get-tuple-element.89), channel_id=1, source_target_pairs={{0,4},{4,0},{8,12},{12,8},{1,5},{5,1},{9,13},{13,9},{2,6},{6,2},{1... | collective-permute-start | bytes 1966088 | tf_op jit(solution)/shard_map/ppermute | solution.py:400
  87.5 36.4 %collective-permute-start.19 = (bf16[2,128,1280]{2,1,0:T(8,128)(2,1)S(1)}, bf16[2,128,1280]{2,1,0:T(8,128)(2,1)S(1)}, u32[]{:S(2)}, u32[]{:S(2)}) collective-permute-start(bf16[2,128,1280]{2,1,0:T(8,128)(2,1)S(1)} %get-tuple-element.90), channel_id=1, source_target_pairs={{0,8},{4,12},{8,0},{12,4},{1,9},{5,13},{9,1},{13,5},{2,10},{6,14},... | collective-permute-start | bytes 1966088 | tf_op jit(solution)/shard_map/ppermute | solution.py:400
  92.7 31.3 %collective-permute-start.20 = (bf16[2,128,1280]{2,1,0:T(8,128)(2,1)S(1)}, bf16[2,128,1280]{2,1,0:T(8,128)(2,1)S(1)}, u32[]{:S(2)}, u32[]{:S(2)}) collective-permute-start(bf16[2,128,1280]{2,1,0:T(8,128)(2,1)S(1)} %get-tuple-element.91), channel_id=1, source_target_pairs={{0,12},{4,8},{8,4},{12,0},{1,13},{5,9},{9,5},{13,1},{2,14},{6,10},... | collective-permute-start | bytes 1966088 | tf_op jit(solution)/shard_map/ppermute | solution.py:400
  129.0 23.3 %collective-permute-start.27 = (bf16[2,256,256]{2,1,0:T(8,128)(2,1)S(1)}, bf16[2,256,256]{2,1,0:T(8,128)(2,1)S(1)}, u32[]{:S(2)}, u32[]{:S(2)}) collective-permute-start(bf16[2,256,256]{2,1,0:T(8,128)(2,1)S(1)} %get-tuple-element.119.refs_4_), channel_id=1, source_target_pairs={{0,1},{1,0},{2,3},{3,2},{4,5},{5,4},{6,7},{7,6},{8,9},{9,8},{10,11... | collective-permute-start | bytes 786440 | tf_op jit(solution)/shard_map/ppermute | solution.py:400
  130.1 23.8 %collective-permute-start.25 = (bf16[2,256,256]{2,1,0:T(8,128)(2,1)S(1)}, bf16[2,256,256]{2,1,0:T(8,128)(2,1)S(1)}, u32[]{:S(2)}, u32[]{:S(2)}) collective-permute-start(bf16[2,256,256]{2,1,0:T(8,128)(2,1)S(1)} %get-tuple-element.100.refs_5_), channel_id=1, source_target_pairs={{0,2},{1,3},{2,0},{3,1},{4,6},{5,7},{6,4},{7,5},{8,10},{9,11},{10,... | collective-permute-start | bytes 786440 | tf_op jit(solution)/shard_map/ppermute | solution.py:400
  131.2 30.6 %collective-permute-start.21 = (bf16[2,256,256]{2,1,0:T(8,128)(2,1)S(1)}, bf16[2,256,256]{2,1,0:T(8,128)(2,1)S(1)}, u32[]{:S(2)}, u32[]{:S(2)}) collective-permute-start(bf16[2,256,256]{2,1,0:T(8,128)(2,1)S(1)} %get-tuple-element.110), channel_id=1, source_target_pairs={{0,1},{1,0},{2,3},{3,2},{4,5},{5,4},{6,7},{7,6},{8,9},{9,8},{10,11... | collective-permute-start | bytes 786440 | tf_op jit(solution)/shard_map/ppermute | solution.py:400
  142.7 47.9 %collective-permute-start.42 = (f32[1,4,128,256]{3,2,1,0:T(8,128)S(1)}, f32[1,4,128,256]{3,2,1,0:T(8,128)S(1)}, u32[]{:S(2)}, u32[]{:S(2)}) collective-permute-start(f32[1,4,128,256]{3,2,1,0:T(8,128)S(1)} %slice.73), channel_id=1, source_target_pairs={{0,16},{16,0},{1,17},{17,1},{2,18},{18,2},{3,19},{19,3},{4,20},{20... | collective-permute-start | bytes 1572872 | tf_op jit(solution)/shard_map/ppermute | solution.py:403
  154.0 36.7 %collective-permute-start.30 = (bf16[2,128,1024]{2,1,0:T(8,128)(2,1)S(1)}, bf16[2,128,1024]{2,1,0:T(8,128)(2,1)S(1)}, u32[]{:S(2)}, u32[]{:S(2)}) collective-permute-start(bf16[2,128,1024]{2,1,0:T(8,128)(2,1)S(1)} %get-tuple-element.105), channel_id=1, source_target_pairs={{0,4},{4,0},{8,12},{12,8},{1,5},{5,1},{9,13},{13,9},{2,6},{6,2},{1... | collective-permute-start | bytes 1572872 | tf_op jit(solution)/shard_map/ppermute | solution.py:400
  168.6 22.1 %collective-permute-start.34 = (bf16[2,256,256]{2,1,0:T(8,128)(2,1)S(1)}, bf16[2,256,256]{2,1,0:T(8,128)(2,1)S(1)}, u32[]{:S(2)}, u32[]{:S(2)}) collective-permute-start(bf16[2,256,256]{2,1,0:T(8,128)(2,1)S(1)} %get-tuple-element.116.refs_5_), channel_id=1, source_target_pairs={{0,2},{1,3},{2,0},{3,1},{4,6},{5,7},{6,4},{7,5},{8,10},{9,11},{10,... | collective-permute-start | bytes 786440 | tf_op jit(solution)/shard_map/ppermute | solution.py:400
  190.6 22.8 %collective-permute-start.46 = (f32[1,4,128,256]{3,2,1,0:T(8,128)S(1)}, f32[1,4,128,256]{3,2,1,0:T(8,128)S(1)}, u32[]{:S(2)}, u32[]{:S(2)}) collective-permute-start(f32[1,4,128,256]{3,2,1,0:T(8,128)S(1)} %slice.79), channel_id=1, source_target_pairs={{0,16},{16,0},{1,17},{17,1},{2,18},{18,2},{3,19},{19,3},{4,20},{20... | collective-permute-start | bytes 1572872 | tf_op jit(solution)/shard_map/ppermute | solution.py:403
  206.7 23.9 %collective-permute-start.50 = (f32[1,4,128,256]{3,2,1,0:T(8,128)S(1)}, f32[1,4,128,256]{3,2,1,0:T(8,128)S(1)}, u32[]{:S(2)}, u32[]{:S(2)}) collective-permute-start(f32[1,4,128,256]{3,2,1,0:T(8,128)S(1)} %slice.85), channel_id=1, source_target_pairs={{0,16},{16,0},{1,17},{17,1},{2,18},{18,2},{3,19},{19,3},{4,20},{20... | collective-permute-start | bytes 1572872 | tf_op jit(solution)/shard_map/ppermute | solution.py:403
  218.0 22.7 %collective-permute-start.36 = (bf16[2,128,1024]{2,1,0:T(8,128)(2,1)S(1)}, bf16[2,128,1024]{2,1,0:T(8,128)(2,1)S(1)}, u32[]{:S(2)}, u32[]{:S(2)}) collective-permute-start(bf16[2,128,1024]{2,1,0:T(8,128)(2,1)S(1)} %get-tuple-element.121), channel_id=1, source_target_pairs={{0,4},{4,0},{8,12},{12,8},{1,5},{5,1},{9,13},{13,9},{2,6},{6,2},{1... | collective-permute-start | bytes 1572872 | tf_op jit(solution)/shard_map/ppermute | solution.py:400
  220.0 28.2 %collective-permute-start.37 = (bf16[2,128,1024]{2,1,0:T(8,128)(2,1)S(1)}, bf16[2,128,1024]{2,1,0:T(8,128)(2,1)S(1)}, u32[]{:S(2)}, u32[]{:S(2)}) collective-permute-start(bf16[2,128,1024]{2,1,0:T(8,128)(2,1)S(1)} %get-tuple-element.122), channel_id=1, source_target_pairs={{0,8},{4,12},{8,0},{12,4},{1,9},{5,13},{9,1},{13,5},{2,10},{6,14},... | collective-permute-start | bytes 1572872 | tf_op jit(solution)/shard_map/ppermute | solution.py:400
  220.3 29.0 %collective-permute-start.38 = (bf16[2,128,1024]{2,1,0:T(8,128)(2,1)S(1)}, bf16[2,128,1024]{2,1,0:T(8,128)(2,1)S(1)}, u32[]{:S(2)}, u32[]{:S(2)}) collective-permute-start(bf16[2,128,1024]{2,1,0:T(8,128)(2,1)S(1)} %get-tuple-element.123), channel_id=1, source_target_pairs={{0,12},{4,8},{8,4},{12,0},{1,13},{5,9},{9,5},{13,1},{2,14},{6,10},... | collective-permute-start | bytes 1572872 | tf_op jit(solution)/shard_map/ppermute | solution.py:400
  230.6 21.1 %collective-permute-start.41 = (bf16[2,256,256]{2,1,0:T(8,128)(2,1)S(1)}, bf16[2,256,256]{2,1,0:T(8,128)(2,1)S(1)}, u32[]{:S(2)}, u32[]{:S(2)}) collective-permute-start(bf16[2,256,256]{2,1,0:T(8,128)(2,1)S(1)} %collective-permute-done.40.refs_6_), channel_id=1, source_target_pairs={{0,1},{1,0},{2,3},{3,2},{4,5},{5,4},{6,7},{7,6},{8,9},{9,8},{10,11... | collective-permute-start | bytes 786440 | tf_op jit(solution)/shard_map/ppermute | solution.py:400
  288.1 29.2 %collective-permute-start.62 = (bf16[2,128,1024]{2,1,0:T(8,128)(2,1)}, bf16[2,128,1024]{2,1,0:T(8,128)(2,1)S(1)}, u32[]{:S(2)}, u32[]{:S(2)}) collective-permute-start(bf16[2,128,1024]{2,1,0:T(8,128)(2,1)} %get-tuple-element.131), channel_id=1, source_target_pairs={{0,4},{4,0},{8,12},{12,8},{1,5},{5,1},{9,13},{13,9},{2,6},{6,2},{1... | collective-permute-start | bytes 1572872 | tf_op jit(solution)/shard_map/ppermute | solution.py:400
  288.9 28.3 %collective-permute-start.63 = (bf16[2,128,1024]{2,1,0:T(8,128)(2,1)}, bf16[2,128,1024]{2,1,0:T(8,128)(2,1)S(1)}, u32[]{:S(2)}, u32[]{:S(2)}) collective-permute-start(bf16[2,128,1024]{2,1,0:T(8,128)(2,1)} %get-tuple-element.132), channel_id=1, source_target_pairs={{0,8},{4,12},{8,0},{12,4},{1,9},{5,13},{9,1},{13,5},{2,10},{6,14},... | collective-permute-start | bytes 1572872 | tf_op jit(solution)/shard_map/ppermute | solution.py:400
  289.8 27.5 %collective-permute-start.64 = (bf16[2,128,1024]{2,1,0:T(8,128)(2,1)}, bf16[2,128,1024]{2,1,0:T(8,128)(2,1)S(1)}, u32[]{:S(2)}, u32[]{:S(2)}) collective-permute-start(bf16[2,128,1024]{2,1,0:T(8,128)(2,1)} %get-tuple-element.133), channel_id=1, source_target_pairs={{0,12},{4,8},{8,4},{12,0},{1,13},{5,9},{9,5},{13,1},{2,14},{6,10},... | collective-permute-start | bytes 1572872 | tf_op jit(solution)/shard_map/ppermute | solution.py:400
  (48 other events, 722.6 us)

commit v3 on v2

v3 whole, which is shorter than its diff:
```python
import functools
import math

import jax
import jax.numpy as jnp
from jax import lax
from jax.experimental import pallas as pl
from jax.experimental.pallas import tpu as pltpu
from jax.sharding import PartitionSpec as P

D = 2048
NS_ITERS = 4
CHUNKS = (2, 2, 2)
VMEM_LIMIT = 24 * 1024 * 1024

beta_one = 0.9
beta_two = 0.999
bias_one = 1.0 - 0.9**10
bias_two = 1.0 - 0.999**10
eps_adam = 1e-08
galore_gain = 4.0
width_root = math.sqrt(D)

F32 = jnp.float32
BF16 = jnp.bfloat16


def dot_tn(a, b):
    return lax.dot_general(a, b, (((0,), (0,)), ((), ())), preferred_element_type=F32)


def dot_nn(a, b):
    return lax.dot_general(a, b, (((1,), (0,)), ((), ())), preferred_element_type=F32)


def dot_nt(a, b):
    return lax.dot_general(a, b, (((1,), (1,)), ((), ())), preferred_element_type=F32)


def split(a):
    high = a.astype(BF16)
    return high, (a - high.astype(F32)).astype(BF16)


def fine(dot, a, b):
    (ah, al), (bh, bl) = a, b
    return dot(ah, bh) + (dot(ah, bl) + dot(al, bh))


def call(body, grid, prefetch, ins, outs, scratch, aliases=None, vmem=VMEM_LIMIT):
    return pl.pallas_call(
        body,
        grid_spec=pltpu.PrefetchScalarGridSpec(
            num_scalar_prefetch=1,
            grid=grid,
            in_specs=[
                pl.BlockSpec(memory_space=pl.ANY) if b is None else pl.BlockSpec(b, m)
                for _, b, m in ins
            ],
            out_specs=[pl.BlockSpec(b, m) for _, _, b, m in outs],
            scratch_shapes=scratch,
        ),
        out_shape=[jax.ShapeDtypeStruct(s, d) for s, d, _, _ in outs],
        input_output_aliases=aliases or {},
        compiler_params=pltpu.CompilerParams(vmem_limit_bytes=vmem),
        cost_estimate=pl.CostEstimate(flops=1, bytes_accessed=1, transcendentals=0),
    )(prefetch, *[a for a, _, _ in ins])


def outgoing(place, gradient, k0, kc, tensors):
    rows, columns = gradient.shape[1:]
    width = columns // tensors
    n = tensors - 1

    def body(place_ref, *refs):
        for m in range(n):
            refs[n + m][...] = refs[m][...]

    return call(
        body,
        (kc,),
        place,
        [
            (gradient, (1, rows, width), lambda i, p, m=m: (k0 + i, 0, jnp.bitwise_xor(p[0], m)))
            for m in range(1, tensors)
        ],
        [((kc, rows, width), BF16, (1, rows, width), lambda i, p: (i, 0, 0))] * n,
        [],
        vmem=60 * 1024 * 1024 if k0 == 0 else VMEM_LIMIT,
    )


def gradient_ins(gradient, got, k0, pick=lambda i, p: i):
    kc, rows, width = got[0].shape
    return [(gradient, (1, rows, width), lambda i, p: (k0 + pick(i, p), 0, p[0]))] + [
        (g, (1, rows, width), lambda i, p: (pick(i, p), 0, 0)) for g in got
    ]


def basis_ins(bases, k0):
    return [
        (a, (1,) + a.shape[1:], lambda i, p, n=a.shape[0]: (lax.rem(k0 + i, n), 0, 0))
        for group in bases
        for a in group
    ]


def basis_blocks(refs, bases, k0, core):
    refs = list(refs)
    blocks = []
    for group in bases:
        mine = refs.pop(0)[0]
        if len(group) == 2:
            owner = (k0 + pl.program_id(0)) // group[0].shape[0]
            mine = jnp.where(owner == core, mine, refs.pop(0)[0])
        blocks.append(mine)
    return blocks


def low_partial(place, gradient, bases, got, k0, sections):
    kc, rows, width = got[0].shape
    rank = bases[0][0].shape[2]
    part = width // sections
    n = len(bases)
    chosen = blocks_sent(sections)

    def body(place_ref, *refs):
        out, total = refs[-1 - len(chosen) : -1], refs[-1]
        blocks = basis_blocks(refs[n:], bases, k0, place_ref[2])
        acc = dot_tn(refs[0][0], blocks[0])
        for m in range(1, n):
            acc += dot_tn(refs[m][0], blocks[m])
        total[...] = acc
        z = place_ref[1]
        for j, block in enumerate(chosen):
            at = pl.multiple_of(block(z) * part, part)
            out[j][0] = total[pl.ds(at, part), :].astype(out[j].dtype)

    return call(
        body,
        (kc,),
        place,
        gradient_ins(gradient, got, k0) + basis_ins(bases, k0),
        [
            ((kc, part, rank), BF16 if j else F32, (1, part, rank), lambda i, p: (i, 0, 0))
            for j in range(len(chosen))
        ],
        [pltpu.VMEM((width, rank), F32)],
    )


def blocks_sent(sections):
    return [lambda z, m=m: jnp.bitwise_xor(z, m) for m in range(sections)]


def gather_into(whole, refs, gathered, z):
    refs = list(refs)
    part = refs[0].shape[-2]
    for j, group in enumerate(gathered):
        block = refs.pop(0)[0, 0]
        for _ in group[1:]:
            block = block + refs.pop(0)[0, 0]
        at = pl.multiple_of(jnp.bitwise_xor(z, j) * part, part)
        whole[pl.ds(at, part), :] = block


def update(place, terms, moment_m, moment_v, before, k0, joined):
    kc, part, rank = terms[0].shape
    n = len(terms)

    def body(place_ref, *refs):
        m_ref, v_ref = refs[n], refs[n + 1]
        *low_out, m_out, v_out = refs[-4 + joined :]
        total = refs[0][0]
        for j in range(1, n):
            total += refs[j][0].astype(F32)
        low_rank = total / width_root
        m_new = beta_one * m_ref[0] + (1.0 - beta_one) * low_rank
        v_new = beta_two * v_ref[0] + (1.0 - beta_two) * low_rank * low_rank
        step = m_new / bias_one / (jnp.sqrt(v_new / bias_two) + eps_adam)
        low_out[0][0, 0] = low_rank.astype(BF16)
        low_out[-1][int(joined), 0] = step.astype(BF16)
        m_out[0] = m_new
        v_out[0] = v_new

    here = lambda i, p: (k0 + i, 0, 0)
    block = (1, part, rank)
    ins = [(a, block, lambda i, p: (i, 0, 0)) for a in terms]
    ins += [(moment_m, block, here), (moment_v, block, here)]
    aliases = {}
    if before is not None:
        ins += [(b, None, None) for b in before]
        aliases = {n + 3: 2 - joined, n + 4: 3 - joined}
    return call(
        body,
        (kc,),
        place,
        ins,
        [
            (
                (1 + joined, kc, part, rank),
                BF16,
                (1 + joined, 1, part, rank),
                lambda i, p: (0, i, 0, 0),
            )
        ]
        * (2 - joined)
        + [
            (moment_m.shape, F32, block, here),
            (moment_v.shape, F32, block, here),
        ],
        [],
        aliases,
    )


def subspace_partial(place, gradient, got, gathered, k0, split_cores):
    kc, rows, width = got[0].shape
    flat = [r for group in gathered for r in group]
    part, rank = flat[0].shape[2:]
    n, s = len(got) + 1, len(flat)
    half = kc // 2

    def pick(i, p):
        if not split_cores:
            return i
        return jnp.where(i < half, 2 * i + p[2], 2 * (i - half) + 1 - p[2])

    def body(place_ref, *refs):
        out, whole = refs[-2:]
        gather_into(whole, refs[n : n + s], gathered, place_ref[1])
        for m in range(n):
            out[0, m] = dot_nn(refs[m][0], whole[...])

    return call(
        body,
        (kc,),
        place,
        gradient_ins(gradient, got, k0, pick)
        + [(r, (1, 1, part, rank), lambda i, p: (0, pick(i, p), 0, 0)) for r in flat],
        [((kc, n, rows, rank), F32, (1, n, rows, rank), lambda i, p: (i, 0, 0, 0))],
        [pltpu.VMEM((width, rank), BF16)],
    )[0]


def delta_parts(place, bases, gathered, k0):
    flat = [r for group in gathered for r in group]
    kc, part, rank = flat[0].shape[1:]
    rows = bases[0][0].shape[1]
    n, s = len(bases), len(flat)
    width = part * len(gathered)

    def body(place_ref, *refs):
        out, whole = refs[-1 - n : -1], refs[-1]
        gather_into(whole, refs[:s], gathered, place_ref[1])
        blocks = basis_blocks(refs[s:], bases, k0, place_ref[2])
        for m in range(n):
            out[m][0] = (-galore_gain / width_root * dot_nt(blocks[m], whole[...])).astype(BF16)

    return call(
        body,
        (kc,),
        place,
        [(r, (1, 1, part, rank), lambda i, p: (0, i, 0, 0)) for r in flat]
        + basis_ins(bases, k0),
        [((kc, rows, width), BF16, (1, rows, width), lambda i, p: (i, 0, 0))] * n,
        [pltpu.VMEM((width, rank), BF16)],
    )


def place_delta(place, parts, before, k0, matrices):
    kc, rows, width = parts[0].shape
    n = len(parts)

    def body(place_ref, *refs):
        out = refs[-1]
        for m in range(n):
            at = pl.multiple_of(jnp.bitwise_xor(place_ref[0], m) * width, width)
            out[0, :, pl.ds(at, width)] = refs[m][0]

    ins = [(p, (1, rows, width), lambda i, p: (i, 0, 0)) for p in parts]
    aliases = {}
    if before is not None:
        ins.append((before, None, None))
        aliases = {n + 1: 0}
    shape = (matrices, rows, n * width)
    return call(
        body,
        (kc,),
        place,
        ins,
        [(shape, BF16, (1, rows, n * width), lambda i, p: (k0 + i, 0, 0))],
        [],
        aliases,
    )[0]


def gram_parts(place, groups):
    n = len(groups[0])
    rows, rank = groups[0][0].shape[1:]
    counts = [g[0].shape[0] for g in groups]
    total = sum(counts)
    part = rank // n
    flat = [p for g in groups for p in g]

    def body(place_ref, *refs):
        pieces, sub, out, whole = refs[: len(flat)], refs[len(flat)], refs[len(flat) + 1 : -1], refs[-1]
        at = 0
        for j, count in enumerate(counts):
            for i in range(count):
                acc = pieces[j * n][i]
                for m in range(1, n):
                    acc += pieces[j * n + m][i]
                sub[at] = acc
                high = split(acc)
                whole[at] = fine(dot_tn, high, high)
                at += 1
        for m in range(n):
            start = pl.multiple_of(jnp.bitwise_xor(place_ref[0], m) * part, part)
            for i in range(total):
                out[m][i] = whole[i, pl.ds(start, part), :]

    zero3 = lambda i, p: (0, 0, 0)
    res = call(
        body,
        (1,),
        place,
        [(p, p.shape, zero3) for p in flat],
        [((total, rows, rank), F32, (total, rows, rank), zero3)]
        + [((total, part, rank), F32, (total, part, rank), zero3)] * n,
        [pltpu.VMEM((total, rank, rank), F32)],
    )
    return res[0], res[1:]


def newton_schulz(place, pieces, sub):
    n = len(pieces)
    total, rows, rank = sub.shape
    part = rank // n

    def body(place_ref, *refs):
        p, s, out, whole = refs[:n], refs[n], refs[n + 1], refs[-1]
        for m in range(n):
            start = pl.multiple_of(jnp.bitwise_xor(place_ref[0], m) * part, part)
            for i in range(total):
                whole[i, pl.ds(start, part), :] = p[m][i]
        row = lax.broadcasted_iota(jnp.int32, (rank, rank), 0)
        col = lax.broadcasted_iota(jnp.int32, (rank, rank), 1)
        eye = jnp.where(row == col, 1.0, 0.0).astype(F32)
        iters, grams, prods = [], [], []
        for i in range(total):
            gram = whole[i]
            bound = jnp.max(jnp.sum(jnp.abs(gram), axis=1, keepdims=True), axis=0, keepdims=True) + 1e-06
            iters.append(s[i] / jnp.sqrt(bound))
            grams.append(gram / bound)
            prods.append(None)
        for turn in range(NS_ITERS):
            for i in range(total):
                factor = 1.5 * eye - 0.5 * grams[i]
                f = split(factor)
                prods[i] = factor if turn == 0 else fine(dot_nn, split(prods[i]), f)
                if turn + 1 < NS_ITERS:
                    half = fine(dot_nn, split(grams[i]), f)
                    grams[i] = fine(dot_nn, split(half), f)
        for i in range(total):
            res = fine(dot_nn, split(iters[i]), split(prods[i]))
            out[i] = (width_root * res).astype(BF16)

    zero3 = lambda i, p: (0, 0, 0)
    return call(
        body,
        (1,),
        place,
        [(p, p.shape, zero3) for p in pieces] + [(sub, sub.shape, zero3)],
        [((total, rows, rank), BF16, (total, rows, rank), zero3)],
        [pltpu.VMEM((total, rank, rank), F32)],
    )[0]


def after(x, *others):
    return lax.optimization_barrier((x, others))[0]


def per_device(shape, gradient, basis, moment_m, moment_v):
    tensors, sections, cores = shape["tensor"], shape["section"], shape["shard"]
    t, z, c = (lax.axis_index(a) for a in ("tensor", "section", "shard"))
    place = jnp.stack([t, z, c]).astype(jnp.int32)
    matrices = gradient.shape[0]
    split_cores = cores == 2
    n = len(CHUNKS)
    starts = [sum(CHUNKS[:j]) for j in range(n)]

    def swap(x, axis, m):
        return lax.ppermute(x, axis, [(i, i ^ m) for i in range(shape[axis])])

    token = ()

    def event(*values):
        nonlocal token, place
        token = values
        place = after(place, *values)

    def send(x, axis, m):
        return swap(after(x, *token), axis, m)

    def other_core(x):
        return lax.ppermute(after(x, *token), "shard", [(0, 1), (1, 0)])

    def send_all(cut):
        return [send(cut[m - 1], "tensor", m) for m in range(1, tensors)]

    grads, parts, sums, roughs, steps, cuts, subs, groups = ({} for _ in range(8))
    state = {"news": None, "delta": None}
    wide = sections != 4

    def cut(j):
        cuts[j] = outgoing(place, gradient, starts[j], CHUNKS[j], tensors)
        event(*cuts[j])

    def send_grads(j):
        grads[j] = send_all(cuts[j])

    def wait_grads(j):
        event(*grads[j])

    def low(j):
        parts[j] = low_partial(place, gradient, bases, grads[j], starts[j], sections)
        event(*parts[j])

    def sum_far(j):
        sums[j] = [parts[j][0]] + [None] * (sections - 1)
        if wide:
            sums[j][1:] = [send(x, "section", m + 1) for m, x in enumerate(parts[j][1:])]
        else:
            sums[j][2] = send(parts[j][3], "section", 1)
            sums[j].pop()

    def sum_near(j):
        if not wide:
            sums[j][1] = send(parts[j][1], "section", 1)

    def sum_two(j):
        if not wide:
            event(sums[j][2])
            both = parts[j][2].astype(F32) + sums[j][2].astype(F32)
            sums[j][2] = send(both.astype(BF16), "section", 2)

    def step(j):
        event(*sums[j])
        *low_out, m_new, v_new = update(
            place, sums[j], moment_m, moment_v, state["news"], starts[j], False
        )
        state["news"] = [m_new, v_new]
        roughs[j], steps[j] = [[[x]] + [None] * (sections - 1) for x in low_out]
        event(*low_out)

    def gather_two(held):
        if wide:
            held[1:] = [[send(held[0][0], "section", m)] for m in range(1, sections)]
        else:
            held[2] = [send(held[0][0], "section", 2)]

    def gather_near(held):
        if not wide:
            held[1] = [send(held[0][0], "section", 1)]

    def gather_far(held):
        if not wide:
            event(held[2][0])
            held[3] = [send(held[2][0], "section", 1)]

    def hop(x, pairs):
        return lax.ppermute(after(x, *token), "section", pairs)

    inwards, across, outwards = ((0, 1), (3, 2)), ((1, 2), (2, 1)), ((1, 0), (2, 3))

    def sum_in(j):
        sums[j] = {"own": parts[j][0]}
        if wide:
            sums[j]["all"] = [send(x, "section", m + 1) for m, x in enumerate(parts[j][1:])]
        else:
            sums[j]["end"] = hop(parts[j][3], inwards)

    def sum_in_two(j):
        if not wide:
            sums[j]["inner"] = hop(parts[j][2], inwards)

    def merged(x, y):
        return (x.astype(F32) + y.astype(F32)).astype(BF16)

    def sum_across(j):
        if not wide:
            event(sums[j]["end"])
            sums[j]["end"] = hop(merged(parts[j][2], sums[j]["end"]), across)

    def sum_across_two(j):
        if not wide:
            event(sums[j]["inner"])
            sums[j]["inner"] = hop(merged(parts[j][3], sums[j]["inner"]), across)

    def sum_out(j):
        if wide:
            sums[j] = [sums[j]["own"]] + sums[j]["all"]
        else:
            event(sums[j]["end"])
            last = send(merged(parts[j][1], sums[j]["end"]), "section", 1)
            sums[j] = [sums[j]["own"], sums[j]["inner"], last]

    def spread_across(held):
        if not wide:
            held[3] = [hop(held[0][0], across)]

    def spread_across_two(held):
        if not wide:
            event(held[1][0])
            held[2] = [hop(held[1][0], across)]

    def spread_out(held):
        if not wide:
            event(held[3][0])
            held[2].append(hop(held[3][0], outwards))

    def spread_out_two(held):
        if wide:
            gather_two(held)
        else:
            event(held[2][0])
            held[3].append(hop(held[2][0], outwards))

    def rough_across(j):
        spread_across(roughs[j])

    def rough_across_two(j):
        spread_across_two(roughs[j])

    def rough_out(j):
        spread_out(roughs[j])

    def rough_out_two(j):
        spread_out_two(roughs[j])

    def step_across(j):
        spread_across(steps[j])

    def step_across_two(j):
        spread_across_two(steps[j])

    def step_out(j):
        spread_out(steps[j])

    def step_out_two(j):
        spread_out_two(steps[j])

    def rough_two(j):
        gather_two(roughs[j])

    def rough_near(j):
        gather_near(roughs[j])

    def rough_far(j):
        gather_far(roughs[j])

    def step_two(j):
        gather_two(steps[j])

    def step_near(j):
        gather_near(steps[j])

    def step_far(j):
        gather_far(steps[j])

    def subspace(j):
        event(roughs[j])
        subs[j] = subspace_partial(place, gradient, grads[j], roughs[j], starts[j], split_cores)
        event(subs[j])

    def share(j):
        if split_cores:
            groups[j] = other_core(subs[j][CHUNKS[j] // 2 :])
        else:
            groups[j] = lax.psum(subs[j], "shard")

    def spread(j):
        event(groups[j])
        total = groups[j]
        if split_cores:
            total = total + subs[j][: CHUNKS[j] // 2]
        groups[j] = [total[:, 0]] + [send(total[:, m], "tensor", m) for m in range(1, tensors)]

    def wait_spread(j):
        event(*groups[j])

    def delta(j):
        event(steps[j])
        cuts[j] = delta_parts(place, bases, steps[j], starts[j])
        event(*cuts[j])

    def send_delta(j):
        cuts[j] = [cuts[j][0]] + send_all(cuts[j][1:])

    def put(j):
        event(*cuts[j])
        state["delta"] = place_delta(place, cuts[j], state["delta"], starts[j], matrices)
        event(state["delta"])

    def fetch():
        mine = basis
        if split_cores:
            mine = lax.dynamic_slice_in_dim(basis, c * (matrices // 2), matrices // 2, 0)
            event(mine)
        bases.extend([send(mine, "tensor", m)] for m in range(1, tensors))

    def hand_over():
        if split_cores:
            event(*[group[0] for group in bases[1:]])
            for group in bases[1:]:
                group.append(other_core(group[0]))

    def gram_kernel():
        state["sub"], state["gram"] = gram_parts(place, [groups[j] for j in range(n)])
        event(*state["gram"])

    def gram_send():
        cut = state["gram"]
        state["gram"] = [cut[0]] + send_all(cut[1:])

    def gram_sum():
        event(*state["gram"])
        state["gram"] = functools.reduce(jnp.add, state["gram"])
        state["reach"] = 1

    def gram_hop():
        state["hop"] = send(state["gram"], "section", state["reach"])
        state["reach"] *= 2

    def gram_add():
        event(state["hop"])
        state["gram"] = state["gram"] + state["hop"]

    def gram_gather():
        gram = state["gram"]
        state["gram"] = [gram] + [send(gram, "tensor", m) for m in range(1, tensors)]

    def newton():
        event(*state["gram"])
        state["done"] = newton_schulz(place, state["gram"], state["sub"])
        event(state["done"])

    def finish():
        done = state["done"]
        if split_cores:
            theirs = other_core(done)
            even = jnp.where(c == 0, done, theirs)
            odd = jnp.where(c == 0, theirs, done)
            done = jnp.stack([even, odd], 1).reshape(basis.shape)
        state["done"] = done

    bases = [[basis]]
    fetch()
    cut(0)
    hand_over()
    send_grads(0)
    cut(1)
    wait_grads(0)
    send_grads(1)
    low(0)
    sum_far(0)
    sum_near(0)
    sum_two(0)
    cut(2)
    step(0)
    step_two(0)
    rough_two(0)
    rough_near(0)
    wait_grads(1)
    send_grads(2)
    low(1)
    sum_far(1)
    sum_near(1)
    rough_far(0)
    sum_two(1)
    subspace(0)
    share(0)
    step_near(0)
    step(1)
    rough_two(1)
    rough_near(1)
    wait_grads(2)
    step_far(0)
    low(2)
    sum_far(2)
    sum_near(2)
    rough_far(1)
    sum_two(2)
    delta(0)
    spread(0)
    subspace(1)
    share(1)
    send_delta(0)
    step(2)
    rough_two(2)
    rough_near(2)
    rough_far(2)
    subspace(2)
    step_two(1)
    step_near(1)
    spread(1)
    put(0)
    share(2)
    step_far(1)
    step_two(2)
    step_near(2)
    spread(2)
    wait_spread(1)
    delta(1)
    send_delta(1)
    wait_spread(0)
    step_far(2)
    wait_spread(2)
    gram_kernel()
    gram_send()
    gram_sum()
    gram_hop()
    put(1)
    delta(2)
    gram_add()
    gram_hop()
    gram_add()
    gram_gather()
    newton()
    send_delta(2)
    finish()
    put(2)
    return (state["delta"], state["done"], *state["news"])


def solution(mesh):
    placed = (
        P(None, ("tensor", "section"), "shard"),
        P(None, ("tensor", "section"), None),
        P(None, ("shard", "tensor", "section"), None),
        P(None, ("shard", "tensor", "section"), None),
    )
    return jax.shard_map(
        functools.partial(per_device, dict(mesh.shape)),
        mesh=mesh,
        in_specs=placed,
        out_specs=placed,
        check_vma=False,
    )
```

time: 320 us -> 310 us (0.969)
  starting transfers between devices: 95.9 us -> 68.7 us
  waiting for transfers between devices: 177 us -> 192 us
    ppermute x62 -> x65, starting transfers between devices: 95.7 us -> 68 us  [swap(): return lax.ppermute(x, axis, [(i, i ^ m) for i in range(shape[axis])])]
    ppermute x62 -> x65, waiting for transfers between devices: 177 us -> 192 us  [swap(): return lax.ppermute(x, axis, [(i, i ^ m) for i in range(shape[axis])])]
  transfers between devices with their start and end apart: 66 -> 72, of which waited for: 32 -> 38; matrix products, arithmetic and copies ran while one was open for 0% -> 1% of each run, Pallas kernels for 10% -> 9%
where the time goes in v3:
time: 310 us
  waiting for transfers between devices  192 us (62%)
  starting transfers between devices  68.7 us (22%)
  Pallas kernels  42 us (14%)
  local copies, waits for them, and re-layouts  4.74 us (2%)
    ppermute x65, waiting for transfers between devices, swap(): return lax.ppermute(x, axis, [(i, i ^ m) for i in range(shape[axis])])  192 us
    ppermute x65, starting transfers between devices, swap(): return lax.ppermute(x, axis, [(i, i ^ m) for i in range(shape[axis])])  68 us
    pallas_call x20, Pallas kernels, call(): pl.pallas_call(body, grid_spec=pltpu.PrefetchScalarGridSpec(num_scalar_pr...  42 us
  transfers between devices with their start and end apart: 72, of which 38 were waited for; matrix products, arithmetic and copies ran while one was open for 1% of the time, Pallas kernels for 9%

profile of v3, /device:TPU:0, one launch (start us, length us, event | category | flops | bytes accessed | tf_op | source)
XLA Modules:
  0.0 309.6 jit_solution(8735757157247692304)
XLA Ops:
  10.3 4.8 %collective-permute-done.1.refs_7_ = bf16[3,128,256]{2,1,0:T(8,128)(2,1)S(1)} collective-permute-done((bf16[3,128,256]{2,1,0:T(8,128)(2,1)S(1)}, bf16[3,128,256]{2,1,0:T(8,128)(2,1)S(1)}, u32[]{:S(2)}, u32[]{:S(2)}) %collective-permute-start.1) | collective-permute-done | bytes 196640 | tf_op jit(solution)/shard_map/ppermute | solution.py:394
  19.2 11.1 %collective-permute-done.3.refs_1_ = bf16[2,128,1024]{2,1,0:T(8,128)(2,1)S(1)} collective-permute-done((bf16[2,128,1024]{2,1,0:T(8,128)(2,1)}, bf16[2,128,1024]{2,1,0:T(8,128)(2,1)S(1)}, u32[]{:S(2)}, u32[]{:S(2)}) %collective-permute-start.3) | collective-permute-done | bytes 524320 | tf_op jit(solution)/shard_map/ppermute | solution.py:394
  33.9 6.5 %collective-permute-done.4.refs_2_ = bf16[2,128,1024]{2,1,0:T(8,128)(2,1)S(1)} collective-permute-done((bf16[2,128,1024]{2,1,0:T(8,128)(2,1)}, bf16[2,128,1024]{2,1,0:T(8,128)(2,1)S(1)}, u32[]{:S(2)}, u32[]{:S(2)}) %collective-permute-start.4) | collective-permute-done | bytes 524320 | tf_op jit(solution)/shard_map/ppermute | solution.py:394
  48.2 6.0 %collective-permute-done.9 = bf16[2,256,256]{2,1,0:T(8,128)(2,1)S(1)} collective-permute-done((bf16[2,256,256]{2,1,0:T(8,128)(2,1)S(1)}, bf16[2,256,256]{2,1,0:T(8,128)(2,1)S(1)}, u32[]{:S(2)}, u32[]{:S(2)}) %collective-permute-start.9) | collective-permute-done | bytes 262176 | tf_op jit(solution)/shard_map/ppermute | solution.py:394
  57.1 7.4 %collective-permute-done.11.refs_2_ = bf16[2,256,256]{2,1,0:T(8,128)(2,1)S(1)} collective-permute-done((bf16[2,256,256]{2,1,0:T(8,128)(2,1)S(1)}, bf16[2,256,256]{2,1,0:T(8,128)(2,1)S(1)}, u32[]{:S(2)}, u32[]{:S(2)}) %collective-permute-start.11) | collective-permute-done | bytes 262176 | tf_op jit(solution)/shard_map/ppermute | solution.py:394
  83.9 4.4 %collective-permute-done.17.refs_5_ = bf16[1,2,256,256]{3,2,1,0:T(8,128)(2,1)S(1)} collective-permute-done((bf16[1,2,256,256]{3,2,1,0:T(8,128)(2,1)S(1)}, bf16[1,2,256,256]{3,2,1,0:T(8,128)(2,1)S(1)}, u32[]{:S(2)}, u32[]{:S(2)}) %collective-permute-start.17) | collective-permute-done | bytes 262176 | tf_op jit(solution)/shard_map/ppermute | solution.py:394
  89.0 5.5 %collective-permute-done.19.refs_1_ = bf16[2,256,256]{2,1,0:T(8,128)(2,1)S(1)} collective-permute-done((bf16[2,256,256]{2,1,0:T(8,128)(2,1)S(1)}, bf16[2,256,256]{2,1,0:T(8,128)(2,1)S(1)}, u32[]{:S(2)}, u32[]{:S(2)}) %collective-permute-start.19) | collective-permute-done | bytes 262176 | tf_op jit(solution)/shard_map/ppermute | solution.py:394
  95.7 4.7 %collective-permute-done.18.refs_7_ = bf16[1,2,256,256]{3,2,1,0:T(8,128)(2,1)S(1)} collective-permute-done((bf16[1,2,256,256]{3,2,1,0:T(8,128)(2,1)S(1)}, bf16[1,2,256,256]{3,2,1,0:T(8,128)(2,1)S(1)}, u32[]{:S(2)}, u32[]{:S(2)}) %collective-permute-start.18) | collective-permute-done | bytes 262176 | tf_op jit(solution)/shard_map/ppermute | solution.py:394
  102.1 10.7 %collective-permute-done.20.refs_2_ = bf16[2,256,256]{2,1,0:T(8,128)(2,1)S(1)} collective-permute-done((bf16[2,256,256]{2,1,0:T(8,128)(2,1)S(1)}, bf16[2,256,256]{2,1,0:T(8,128)(2,1)S(1)}, u32[]{:S(2)}, u32[]{:S(2)}) %collective-permute-start.20) | collective-permute-done | bytes 262176 | tf_op jit(solution)/shard_map/ppermute | solution.py:394
  123.0 4.3 %collective-permute-done.25.refs_6_ = bf16[1,2,256,256]{3,2,1,0:T(8,128)(2,1)S(1)} collective-permute-done((bf16[1,2,256,256]{3,2,1,0:T(8,128)(2,1)S(1)}, bf16[1,2,256,256]{3,2,1,0:T(8,128)(2,1)S(1)}, u32[]{:S(2)}, u32[]{:S(2)}) %collective-permute-start.25) | collective-permute-done | bytes 262176 | tf_op jit(solution)/shard_map/ppermute | solution.py:394
  127.3 4.7 %collective-permute-done.26 = bf16[2,256,256]{2,1,0:T(8,128)(2,1)S(1)} collective-permute-done((bf16[2,256,256]{2,1,0:T(8,128)(2,1)S(1)}, bf16[2,256,256]{2,1,0:T(8,128)(2,1)S(1)}, u32[]{:S(2)}, u32[]{:S(2)}) %collective-permute-start.26) | collective-permute-done | bytes 262176 | tf_op jit(solution)/shard_map/ppermute | solution.py:394
  132.1 5.5 %collective-permute-done.28.refs_3_ = bf16[1,2,256,256]{3,2,1,0:T(8,128)(2,1)S(1)} collective-permute-done((bf16[1,2,256,256]{3,2,1,0:T(8,128)(2,1)S(1)}, bf16[1,2,256,256]{3,2,1,0:T(8,128)(2,1)S(1)}, u32[]{:S(2)}, u32[]{:S(2)}) %collective-permute-start.28) | collective-permute-done | bytes 262176 | tf_op jit(solution)/shard_map/ppermute | solution.py:394
  137.6 8.4 %collective-permute-done.27.refs_1_ = bf16[1,2,256,256]{3,2,1,0:T(8,128)(2,1)S(1)} collective-permute-done((bf16[1,2,256,256]{3,2,1,0:T(8,128)(2,1)S(1)}, bf16[1,2,256,256]{3,2,1,0:T(8,128)(2,1)S(1)}, u32[]{:S(2)}, u32[]{:S(2)}) %collective-permute-start.27) | collective-permute-done | bytes 262176 | tf_op jit(solution)/shard_map/ppermute | solution.py:394
  148.3 6.1 %collective-permute-done.30.refs_5_ = bf16[1,2,256,256]{3,2,1,0:T(8,128)(2,1)S(1)} collective-permute-done((bf16[1,2,256,256]{3,2,1,0:T(8,128)(2,1)S(1)}, bf16[1,2,256,256]{3,2,1,0:T(8,128)(2,1)S(1)}, u32[]{:S(2)}, u32[]{:S(2)}) %collective-permute-start.30) | collective-permute-done | bytes 262176 | tf_op jit(solution)/shard_map/ppermute | solution.py:394
  154.5 5.6 %collective-permute-done.31.refs_7_ = bf16[1,2,256,256]{3,2,1,0:T(8,128)(2,1)S(1)} collective-permute-done((bf16[1,2,256,256]{3,2,1,0:T(8,128)(2,1)S(1)}, bf16[1,2,256,256]{3,2,1,0:T(8,128)(2,1)S(1)}, u32[]{:S(2)}, u32[]{:S(2)}) %collective-permute-start.31) | collective-permute-done | bytes 262176 | tf_op jit(solution)/shard_map/ppermute | solution.py:394
  170.1 7.3 %collective-permute-done.34.refs_6_ = bf16[1,2,256,256]{3,2,1,0:T(8,128)(2,1)S(1)} collective-permute-done((bf16[1,2,256,256]{3,2,1,0:T(8,128)(2,1)S(1)}, bf16[1,2,256,256]{3,2,1,0:T(8,128)(2,1)S(1)}, u32[]{:S(2)}, u32[]{:S(2)}) %collective-permute-start.34) | collective-permute-done | bytes 262176 | tf_op jit(solution)/shard_map/ppermute | solution.py:394
  178.7 7.3 %collective-permute-done.36.refs_7_ = bf16[1,2,256,256]{3,2,1,0:T(8,128)(2,1)S(1)} collective-permute-done((bf16[1,2,256,256]{3,2,1,0:T(8,128)(2,1)S(1)}, bf16[1,2,256,256]{3,2,1,0:T(8,128)(2,1)S(1)}, u32[]{:S(2)}, u32[]{:S(2)}) %collective-permute-start.36) | collective-permute-done | bytes 262176 | tf_op jit(solution)/shard_map/ppermute | solution.py:394
  187.8 7.6 %collective-permute-done.39.refs_2_ = bf16[2,128,1024]{2,1,0:T(8,128)(2,1)S(1)} collective-permute-done((bf16[2,128,1024]{2,1,0:T(8,128)(2,1)S(1)}, bf16[2,128,1024]{2,1,0:T(8,128)(2,1)S(1)}, u32[]{:S(2)}, u32[]{:S(2)}) %collective-permute-start.39) | collective-permute-done | bytes 524320 | tf_op jit(solution)/shard_map/ppermute | solution.py:394
  201.6 11.7 %collective-permute-done.41.refs_2_ = bf16[1,2,256,256]{3,2,1,0:T(8,128)(2,1)S(1)} collective-permute-done((bf16[1,2,256,256]{3,2,1,0:T(8,128)(2,1)S(1)}, bf16[1,2,256,256]{3,2,1,0:T(8,128)(2,1)S(1)}, u32[]{:S(2)}, u32[]{:S(2)}) %collective-permute-start.41) | collective-permute-done | bytes 262176 | tf_op jit(solution)/shard_map/ppermute | solution.py:394
  249.1 7.5 %collective-permute-done.63 = f32[3,64,256]{2,1,0:T(8,128)S(1)} collective-permute-done((f32[3,64,256]{2,1,0:T(8,128)S(1)}, f32[3,64,256]{2,1,0:T(8,128)S(1)}, u32[]{:S(2)}, u32[]{:S(2)}) %collective-permute-start.63) | collective-permute-done | bytes 196640 | tf_op jit(solution)/shard_map/ppermute | solution.py:394
  259.3 6.1 %collective-permute-done.64 = f32[3,64,256]{2,1,0:T(8,128)S(1)} collective-permute-done((f32[3,64,256]{2,1,0:T(8,128)S(1)}, f32[3,64,256]{2,1,0:T(8,128)S(1)}, u32[]{:S(2)}, u32[]{:S(2)}) %collective-permute-start.64) | collective-permute-done | bytes 196640 | tf_op jit(solution)/shard_map/ppermute | solution.py:394
  275.9 5.1 %shard_map.93 = bf16[3,128,256]{2,1,0:T(8,128)(2,1)S(1)} custom-call(s32[3]{0:T(128)S(1)} %copy-done.4, f32[3,64,256]{2,1,0:T(8,128)S(1)} %add.47.refs_0_, f32[3,64,256]{2,1,0:T(8,128)S(1)} %collective-permute-done.65.refs_1_, f32[3,64,256]{2,1,0:T(8,128)S(1)} %collective-permute-done.66.refs_2_, f32[3,64,256]{2,1,0:T(8,128)S(1)} %collective-permute-done.67.refs_3_, ...), custom_call_target="tpu_custom_call" | custom-call | flops 1 | bytes 1 | tf_op jit(solution)/shard_map/pallas_call | solution.py:51
  285.6 10.6 %collective-permute-done.68.refs_1_ = bf16[2,128,1024]{2,1,0:T(8,128)(2,1)S(1)} collective-permute-done((bf16[2,128,1024]{2,1,0:T(8,128)(2,1)}, bf16[2,128,1024]{2,1,0:T(8,128)(2,1)S(1)}, u32[]{:S(2)}, u32[]{:S(2)}) %collective-permute-start.68) | collective-permute-done | bytes 524320 | tf_op jit(solution)/shard_map/ppermute | solution.py:394
  296.1 11.5 %collective-permute-done.69.refs_2_ = bf16[2,128,1024]{2,1,0:T(8,128)(2,1)S(1)} collective-permute-done((bf16[2,128,1024]{2,1,0:T(8,128)(2,1)}, bf16[2,128,1024]{2,1,0:T(8,128)(2,1)S(1)}, u32[]{:S(2)}, u32[]{:S(2)}) %collective-permute-start.69) | collective-permute-done | bytes 524320 | tf_op jit(solution)/shard_map/ppermute | solution.py:394
  (175 shorter events, 138.1 us)
Async XLA Ops:
  16.4 24.0 %collective-permute-start.4 = (bf16[2,128,1024]{2,1,0:T(8,128)(2,1)}, bf16[2,128,1024]{2,1,0:T(8,128)(2,1)S(1)}, u32[]{:S(2)}, u32[]{:S(2)}) collective-permute-start(bf16[2,128,1024]{2,1,0:T(8,128)(2,1)} %get-tuple-element.184), channel_id=1, source_target_pairs={{0,8},{4,12},{8,0},{12,4},{1,9},{5,13},{9,1},{13,5},{2,10},{6,14},... | collective-permute-start | bytes 1572872 | tf_op jit(solution)/shard_map/ppermute | solution.py:394
  17.2 23.1 %collective-permute-start.5 = (bf16[2,128,1024]{2,1,0:T(8,128)(2,1)}, bf16[2,128,1024]{2,1,0:T(8,128)(2,1)S(1)}, u32[]{:S(2)}, u32[]{:S(2)}) collective-permute-start(bf16[2,128,1024]{2,1,0:T(8,128)(2,1)} %get-tuple-element.185), channel_id=1, source_target_pairs={{0,12},{4,8},{8,4},{12,0},{1,13},{5,9},{9,5},{13,1},{2,14},{6,10},... | collective-permute-start | bytes 1572872 | tf_op jit(solution)/shard_map/ppermute | solution.py:394
  18.7 21.7 %collective-permute-start.6 = (bf16[3,128,256]{2,1,0:T(8,128)(2,1)S(1)}, bf16[3,128,256]{2,1,0:T(8,128)(2,1)S(1)}, u32[]{:S(2)}, u32[]{:S(2)}) collective-permute-start(bf16[3,128,256]{2,1,0:T(8,128)(2,1)S(1)} %collective-permute-done.refs_5_), channel_id=1, source_target_pairs={{0,16},{16,0},{1,17},{17,1},{2,18},{18,2},{3,19},{19,3},{4,20},{20... | collective-permute-start | bytes 589832 | tf_op jit(solution)/shard_map/ppermute | solution.py:407
  18.7 21.7 %collective-permute-start.7 = (bf16[3,128,256]{2,1,0:T(8,128)(2,1)S(1)}, bf16[3,128,256]{2,1,0:T(8,128)(2,1)S(1)}, u32[]{:S(2)}, u32[]{:S(2)}) collective-permute-start(bf16[3,128,256]{2,1,0:T(8,128)(2,1)S(1)} %collective-permute-done.1.refs_7_), channel_id=1, source_target_pairs={{0,16},{16,0},{1,17},{17,1},{2,18},{18,2},{3,19},{19,3},{4,20},{20... | collective-permute-start | bytes 589832 | tf_op jit(solution)/shard_map/ppermute | solution.py:407
  44.3 22.1 %collective-permute-start.12 = (bf16[2,128,1024]{2,1,0:T(8,128)(2,1)S(1)}, bf16[2,128,1024]{2,1,0:T(8,128)(2,1)S(1)}, u32[]{:S(2)}, u32[]{:S(2)}) collective-permute-start(bf16[2,128,1024]{2,1,0:T(8,128)(2,1)S(1)} %get-tuple-element.207), channel_id=1, source_target_pairs={{0,4},{4,0},{8,12},{12,8},{1,5},{5,1},{9,13},{13,9},{2,6},{6,2},{1... | collective-permute-start | bytes 1572872 | tf_op jit(solution)/shard_map/ppermute | solution.py:394
  44.9 22.0 %collective-permute-start.13 = (bf16[2,128,1024]{2,1,0:T(8,128)(2,1)S(1)}, bf16[2,128,1024]{2,1,0:T(8,128)(2,1)S(1)}, u32[]{:S(2)}, u32[]{:S(2)}) collective-permute-start(bf16[2,128,1024]{2,1,0:T(8,128)(2,1)S(1)} %get-tuple-element.208), channel_id=1, source_target_pairs={{0,8},{4,12},{8,0},{12,4},{1,9},{5,13},{9,1},{13,5},{2,10},{6,14},... | collective-permute-start | bytes 1572872 | tf_op jit(solution)/shard_map/ppermute | solution.py:394
  46.0 20.9 %collective-permute-start.14 = (bf16[2,128,1024]{2,1,0:T(8,128)(2,1)S(1)}, bf16[2,128,1024]{2,1,0:T(8,128)(2,1)S(1)}, u32[]{:S(2)}, u32[]{:S(2)}) collective-permute-start(bf16[2,128,1024]{2,1,0:T(8,128)(2,1)S(1)} %get-tuple-element.209), channel_id=1, source_target_pairs={{0,12},{4,8},{8,4},{12,0},{1,13},{5,9},{9,5},{13,1},{2,14},{6,10},... | collective-permute-start | bytes 1572872 | tf_op jit(solution)/shard_map/ppermute | solution.py:394
  73.8 20.7 %collective-permute-start.19 = (bf16[2,256,256]{2,1,0:T(8,128)(2,1)S(1)}, bf16[2,256,256]{2,1,0:T(8,128)(2,1)S(1)}, u32[]{:S(2)}, u32[]{:S(2)}) collective-permute-start(bf16[2,256,256]{2,1,0:T(8,128)(2,1)S(1)} %get-tuple-element.223), channel_id=1, source_target_pairs={{0,1},{1,0},{2,3},{3,2},{4,5},{5,4},{6,7},{7,6},{8,9},{9,8},{10,11... | collective-permute-start | bytes 786440 | tf_op jit(solution)/shard_map/ppermute | solution.py:394
  74.3 40.4 %collective-permute-start.21 = (bf16[2,128,1024]{2,1,0:T(8,128)(2,1)S(1)}, bf16[2,128,1024]{2,1,0:T(8,128)(2,1)S(1)}, u32[]{:S(2)}, u32[]{:S(2)}) collective-permute-start(bf16[2,128,1024]{2,1,0:T(8,128)(2,1)S(1)} %get-tuple-element.231), channel_id=1, source_target_pairs={{0,4},{4,0},{8,12},{12,8},{1,5},{5,1},{9,13},{13,9},{2,6},{6,2},{1... | collective-permute-start | bytes 1572872 | tf_op jit(solution)/shard_map/ppermute | solution.py:394
  77.8 36.9 %collective-permute-start.22 = (bf16[2,128,1024]{2,1,0:T(8,128)(2,1)S(1)}, bf16[2,128,1024]{2,1,0:T(8,128)(2,1)S(1)}, u32[]{:S(2)}, u32[]{:S(2)}) collective-permute-start(bf16[2,128,1024]{2,1,0:T(8,128)(2,1)S(1)} %get-tuple-element.232), channel_id=1, source_target_pairs={{0,8},{4,12},{8,0},{12,4},{1,9},{5,13},{9,1},{13,5},{2,10},{6,14},... | collective-permute-start | bytes 1572872 | tf_op jit(solution)/shard_map/ppermute | solution.py:394
  82.7 32.0 %collective-permute-start.23 = (bf16[2,128,1024]{2,1,0:T(8,128)(2,1)S(1)}, bf16[2,128,1024]{2,1,0:T(8,128)(2,1)S(1)}, u32[]{:S(2)}, u32[]{:S(2)}) collective-permute-start(bf16[2,128,1024]{2,1,0:T(8,128)(2,1)S(1)} %get-tuple-element.233), channel_id=1, source_target_pairs={{0,12},{4,8},{8,4},{12,0},{1,13},{5,9},{9,5},{13,1},{2,14},{6,10},... | collective-permute-start | bytes 1572872 | tf_op jit(solution)/shard_map/ppermute | solution.py:394
  120.8 27.5 %collective-permute-start.29 = (f32[1,4,128,256]{3,2,1,0:T(8,128)S(1)}, f32[1,4,128,256]{3,2,1,0:T(8,128)S(1)}, u32[]{:S(2)}, u32[]{:S(2)}) collective-permute-start(f32[1,4,128,256]{3,2,1,0:T(8,128)S(1)} %slice.72), channel_id=1, source_target_pairs={{0,16},{16,0},{1,17},{17,1},{2,18},{18,2},{3,19},{19,3},{4,20},{20... | collective-permute-start | bytes 1572872 | tf_op jit(solution)/shard_map/ppermute | solution.py:407
  121.0 25.0 %collective-permute-start.27 = (bf16[1,2,256,256]{3,2,1,0:T(8,128)(2,1)S(1)}, bf16[1,2,256,256]{3,2,1,0:T(8,128)(2,1)S(1)}, u32[]{:S(2)}, u32[]{:S(2)}) collective-permute-start(bf16[1,2,256,256]{3,2,1,0:T(8,128)(2,1)S(1)} %get-tuple-element.246.refs_0_), channel_id=1, source_target_pairs={{0,1},{1,0},{2,3},{3,2},{4,5},{5,4},{6,7},{7,6},{8,9},{9,8},{10,11... | collective-permute-start | bytes 786440 | tf_op jit(solution)/shard_map/ppermute | solution.py:394
  127.3 27.1 %collective-permute-start.30 = (bf16[1,2,256,256]{3,2,1,0:T(8,128)(2,1)S(1)}, bf16[1,2,256,256]{3,2,1,0:T(8,128)(2,1)S(1)}, u32[]{:S(2)}, u32[]{:S(2)}) collective-permute-start(bf16[1,2,256,256]{3,2,1,0:T(8,128)(2,1)S(1)} %get-tuple-element.242.refs_4_), channel_id=1, source_target_pairs={{0,1},{1,0},{2,3},{3,2},{4,5},{5,4},{6,7},{7,6},{8,9},{9,8},{10,11... | collective-permute-start | bytes 786440 | tf_op jit(solution)/shard_map/ppermute | solution.py:394
  132.0 28.1 %collective-permute-start.31 = (bf16[1,2,256,256]{3,2,1,0:T(8,128)(2,1)S(1)}, bf16[1,2,256,256]{3,2,1,0:T(8,128)(2,1)S(1)}, u32[]{:S(2)}, u32[]{:S(2)}) collective-permute-start(bf16[1,2,256,256]{3,2,1,0:T(8,128)(2,1)S(1)} %collective-permute-done.25.refs_6_), channel_id=1, source_target_pairs={{0,1},{1,0},{2,3},{3,2},{4,5},{5,4},{6,7},{7,6},{8,9},{9,8},{10,11... | collective-permute-start | bytes 786440 | tf_op jit(solution)/shard_map/ppermute | solution.py:394
  137.6 25.8 %collective-permute-start.32 = (bf16[2,256,256]{2,1,0:T(8,128)(2,1)S(1)}, bf16[2,256,256]{2,1,0:T(8,128)(2,1)S(1)}, u32[]{:S(2)}, u32[]{:S(2)}) collective-permute-start(bf16[2,256,256]{2,1,0:T(8,128)(2,1)S(1)} %get-tuple-element.259), channel_id=1, source_target_pairs={{0,1},{1,0},{2,3},{3,2},{4,5},{5,4},{6,7},{7,6},{8,9},{9,8},{10,11... | collective-permute-start | bytes 786440 | tf_op jit(solution)/shard_map/ppermute | solution.py:394
  168.0 19.8 %collective-permute-start.37 = (f32[1,4,128,256]{3,2,1,0:T(8,128)S(1)}, f32[1,4,128,256]{3,2,1,0:T(8,128)S(1)}, u32[]{:S(2)}, u32[]{:S(2)}) collective-permute-start(f32[1,4,128,256]{3,2,1,0:T(8,128)S(1)} %slice.73), channel_id=1, source_target_pairs={{0,16},{16,0},{1,17},{17,1},{2,18},{18,2},{3,19},{19,3},{4,20},{20... | collective-permute-start | bytes 1572872 | tf_op jit(solution)/shard_map/ppermute | solution.py:407
  170.1 25.2 %collective-permute-start.39 = (bf16[2,128,1024]{2,1,0:T(8,128)(2,1)S(1)}, bf16[2,128,1024]{2,1,0:T(8,128)(2,1)S(1)}, u32[]{:S(2)}, u32[]{:S(2)}) collective-permute-start(bf16[2,128,1024]{2,1,0:T(8,128)(2,1)S(1)} %get-tuple-element.275), channel_id=1, source_target_pairs={{0,8},{4,12},{8,0},{12,4},{1,9},{5,13},{9,1},{13,5},{2,10},{6,14},... | collective-permute-start | bytes 1572872 | tf_op jit(solution)/shard_map/ppermute | solution.py:394
  199.4 25.7 %collective-permute-start.46 = (bf16[1,2,256,256]{3,2,1,0:T(8,128)(2,1)S(1)}, bf16[1,2,256,256]{3,2,1,0:T(8,128)(2,1)S(1)}, u32[]{:S(2)}, u32[]{:S(2)}) collective-permute-start(bf16[1,2,256,256]{3,2,1,0:T(8,128)(2,1)S(1)} %get-tuple-element.279.refs_0_), channel_id=1, source_target_pairs={{0,1},{1,0},{2,3},{3,2},{4,5},{5,4},{6,7},{7,6},{8,9},{9,8},{10,11... | collective-permute-start | bytes 786440 | tf_op jit(solution)/shard_map/ppermute | solution.py:394
  237.4 28.0 %collective-permute-start.58 = (bf16[2,128,1024]{2,1,0:T(8,128)(2,1)S(1)}, bf16[2,128,1024]{2,1,0:T(8,128)(2,1)S(1)}, u32[]{:S(2)}, u32[]{:S(2)}) collective-permute-start(bf16[2,128,1024]{2,1,0:T(8,128)(2,1)S(1)} %get-tuple-element.313), channel_id=1, source_target_pairs={{0,4},{4,0},{8,12},{12,8},{1,5},{5,1},{9,13},{13,9},{2,6},{6,2},{1... | collective-permute-start | bytes 1572872 | tf_op jit(solution)/shard_map/ppermute | solution.py:394
  238.8 28.1 %collective-permute-start.59 = (bf16[2,128,1024]{2,1,0:T(8,128)(2,1)S(1)}, bf16[2,128,1024]{2,1,0:T(8,128)(2,1)S(1)}, u32[]{:S(2)}, u32[]{:S(2)}) collective-permute-start(bf16[2,128,1024]{2,1,0:T(8,128)(2,1)S(1)} %get-tuple-element.314), channel_id=1, source_target_pairs={{0,8},{4,12},{8,0},{12,4},{1,9},{5,13},{9,1},{13,5},{2,10},{6,14},... | collective-permute-start | bytes 1572872 | tf_op jit(solution)/shard_map/ppermute | solution.py:394
  241.7 26.5 %collective-permute-start.60 = (bf16[2,128,1024]{2,1,0:T(8,128)(2,1)S(1)}, bf16[2,128,1024]{2,1,0:T(8,128)(2,1)S(1)}, u32[]{:S(2)}, u32[]{:S(2)}) collective-permute-start(bf16[2,128,1024]{2,1,0:T(8,128)(2,1)S(1)} %get-tuple-element.315), channel_id=1, source_target_pairs={{0,12},{4,8},{8,4},{12,0},{1,13},{5,9},{9,5},{13,1},{2,14},{6,10},... | collective-permute-start | bytes 1572872 | tf_op jit(solution)/shard_map/ppermute | solution.py:394
  282.2 25.4 %collective-permute-start.69 = (bf16[2,128,1024]{2,1,0:T(8,128)(2,1)}, bf16[2,128,1024]{2,1,0:T(8,128)(2,1)S(1)}, u32[]{:S(2)}, u32[]{:S(2)}) collective-permute-start(bf16[2,128,1024]{2,1,0:T(8,128)(2,1)} %get-tuple-element.334), channel_id=1, source_target_pairs={{0,8},{4,12},{8,0},{12,4},{1,9},{5,13},{9,1},{13,5},{2,10},{6,14},... | collective-permute-start | bytes 1572872 | tf_op jit(solution)/shard_map/ppermute | solution.py:394
  283.2 24.4 %collective-permute-start.70 = (bf16[2,128,1024]{2,1,0:T(8,128)(2,1)S(1)}, bf16[2,128,1024]{2,1,0:T(8,128)(2,1)S(1)}, u32[]{:S(2)}, u32[]{:S(2)}) collective-permute-start(bf16[2,128,1024]{2,1,0:T(8,128)(2,1)S(1)} %get-tuple-element.335), channel_id=1, source_target_pairs={{0,12},{4,8},{8,4},{12,0},{1,13},{5,9},{9,5},{13,1},{2,14},{6,10},... | collective-permute-start | bytes 1572872 | tf_op jit(solution)/shard_map/ppermute | solution.py:394
  (55 other events, 643.3 us)

commit v4 on v3

--- a/solution.py
+++ b/solution.py
@@ -669,11 +669,11 @@
     sum_two(0)
     cut(2)
     step(0)
+    rough_two(0)
+    send_grads(2)
     step_two(0)
-    rough_two(0)
+    wait_grads(1)
     rough_near(0)
-    wait_grads(1)
-    send_grads(2)
     low(1)
     sum_far(1)
     sum_near(1)
@@ -683,31 +683,33 @@
     share(0)
     step_near(0)
     step(1)
-    rough_two(1)
-    rough_near(1)
+    rough_across(1)
     wait_grads(2)
     step_far(0)
+    rough_near(1)
     low(2)
     sum_far(2)
     sum_near(2)
-    rough_far(1)
+    rough_across_two(1)
     sum_two(2)
     delta(0)
-    spread(0)
+    send_delta(0)
+    rough_out(1)
+    step(2)
+    rough_out_two(1)
+    rough_two(2)
     subspace(1)
-    share(1)
-    send_delta(0)
-    step(2)
-    rough_two(2)
     rough_near(2)
     rough_far(2)
+    spread(0)
+    share(1)
     subspace(2)
     step_two(1)
-    step_near(1)
-    spread(1)
     put(0)
     share(2)
     step_far(1)
+    spread(1)
+    step_near(1)
     step_two(2)
     step_near(2)
     spread(2)

time: 310 us -> 286 us (0.923)
  waiting for transfers between devices: 192 us -> 162 us
  starting transfers between devices: 68.7 us -> 75.6 us
    ppermute x65 -> x63, waiting for transfers between devices: 192 us -> 152 us  [swap(): return lax.ppermute(x, axis, [(i, i ^ m) for i in range(shape[axis])])]
    ppermute x0 -> x4, waiting for transfers between devices: none -> 9.85 us  [hop(): return lax.ppermute(after(x, *token), 'section', pairs)]
    ppermute x0 -> x4, starting transfers between devices: none -> 4.07 us  [hop(): return lax.ppermute(after(x, *token), 'section', pairs)]
    ppermute x65 -> x63, starting transfers between devices: 68 us -> 70.8 us  [swap(): return lax.ppermute(x, axis, [(i, i ^ m) for i in range(shape[axis])])]
  transfers between devices with their start and end apart: 72 -> 74, of which waited for: 38 -> 38; matrix products, arithmetic and copies ran while one was open for 1% -> 1% of each run, Pallas kernels for 9% -> 11%
where the time goes in v4:
time: 286 us
  waiting for transfers between devices  162 us (57%)
  starting transfers between devices  75.6 us (26%)
  Pallas kernels  41.8 us (15%)
  local copies, waits for them, and re-layouts  4.74 us (2%)
    ppermute x63, waiting for transfers between devices, swap(): return lax.ppermute(x, axis, [(i, i ^ m) for i in range(shape[axis])])  152 us
    ppermute x63, starting transfers between devices, swap(): return lax.ppermute(x, axis, [(i, i ^ m) for i in range(shape[axis])])  70.8 us
    pallas_call x20, Pallas kernels, call(): pl.pallas_call(body, grid_spec=pltpu.PrefetchScalarGridSpec(num_scalar_pr...  41.8 us
    ppermute x4, waiting for transfers between devices, hop(): return lax.ppermute(after(x, *token), 'section', pairs)  9.85 us
  transfers between devices with their start and end apart: 74, of which 38 were waited for; matrix products, arithmetic and copies ran while one was open for 1% of the time, Pallas kernels for 11%

profile of v4, /device:TPU:0, one launch (start us, length us, event | category | flops | bytes accessed | tf_op | source)
XLA Modules:
  0.0 285.9 jit_solution(14199564758811687393)
XLA Ops:
  10.3 4.8 %collective-permute-done.1.refs_7_ = bf16[3,128,256]{2,1,0:T(8,128)(2,1)S(1)} collective-permute-done((bf16[3,128,256]{2,1,0:T(8,128)(2,1)S(1)}, bf16[3,128,256]{2,1,0:T(8,128)(2,1)S(1)}, u32[]{:S(2)}, u32[]{:S(2)}) %collective-permute-start.1) | collective-permute-done | bytes 196640 | tf_op jit(solution)/shard_map/ppermute | solution.py:394
  19.2 11.1 %collective-permute-done.3.refs_1_ = bf16[2,128,1024]{2,1,0:T(8,128)(2,1)S(1)} collective-permute-done((bf16[2,128,1024]{2,1,0:T(8,128)(2,1)}, bf16[2,128,1024]{2,1,0:T(8,128)(2,1)S(1)}, u32[]{:S(2)}, u32[]{:S(2)}) %collective-permute-start.3) | collective-permute-done | bytes 524320 | tf_op jit(solution)/shard_map/ppermute | solution.py:394
  33.9 6.5 %collective-permute-done.4.refs_2_ = bf16[2,128,1024]{2,1,0:T(8,128)(2,1)S(1)} collective-permute-done((bf16[2,128,1024]{2,1,0:T(8,128)(2,1)}, bf16[2,128,1024]{2,1,0:T(8,128)(2,1)S(1)}, u32[]{:S(2)}, u32[]{:S(2)}) %collective-permute-start.4) | collective-permute-done | bytes 524320 | tf_op jit(solution)/shard_map/ppermute | solution.py:394
  48.2 6.0 %collective-permute-done.9 = bf16[2,256,256]{2,1,0:T(8,128)(2,1)S(1)} collective-permute-done((bf16[2,256,256]{2,1,0:T(8,128)(2,1)S(1)}, bf16[2,256,256]{2,1,0:T(8,128)(2,1)S(1)}, u32[]{:S(2)}, u32[]{:S(2)}) %collective-permute-start.9) | collective-permute-done | bytes 262176 | tf_op jit(solution)/shard_map/ppermute | solution.py:394
  57.1 12.9 %collective-permute-done.11.refs_2_ = bf16[2,256,256]{2,1,0:T(8,128)(2,1)S(1)} collective-permute-done((bf16[2,256,256]{2,1,0:T(8,128)(2,1)S(1)}, bf16[2,256,256]{2,1,0:T(8,128)(2,1)S(1)}, u32[]{:S(2)}, u32[]{:S(2)}) %collective-permute-start.11) | collective-permute-done | bytes 262176 | tf_op jit(solution)/shard_map/ppermute | solution.py:394
  82.3 3.2 %collective-permute-done.16 = bf16[2,256,256]{2,1,0:T(8,128)(2,1)S(1)} collective-permute-done((bf16[2,256,256]{2,1,0:T(8,128)(2,1)S(1)}, bf16[2,256,256]{2,1,0:T(8,128)(2,1)S(1)}, u32[]{:S(2)}, u32[]{:S(2)}) %collective-permute-start.16) | collective-permute-done | bytes 262176 | tf_op jit(solution)/shard_map/ppermute | solution.py:394
  86.7 5.9 %collective-permute-done.17.refs_5_ = bf16[1,2,256,256]{3,2,1,0:T(8,128)(2,1)S(1)} collective-permute-done((bf16[1,2,256,256]{3,2,1,0:T(8,128)(2,1)S(1)}, bf16[1,2,256,256]{3,2,1,0:T(8,128)(2,1)S(1)}, u32[]{:S(2)}, u32[]{:S(2)}) %collective-permute-start.17) | collective-permute-done | bytes 262176 | tf_op jit(solution)/shard_map/ppermute | solution.py:394
  97.6 4.0 %collective-permute-done.18.refs_7_ = bf16[1,2,256,256]{3,2,1,0:T(8,128)(2,1)S(1)} collective-permute-done((bf16[1,2,256,256]{3,2,1,0:T(8,128)(2,1)S(1)}, bf16[1,2,256,256]{3,2,1,0:T(8,128)(2,1)S(1)}, u32[]{:S(2)}, u32[]{:S(2)}) %collective-permute-start.18) | collective-permute-done | bytes 262176 | tf_op jit(solution)/shard_map/ppermute | solution.py:394
  103.3 3.7 %collective-permute-done.20.refs_2_ = bf16[2,256,256]{2,1,0:T(8,128)(2,1)S(1)} collective-permute-done((bf16[2,256,256]{2,1,0:T(8,128)(2,1)S(1)}, bf16[2,256,256]{2,1,0:T(8,128)(2,1)S(1)}, u32[]{:S(2)}, u32[]{:S(2)}) %collective-permute-start.20) | collective-permute-done | bytes 262176 | tf_op jit(solution)/shard_map/ppermute | solution.py:394
  108.9 5.1 %collective-permute-done.24.refs_2_ = bf16[1,2,256,256]{3,2,1,0:T(8,128)(2,1)S(1)} collective-permute-done((bf16[1,2,256,256]{3,2,1,0:T(8,128)(2,1)S(1)}, bf16[1,2,256,256]{3,2,1,0:T(8,128)(2,1)S(1)}, u32[]{:S(2)}, u32[]{:S(2)}) %collective-permute-start.24) | collective-permute-done | bytes 262176 | tf_op jit(solution)/shard_map/ppermute | solution.py:394
  119.0 6.9 %collective-permute-done.25.refs_5_ = bf16[1,2,256,256]{3,2,1,0:T(8,128)(2,1)S(1)} collective-permute-done((bf16[1,2,256,256]{3,2,1,0:T(8,128)(2,1)S(1)}, bf16[1,2,256,256]{3,2,1,0:T(8,128)(2,1)S(1)}, u32[]{:S(2)}, u32[]{:S(2)}) %collective-permute-start.25) | collective-permute-done | bytes 262176 | tf_op jit(solution)/shard_map/ppermute | solution.py:394
  134.7 4.7 %collective-permute-done.27.refs_1_ = bf16[1,2,256,256]{3,2,1,0:T(8,128)(2,1)S(1)} collective-permute-done((bf16[1,2,256,256]{3,2,1,0:T(8,128)(2,1)S(1)}, bf16[1,2,256,256]{3,2,1,0:T(8,128)(2,1)S(1)}, u32[]{:S(2)}, u32[]{:S(2)}) %collective-permute-start.27) | collective-permute-done | bytes 262176 | tf_op jit(solution)/shard_map/ppermute | solution.py:394
  143.1 3.7 %collective-permute-done.30.refs_1_ = bf16[2,256,256]{2,1,0:T(8,128)(2,1)S(1)} collective-permute-done((bf16[2,256,256]{2,1,0:T(8,128)(2,1)S(1)}, bf16[2,256,256]{2,1,0:T(8,128)(2,1)S(1)}, u32[]{:S(2)}, u32[]{:S(2)}) %collective-permute-start.30) | collective-permute-done | bytes 262176 | tf_op jit(solution)/shard_map/ppermute | solution.py:394
  149.1 3.9 %collective-permute-done.33.refs_7_ = bf16[1,2,256,256]{3,2,1,0:T(8,128)(2,1)S(1)} collective-permute-done((bf16[1,2,256,256]{3,2,1,0:T(8,128)(2,1)S(1)}, bf16[1,2,256,256]{3,2,1,0:T(8,128)(2,1)S(1)}, u32[]{:S(2)}, u32[]{:S(2)}) %collective-permute-start.33) | collective-permute-done | bytes 262176 | tf_op jit(solution)/shard_map/ppermute | solution.py:473
  153.0 5.9 %collective-permute-done.34.refs_9_ = bf16[1,2,256,256]{3,2,1,0:T(8,128)(2,1)S(1)} collective-permute-done((bf16[1,2,256,256]{3,2,1,0:T(8,128)(2,1)S(1)}, bf16[1,2,256,256]{3,2,1,0:T(8,128)(2,1)S(1)}, u32[]{:S(2)}, u32[]{:S(2)}) %collective-permute-start.34) | collective-permute-done | bytes 262176 | tf_op jit(solution)/shard_map/ppermute | solution.py:473
  175.5 5.7 %collective-permute-done.40.refs_2_ = bf16[2,128,1024]{2,1,0:T(8,128)(2,1)S(1)} collective-permute-done((bf16[2,128,1024]{2,1,0:T(8,128)(2,1)S(1)}, bf16[2,128,1024]{2,1,0:T(8,128)(2,1)S(1)}, u32[]{:S(2)}, u32[]{:S(2)}) %collective-permute-start.40) | collective-permute-done | bytes 524320 | tf_op jit(solution)/shard_map/ppermute | solution.py:394
  193.1 3.4 %collective-permute-done.46.refs_6_ = f32[1,128,256]{2,1,0:T(8,128)S(1)} collective-permute-done((f32[1,128,256]{2,1,0:T(8,128)S(1)}, f32[1,128,256]{2,1,0:T(8,128)S(1)}, u32[]{:S(2)}, u32[]{:S(2)}) %collective-permute-start.46) | collective-permute-done | bytes 131104 | tf_op jit(solution)/shard_map/ppermute | solution.py:394
  196.6 3.8 %collective-permute-start.52 = (f32[1,128,256]{2,1,0:T(8,128)S(1)}, f32[1,128,256]{2,1,0:T(8,128)S(1)}, u32[]{:S(2)}, u32[]{:S(2)}) collective-permute-start(f32[1,128,256]{2,1,0:T(8,128)S(1)} %get-tuple-element.312), channel_id=1, source_target_pairs={{0,12},{4,8},{8,4},{12,0},{1,13},{5,9},{9,5},{13,1},{2,14},{6,10},... | collective-permute-start | bytes 393224 | tf_op jit(solution)/shard_map/ppermute | solution.py:394
  219.6 3.3 %collective-permute-done.58 = f32[3,64,256]{2,1,0:T(8,128)S(1)} collective-permute-done((f32[3,64,256]{2,1,0:T(8,128)S(1)}, f32[3,64,256]{2,1,0:T(8,128)S(1)}, u32[]{:S(2)}, u32[]{:S(2)}) %collective-permute-start.58) | collective-permute-done | bytes 196640 | tf_op jit(solution)/shard_map/ppermute | solution.py:394
  223.7 8.8 %collective-permute-done.65 = f32[3,64,256]{2,1,0:T(8,128)S(1)} collective-permute-done((f32[3,64,256]{2,1,0:T(8,128)S(1)}, f32[3,64,256]{2,1,0:T(8,128)S(1)}, u32[]{:S(2)}, u32[]{:S(2)}) %collective-permute-start.65) | collective-permute-done | bytes 196640 | tf_op jit(solution)/shard_map/ppermute | solution.py:394
  235.8 5.3 %collective-permute-done.66 = f32[3,64,256]{2,1,0:T(8,128)S(1)} collective-permute-done((f32[3,64,256]{2,1,0:T(8,128)S(1)}, f32[3,64,256]{2,1,0:T(8,128)S(1)}, u32[]{:S(2)}, u32[]{:S(2)}) %collective-permute-start.66) | collective-permute-done | bytes 196640 | tf_op jit(solution)/shard_map/ppermute | solution.py:394
  252.7 5.1 %shard_map.93 = bf16[3,128,256]{2,1,0:T(8,128)(2,1)S(1)} custom-call(s32[3]{0:T(128)S(1)} %copy-done.4, f32[3,64,256]{2,1,0:T(8,128)S(1)} %add.47.refs_0_, f32[3,64,256]{2,1,0:T(8,128)S(1)} %collective-permute-done.67.refs_1_, f32[3,64,256]{2,1,0:T(8,128)S(1)} %collective-permute-done.68.refs_2_, f32[3,64,256]{2,1,0:T(8,128)S(1)} %collective-permute-done.69.refs_3_, ...), custom_call_target="tpu_custom_call" | custom-call | flops 1 | bytes 1 | tf_op jit(solution)/shard_map/pallas_call | solution.py:51
  262.3 10.6 %collective-permute-done.70.refs_1_ = bf16[2,128,1024]{2,1,0:T(8,128)(2,1)S(1)} collective-permute-done((bf16[2,128,1024]{2,1,0:T(8,128)(2,1)}, bf16[2,128,1024]{2,1,0:T(8,128)(2,1)S(1)}, u32[]{:S(2)}, u32[]{:S(2)}) %collective-permute-start.70) | collective-permute-done | bytes 524320 | tf_op jit(solution)/shard_map/ppermute | solution.py:394
  272.9 11.1 %collective-permute-done.71.refs_2_ = bf16[2,128,1024]{2,1,0:T(8,128)(2,1)S(1)} collective-permute-done((bf16[2,128,1024]{2,1,0:T(8,128)(2,1)}, bf16[2,128,1024]{2,1,0:T(8,128)(2,1)S(1)}, u32[]{:S(2)}, u32[]{:S(2)}) %collective-permute-start.71) | collective-permute-done | bytes 524320 | tf_op jit(solution)/shard_map/ppermute | solution.py:394
  (179 shorter events, 139.4 us)
Async XLA Ops:
  16.4 24.0 %collective-permute-start.4 = (bf16[2,128,1024]{2,1,0:T(8,128)(2,1)}, bf16[2,128,1024]{2,1,0:T(8,128)(2,1)S(1)}, u32[]{:S(2)}, u32[]{:S(2)}) collective-permute-start(bf16[2,128,1024]{2,1,0:T(8,128)(2,1)} %get-tuple-element.192), channel_id=1, source_target_pairs={{0,8},{4,12},{8,0},{12,4},{1,9},{5,13},{9,1},{13,5},{2,10},{6,14},... | collective-permute-start | bytes 1572872 | tf_op jit(solution)/shard_map/ppermute | solution.py:394
  17.2 23.1 %collective-permute-start.5 = (bf16[2,128,1024]{2,1,0:T(8,128)(2,1)}, bf16[2,128,1024]{2,1,0:T(8,128)(2,1)S(1)}, u32[]{:S(2)}, u32[]{:S(2)}) collective-permute-start(bf16[2,128,1024]{2,1,0:T(8,128)(2,1)} %get-tuple-element.193), channel_id=1, source_target_pairs={{0,12},{4,8},{8,4},{12,0},{1,13},{5,9},{9,5},{13,1},{2,14},{6,10},... | collective-permute-start | bytes 1572872 | tf_op jit(solution)/shard_map/ppermute | solution.py:394
  18.7 21.7 %collective-permute-start.6 = (bf16[3,128,256]{2,1,0:T(8,128)(2,1)S(1)}, bf16[3,128,256]{2,1,0:T(8,128)(2,1)S(1)}, u32[]{:S(2)}, u32[]{:S(2)}) collective-permute-start(bf16[3,128,256]{2,1,0:T(8,128)(2,1)S(1)} %collective-permute-done.refs_5_), channel_id=1, source_target_pairs={{0,16},{16,0},{1,17},{17,1},{2,18},{18,2},{3,19},{19,3},{4,20},{20... | collective-permute-start | bytes 589832 | tf_op jit(solution)/shard_map/ppermute | solution.py:407
  18.7 21.7 %collective-permute-start.7 = (bf16[3,128,256]{2,1,0:T(8,128)(2,1)S(1)}, bf16[3,128,256]{2,1,0:T(8,128)(2,1)S(1)}, u32[]{:S(2)}, u32[]{:S(2)}) collective-permute-start(bf16[3,128,256]{2,1,0:T(8,128)(2,1)S(1)} %collective-permute-done.1.refs_7_), channel_id=1, source_target_pairs={{0,16},{16,0},{1,17},{17,1},{2,18},{18,2},{3,19},{19,3},{4,20},{20... | collective-permute-start | bytes 589832 | tf_op jit(solution)/shard_map/ppermute | solution.py:407
  44.3 27.5 %collective-permute-start.12 = (bf16[2,128,1024]{2,1,0:T(8,128)(2,1)S(1)}, bf16[2,128,1024]{2,1,0:T(8,128)(2,1)S(1)}, u32[]{:S(2)}, u32[]{:S(2)}) collective-permute-start(bf16[2,128,1024]{2,1,0:T(8,128)(2,1)S(1)} %get-tuple-element.215), channel_id=1, source_target_pairs={{0,4},{4,0},{8,12},{12,8},{1,5},{5,1},{9,13},{13,9},{2,6},{6,2},{1... | collective-permute-start | bytes 1572872 | tf_op jit(solution)/shard_map/ppermute | solution.py:394
  44.9 26.9 %collective-permute-start.13 = (bf16[2,128,1024]{2,1,0:T(8,128)(2,1)S(1)}, bf16[2,128,1024]{2,1,0:T(8,128)(2,1)S(1)}, u32[]{:S(2)}, u32[]{:S(2)}) collective-permute-start(bf16[2,128,1024]{2,1,0:T(8,128)(2,1)S(1)} %get-tuple-element.216), channel_id=1, source_target_pairs={{0,8},{4,12},{8,0},{12,4},{1,9},{5,13},{9,1},{13,5},{2,10},{6,14},... | collective-permute-start | bytes 1572872 | tf_op jit(solution)/shard_map/ppermute | solution.py:394
  46.0 25.8 %collective-permute-start.14 = (bf16[2,128,1024]{2,1,0:T(8,128)(2,1)S(1)}, bf16[2,128,1024]{2,1,0:T(8,128)(2,1)S(1)}, u32[]{:S(2)}, u32[]{:S(2)}) collective-permute-start(bf16[2,128,1024]{2,1,0:T(8,128)(2,1)S(1)} %get-tuple-element.217), channel_id=1, source_target_pairs={{0,12},{4,8},{8,4},{12,0},{1,13},{5,9},{9,5},{13,1},{2,14},{6,10},... | collective-permute-start | bytes 1572872 | tf_op jit(solution)/shard_map/ppermute | solution.py:394
  76.5 19.6 %collective-permute-start.19 = (bf16[2,256,256]{2,1,0:T(8,128)(2,1)S(1)}, bf16[2,256,256]{2,1,0:T(8,128)(2,1)S(1)}, u32[]{:S(2)}, u32[]{:S(2)}) collective-permute-start(bf16[2,256,256]{2,1,0:T(8,128)(2,1)S(1)} %get-tuple-element.232), channel_id=1, source_target_pairs={{0,1},{1,0},{2,3},{3,2},{4,5},{5,4},{6,7},{7,6},{8,9},{9,8},{10,11... | collective-permute-start | bytes 786440 | tf_op jit(solution)/shard_map/ppermute | solution.py:394
  81.4 20.3 %collective-permute-start.18 = (bf16[1,2,256,256]{3,2,1,0:T(8,128)(2,1)S(1)}, bf16[1,2,256,256]{3,2,1,0:T(8,128)(2,1)S(1)}, u32[]{:S(2)}, u32[]{:S(2)}) collective-permute-start(bf16[1,2,256,256]{3,2,1,0:T(8,128)(2,1)S(1)} %collective-permute-done.15.refs_6_), channel_id=1, source_target_pairs={{0,1},{1,0},{2,3},{3,2},{4,5},{5,4},{6,7},{7,6},{8,9},{9,8},{10,11... | collective-permute-start | bytes 786440 | tf_op jit(solution)/shard_map/ppermute | solution.py:394
  81.4 33.0 %collective-permute-start.21 = (bf16[2,128,1024]{2,1,0:T(8,128)(2,1)S(1)}, bf16[2,128,1024]{2,1,0:T(8,128)(2,1)S(1)}, u32[]{:S(2)}, u32[]{:S(2)}) collective-permute-start(bf16[2,128,1024]{2,1,0:T(8,128)(2,1)S(1)} %get-tuple-element.240), channel_id=1, source_target_pairs={{0,4},{4,0},{8,12},{12,8},{1,5},{5,1},{9,13},{13,9},{2,6},{6,2},{1... | collective-permute-start | bytes 1572872 | tf_op jit(solution)/shard_map/ppermute | solution.py:394
  85.6 28.8 %collective-permute-start.22 = (bf16[2,128,1024]{2,1,0:T(8,128)(2,1)S(1)}, bf16[2,128,1024]{2,1,0:T(8,128)(2,1)S(1)}, u32[]{:S(2)}, u32[]{:S(2)}) collective-permute-start(bf16[2,128,1024]{2,1,0:T(8,128)(2,1)S(1)} %get-tuple-element.241), channel_id=1, source_target_pairs={{0,8},{4,12},{8,0},{12,4},{1,9},{5,13},{9,1},{13,5},{2,10},{6,14},... | collective-permute-start | bytes 1572872 | tf_op jit(solution)/shard_map/ppermute | solution.py:394
  92.6 21.8 %collective-permute-start.23 = (bf16[2,128,1024]{2,1,0:T(8,128)(2,1)S(1)}, bf16[2,128,1024]{2,1,0:T(8,128)(2,1)S(1)}, u32[]{:S(2)}, u32[]{:S(2)}) collective-permute-start(bf16[2,128,1024]{2,1,0:T(8,128)(2,1)S(1)} %get-tuple-element.242), channel_id=1, source_target_pairs={{0,12},{4,8},{8,4},{12,0},{1,13},{5,9},{9,5},{13,1},{2,14},{6,10},... | collective-permute-start | bytes 1572872 | tf_op jit(solution)/shard_map/ppermute | solution.py:394
  130.1 16.8 %collective-permute-start.30 = (bf16[2,256,256]{2,1,0:T(8,128)(2,1)S(1)}, bf16[2,256,256]{2,1,0:T(8,128)(2,1)S(1)}, u32[]{:S(2)}, u32[]{:S(2)}) collective-permute-start(bf16[2,256,256]{2,1,0:T(8,128)(2,1)S(1)} %get-tuple-element.265), channel_id=1, source_target_pairs={{0,1},{1,0},{2,3},{3,2},{4,5},{5,4},{6,7},{7,6},{8,9},{9,8},{10,11... | collective-permute-start | bytes 786440 | tf_op jit(solution)/shard_map/ppermute | solution.py:394
  133.2 32.0 %collective-permute-start.36 = (f32[1,4,128,256]{3,2,1,0:T(8,128)S(1)}, f32[1,4,128,256]{3,2,1,0:T(8,128)S(1)}, u32[]{:S(2)}, u32[]{:S(2)}) collective-permute-start(f32[1,4,128,256]{3,2,1,0:T(8,128)S(1)} %slice.72), channel_id=1, source_target_pairs={{0,16},{16,0},{1,17},{17,1},{2,18},{18,2},{3,19},{19,3},{4,20},{20... | collective-permute-start | bytes 1572872 | tf_op jit(solution)/shard_map/ppermute | solution.py:407
  133.4 19.7 %collective-permute-start.33 = (bf16[1,2,256,256]{3,2,1,0:T(8,128)(2,1)S(1)}, bf16[1,2,256,256]{3,2,1,0:T(8,128)(2,1)S(1)}, u32[]{:S(2)}, u32[]{:S(2)}) collective-permute-start(bf16[1,2,256,256]{3,2,1,0:T(8,128)(2,1)S(1)} %collective-permute-done.29.refs_8_), channel_id=1, source_target_pairs={{1,0},{2,3},{5,4},{6,7},{9,8},{10,11},{13,12},{14,15},{17,16},{18,... | collective-permute-start | bytes 786440 | tf_op jit(solution)/shard_map/ppermute | solution.py:473
  139.3 19.6 %collective-permute-start.34 = (bf16[1,2,256,256]{3,2,1,0:T(8,128)(2,1)S(1)}, bf16[1,2,256,256]{3,2,1,0:T(8,128)(2,1)S(1)}, u32[]{:S(2)}, u32[]{:S(2)}) collective-permute-start(bf16[1,2,256,256]{3,2,1,0:T(8,128)(2,1)S(1)} %collective-permute-done.32.refs_6_), channel_id=1, source_target_pairs={{1,0},{2,3},{5,4},{6,7},{9,8},{10,11},{13,12},{14,15},{17,16},{18,... | collective-permute-start | bytes 786440 | tf_op jit(solution)/shard_map/ppermute | solution.py:473
  163.6 17.5 %collective-permute-start.40 = (bf16[2,128,1024]{2,1,0:T(8,128)(2,1)S(1)}, bf16[2,128,1024]{2,1,0:T(8,128)(2,1)S(1)}, u32[]{:S(2)}, u32[]{:S(2)}) collective-permute-start(bf16[2,128,1024]{2,1,0:T(8,128)(2,1)S(1)} %get-tuple-element.288), channel_id=1, source_target_pairs={{0,8},{4,12},{8,0},{12,4},{1,9},{5,13},{9,1},{13,5},{2,10},{6,14},... | collective-permute-start | bytes 1572872 | tf_op jit(solution)/shard_map/ppermute | solution.py:394
  167.1 18.6 %collective-permute-start.43 = (f32[1,4,128,256]{3,2,1,0:T(8,128)S(1)}, f32[1,4,128,256]{3,2,1,0:T(8,128)S(1)}, u32[]{:S(2)}, u32[]{:S(2)}) collective-permute-start(f32[1,4,128,256]{3,2,1,0:T(8,128)S(1)} %slice.73), channel_id=1, source_target_pairs={{0,16},{16,0},{1,17},{17,1},{2,18},{18,2},{3,19},{19,3},{4,20},{20... | collective-permute-start | bytes 1572872 | tf_op jit(solution)/shard_map/ppermute | solution.py:407
  214.1 27.1 %collective-permute-start.60 = (bf16[2,128,1024]{2,1,0:T(8,128)(2,1)S(1)}, bf16[2,128,1024]{2,1,0:T(8,128)(2,1)S(1)}, u32[]{:S(2)}, u32[]{:S(2)}) collective-permute-start(bf16[2,128,1024]{2,1,0:T(8,128)(2,1)S(1)} %get-tuple-element.329), channel_id=1, source_target_pairs={{0,4},{4,0},{8,12},{12,8},{1,5},{5,1},{9,13},{13,9},{2,6},{6,2},{1... | collective-permute-start | bytes 1572872 | tf_op jit(solution)/shard_map/ppermute | solution.py:394
  215.8 26.8 %collective-permute-start.61 = (bf16[2,128,1024]{2,1,0:T(8,128)(2,1)S(1)}, bf16[2,128,1024]{2,1,0:T(8,128)(2,1)S(1)}, u32[]{:S(2)}, u32[]{:S(2)}) collective-permute-start(bf16[2,128,1024]{2,1,0:T(8,128)(2,1)S(1)} %get-tuple-element.330), channel_id=1, source_target_pairs={{0,8},{4,12},{8,0},{12,4},{1,9},{5,13},{9,1},{13,5},{2,10},{6,14},... | collective-permute-start | bytes 1572872 | tf_op jit(solution)/shard_map/ppermute | solution.py:394
  218.3 27.4 %collective-permute-start.62 = (bf16[2,128,1024]{2,1,0:T(8,128)(2,1)S(1)}, bf16[2,128,1024]{2,1,0:T(8,128)(2,1)S(1)}, u32[]{:S(2)}, u32[]{:S(2)}) collective-permute-start(bf16[2,128,1024]{2,1,0:T(8,128)(2,1)S(1)} %get-tuple-element.331), channel_id=1, source_target_pairs={{0,12},{4,8},{8,4},{12,0},{1,13},{5,9},{9,5},{13,1},{2,14},{6,10},... | collective-permute-start | bytes 1572872 | tf_op jit(solution)/shard_map/ppermute | solution.py:394
  233.4 16.4 %collective-permute-start.63 = (bf16[1,2,256,256]{3,2,1,0:T(8,128)(2,1)S(1)}, bf16[1,2,256,256]{3,2,1,0:T(8,128)(2,1)S(1)}, u32[]{:S(2)}, u32[]{:S(2)}) collective-permute-start(bf16[1,2,256,256]{3,2,1,0:T(8,128)(2,1)S(1)} %get-tuple-element.314.refs_0_), channel_id=1, source_target_pairs={{0,1},{1,0},{2,3},{3,2},{4,5},{5,4},{6,7},{7,6},{8,9},{9,8},{10,11... | collective-permute-start | bytes 786440 | tf_op jit(solution)/shard_map/ppermute | solution.py:394
  258.2 25.8 %collective-permute-start.71 = (bf16[2,128,1024]{2,1,0:T(8,128)(2,1)}, bf16[2,128,1024]{2,1,0:T(8,128)(2,1)S(1)}, u32[]{:S(2)}, u32[]{:S(2)}) collective-permute-start(bf16[2,128,1024]{2,1,0:T(8,128)(2,1)} %get-tuple-element.350), channel_id=1, source_target_pairs={{0,8},{4,12},{8,0},{12,4},{1,9},{5,13},{9,1},{13,5},{2,10},{6,14},... | collective-permute-start | bytes 1572872 | tf_op jit(solution)/shard_map/ppermute | solution.py:394
  260.3 23.7 %collective-permute-start.72 = (bf16[2,128,1024]{2,1,0:T(8,128)(2,1)S(1)}, bf16[2,128,1024]{2,1,0:T(8,128)(2,1)S(1)}, u32[]{:S(2)}, u32[]{:S(2)}) collective-permute-start(bf16[2,128,1024]{2,1,0:T(8,128)(2,1)S(1)} %get-tuple-element.351), channel_id=1, source_target_pairs={{0,12},{4,8},{8,4},{12,0},{1,13},{5,9},{9,5},{13,1},{2,14},{6,10},... | collective-permute-start | bytes 1572872 | tf_op jit(solution)/shard_map/ppermute | solution.py:394
  (57 other events, 616.5 us)

commit v5 on v4

--- a/solution.py
+++ b/solution.py
@@ -671,21 +671,21 @@
     step(0)
     rough_two(0)
     send_grads(2)
-    step_two(0)
     wait_grads(1)
     rough_near(0)
     low(1)
+    step_two(0)
     sum_far(1)
+    rough_far(0)
     sum_near(1)
-    rough_far(0)
     sum_two(1)
     subspace(0)
     share(0)
     step_near(0)
     step(1)
-    rough_across(1)
     wait_grads(2)
     step_far(0)
+    rough_across(1)
     rough_near(1)
     low(2)
     sum_far(2)
@@ -696,39 +696,39 @@
     send_delta(0)
     rough_out(1)
     step(2)
+    step_near(1)
     rough_out_two(1)
     rough_two(2)
-    subspace(1)
-    rough_near(2)
+    step_two(1)
     rough_far(2)
     spread(0)
+    rough_near(2)
+    subspace(1)
     share(1)
     subspace(2)
-    step_two(1)
     put(0)
     share(2)
     step_far(1)
     spread(1)
-    step_near(1)
     step_two(2)
     step_near(2)
     spread(2)
     wait_spread(1)
     delta(1)
+    wait_spread(0)
     send_delta(1)
-    wait_spread(0)
-    step_far(2)
     wait_spread(2)
     gram_kernel()
     gram_send()
+    step_far(2)
     gram_sum()
     gram_hop()
     put(1)
-    delta(2)
     gram_add()
     gram_hop()
     gram_add()
     gram_gather()
+    delta(2)
     newton()
     send_delta(2)
     finish()

time: 286 us -> 284 us (level)
    ppermute x63, waiting for transfers between devices: 152 us -> 156 us  [swap(): return lax.ppermute(x, axis, [(i, i ^ m) for i in range(shape[axis])])]
    ppermute x4, waiting for transfers between devices: 9.85 us -> 5.59 us  [hop(): return lax.ppermute(after(x, *token), 'section', pairs)]
  transfers between devices with their start and end apart: 74 -> 74, of which waited for: 38 -> 39; matrix products, arithmetic and copies ran while one was open for 1% -> 1% of each run, Pallas kernels for 11% -> 10%
where the time goes in v5:
time: 284 us
  waiting for transfers between devices  162 us (57%)
  starting transfers between devices  73.3 us (26%)
  Pallas kernels  41.8 us (15%)
  local copies, waits for them, and re-layouts  4.75 us (2%)
    ppermute x63, waiting for transfers between devices, swap(): return lax.ppermute(x, axis, [(i, i ^ m) for i in range(shape[axis])])  156 us
    ppermute x63, starting transfers between devices, swap(): return lax.ppermute(x, axis, [(i, i ^ m) for i in range(shape[axis])])  68.5 us
    pallas_call x20, Pallas kernels, call(): pl.pallas_call(body, grid_spec=pltpu.PrefetchScalarGridSpec(num_scalar_pr...  41.8 us
  transfers between devices with their start and end apart: 74, of which 39 were waited for; matrix products, arithmetic and copies ran while one was open for 1% of the time, Pallas kernels for 10%

profile of v5, /device:TPU:0, one launch (start us, length us, event | category | flops | bytes accessed | tf_op | source)
XLA Modules:
  0.0 284.0 jit_solution(4735424361744064695)
XLA Ops:
  6.7 3.1 %shard_map.75 = (bf16[2,128,1024]{2,1,0:T(8,128)(2,1)}, bf16[2,128,1024]{2,1,0:T(8,128)(2,1)}, bf16[2,128,1024]{2,1,0:T(8,128)(2,1)}) custom-call(s32[3]{0:T(128)} %pad_add_fusion.place_ref, bf16[6,128,4096]{2,1,0:T(8,128)(2,1)} %refs_0_.17, bf16[6,128,4096]{2,1,0:T(8,128)(2,1)} %refs_0_.17, bf16[6,128,4096]{2,1,0:T(8,128)(2,1)} %refs_0_.17), custom_call_target="tpu_custom_call" | custom-call | flops 1 | bytes 1 | tf_op jit(solution)/shard_map/pallas_call | solution.py:51
  10.3 4.8 %collective-permute-done.1.refs_7_ = bf16[3,128,256]{2,1,0:T(8,128)(2,1)S(1)} collective-permute-done((bf16[3,128,256]{2,1,0:T(8,128)(2,1)S(1)}, bf16[3,128,256]{2,1,0:T(8,128)(2,1)S(1)}, u32[]{:S(2)}, u32[]{:S(2)}) %collective-permute-start.1) | collective-permute-done | bytes 196640 | tf_op jit(solution)/shard_map/ppermute | solution.py:394
  19.2 11.1 %collective-permute-done.3.refs_1_ = bf16[2,128,1024]{2,1,0:T(8,128)(2,1)S(1)} collective-permute-done((bf16[2,128,1024]{2,1,0:T(8,128)(2,1)}, bf16[2,128,1024]{2,1,0:T(8,128)(2,1)S(1)}, u32[]{:S(2)}, u32[]{:S(2)}) %collective-permute-start.3) | collective-permute-done | bytes 524320 | tf_op jit(solution)/shard_map/ppermute | solution.py:394
  33.9 6.5 %collective-permute-done.4.refs_2_ = bf16[2,128,1024]{2,1,0:T(8,128)(2,1)S(1)} collective-permute-done((bf16[2,128,1024]{2,1,0:T(8,128)(2,1)}, bf16[2,128,1024]{2,1,0:T(8,128)(2,1)S(1)}, u32[]{:S(2)}, u32[]{:S(2)}) %collective-permute-start.4) | collective-permute-done | bytes 524320 | tf_op jit(solution)/shard_map/ppermute | solution.py:394
  48.2 6.0 %collective-permute-done.9 = bf16[2,256,256]{2,1,0:T(8,128)(2,1)S(1)} collective-permute-done((bf16[2,256,256]{2,1,0:T(8,128)(2,1)S(1)}, bf16[2,256,256]{2,1,0:T(8,128)(2,1)S(1)}, u32[]{:S(2)}, u32[]{:S(2)}) %collective-permute-start.9) | collective-permute-done | bytes 262176 | tf_op jit(solution)/shard_map/ppermute | solution.py:394
  57.1 12.9 %collective-permute-done.11.refs_2_ = bf16[2,256,256]{2,1,0:T(8,128)(2,1)S(1)} collective-permute-done((bf16[2,256,256]{2,1,0:T(8,128)(2,1)S(1)}, bf16[2,256,256]{2,1,0:T(8,128)(2,1)S(1)}, u32[]{:S(2)}, u32[]{:S(2)}) %collective-permute-start.11) | collective-permute-done | bytes 262176 | tf_op jit(solution)/shard_map/ppermute | solution.py:394
  76.5 4.9 %collective-permute-done.15.refs_6_ = bf16[1,2,256,256]{3,2,1,0:T(8,128)(2,1)S(1)} collective-permute-done((bf16[1,2,256,256]{3,2,1,0:T(8,128)(2,1)S(1)}, bf16[1,2,256,256]{3,2,1,0:T(8,128)(2,1)S(1)}, u32[]{:S(2)}, u32[]{:S(2)}) %collective-permute-start.15) | collective-permute-done | bytes 262176 | tf_op jit(solution)/shard_map/ppermute | solution.py:394
  87.1 5.6 %collective-permute-done.17.refs_5_ = bf16[1,2,256,256]{3,2,1,0:T(8,128)(2,1)S(1)} collective-permute-done((bf16[1,2,256,256]{3,2,1,0:T(8,128)(2,1)S(1)}, bf16[1,2,256,256]{3,2,1,0:T(8,128)(2,1)S(1)}, u32[]{:S(2)}, u32[]{:S(2)}) %collective-permute-start.17) | collective-permute-done | bytes 262176 | tf_op jit(solution)/shard_map/ppermute | solution.py:394
  92.7 3.3 %collective-permute-done.18.refs_7_ = bf16[1,2,256,256]{3,2,1,0:T(8,128)(2,1)S(1)} collective-permute-done((bf16[1,2,256,256]{3,2,1,0:T(8,128)(2,1)S(1)}, bf16[1,2,256,256]{3,2,1,0:T(8,128)(2,1)S(1)}, u32[]{:S(2)}, u32[]{:S(2)}) %collective-permute-start.18) | collective-permute-done | bytes 262176 | tf_op jit(solution)/shard_map/ppermute | solution.py:394
  97.6 4.1 %collective-permute-done.19.refs_1_ = bf16[2,256,256]{2,1,0:T(8,128)(2,1)S(1)} collective-permute-done((bf16[2,256,256]{2,1,0:T(8,128)(2,1)S(1)}, bf16[2,256,256]{2,1,0:T(8,128)(2,1)S(1)}, u32[]{:S(2)}, u32[]{:S(2)}) %collective-permute-start.19) | collective-permute-done | bytes 262176 | tf_op jit(solution)/shard_map/ppermute | solution.py:394
  103.4 3.6 %collective-permute-done.20.refs_2_ = bf16[2,256,256]{2,1,0:T(8,128)(2,1)S(1)} collective-permute-done((bf16[2,256,256]{2,1,0:T(8,128)(2,1)S(1)}, bf16[2,256,256]{2,1,0:T(8,128)(2,1)S(1)}, u32[]{:S(2)}, u32[]{:S(2)}) %collective-permute-start.20) | collective-permute-done | bytes 262176 | tf_op jit(solution)/shard_map/ppermute | solution.py:394
  108.8 4.4 %collective-permute-done.24.refs_2_ = bf16[1,2,256,256]{3,2,1,0:T(8,128)(2,1)S(1)} collective-permute-done((bf16[1,2,256,256]{3,2,1,0:T(8,128)(2,1)S(1)}, bf16[1,2,256,256]{3,2,1,0:T(8,128)(2,1)S(1)}, u32[]{:S(2)}, u32[]{:S(2)}) %collective-permute-start.24) | collective-permute-done | bytes 262176 | tf_op jit(solution)/shard_map/ppermute | solution.py:394
  125.8 7.9 %collective-permute-done.25.refs_5_ = bf16[1,2,256,256]{3,2,1,0:T(8,128)(2,1)S(1)} collective-permute-done((bf16[1,2,256,256]{3,2,1,0:T(8,128)(2,1)S(1)}, bf16[1,2,256,256]{3,2,1,0:T(8,128)(2,1)S(1)}, u32[]{:S(2)}, u32[]{:S(2)}) %collective-permute-start.25) | collective-permute-done | bytes 262176 | tf_op jit(solution)/shard_map/ppermute | solution.py:394
  133.7 3.3 %collective-permute-done.27.refs_1_ = bf16[1,2,256,256]{3,2,1,0:T(8,128)(2,1)S(1)} collective-permute-done((bf16[1,2,256,256]{3,2,1,0:T(8,128)(2,1)S(1)}, bf16[1,2,256,256]{3,2,1,0:T(8,128)(2,1)S(1)}, u32[]{:S(2)}, u32[]{:S(2)}) %collective-permute-start.27) | collective-permute-done | bytes 262176 | tf_op jit(solution)/shard_map/ppermute | solution.py:394
  140.5 8.1 %collective-permute-done.31.refs_2_ = bf16[2,256,256]{2,1,0:T(8,128)(2,1)S(1)} collective-permute-done((bf16[2,256,256]{2,1,0:T(8,128)(2,1)S(1)}, bf16[2,256,256]{2,1,0:T(8,128)(2,1)S(1)}, u32[]{:S(2)}, u32[]{:S(2)}) %collective-permute-start.31) | collective-permute-done | bytes 262176 | tf_op jit(solution)/shard_map/ppermute | solution.py:394
  162.0 3.1 %collective-permute-done.35.refs_7_ = bf16[1,2,256,256]{3,2,1,0:T(8,128)(2,1)S(1)} collective-permute-done((bf16[1,2,256,256]{3,2,1,0:T(8,128)(2,1)S(1)}, bf16[1,2,256,256]{3,2,1,0:T(8,128)(2,1)S(1)}, u32[]{:S(2)}, u32[]{:S(2)}) %collective-permute-start.35) | collective-permute-done | bytes 262176 | tf_op jit(solution)/shard_map/ppermute | solution.py:473
  183.2 3.3 %collective-permute-done.42.refs_2_ = bf16[1,2,256,256]{3,2,1,0:T(8,128)(2,1)S(1)} collective-permute-done((bf16[1,2,256,256]{3,2,1,0:T(8,128)(2,1)S(1)}, bf16[1,2,256,256]{3,2,1,0:T(8,128)(2,1)S(1)}, u32[]{:S(2)}, u32[]{:S(2)}) %collective-permute-start.42) | collective-permute-done | bytes 262176 | tf_op jit(solution)/shard_map/ppermute | solution.py:394
  191.5 3.1 %collective-permute-done.49.refs_3_ = bf16[1,2,256,256]{3,2,1,0:T(8,128)(2,1)S(1)} collective-permute-done((bf16[1,2,256,256]{3,2,1,0:T(8,128)(2,1)S(1)}, bf16[1,2,256,256]{3,2,1,0:T(8,128)(2,1)S(1)}, u32[]{:S(2)}, u32[]{:S(2)}) %collective-permute-start.49) | collective-permute-done | bytes 262176 | tf_op jit(solution)/shard_map/ppermute | solution.py:394
  217.3 3.2 %collective-permute-done.58 = f32[3,64,256]{2,1,0:T(8,128)S(1)} collective-permute-done((f32[3,64,256]{2,1,0:T(8,128)S(1)}, f32[3,64,256]{2,1,0:T(8,128)S(1)}, u32[]{:S(2)}, u32[]{:S(2)}) %collective-permute-start.58) | collective-permute-done | bytes 196640 | tf_op jit(solution)/shard_map/ppermute | solution.py:394
  223.0 4.8 %collective-permute-done.63 = f32[3,64,256]{2,1,0:T(8,128)S(1)} collective-permute-done((f32[3,64,256]{2,1,0:T(8,128)S(1)}, f32[3,64,256]{2,1,0:T(8,128)S(1)}, u32[]{:S(2)}, u32[]{:S(2)}) %collective-permute-start.63) | collective-permute-done | bytes 196640 | tf_op jit(solution)/shard_map/ppermute | solution.py:394
  229.6 7.7 %collective-permute-done.56.refs_2_ = bf16[1,2,256,256]{3,2,1,0:T(8,128)(2,1)S(1)} collective-permute-done((bf16[1,2,256,256]{3,2,1,0:T(8,128)(2,1)S(1)}, bf16[1,2,256,256]{3,2,1,0:T(8,128)(2,1)S(1)}, u32[]{:S(2)}, u32[]{:S(2)}) %collective-permute-start.56) | collective-permute-done | bytes 262176 | tf_op jit(solution)/shard_map/ppermute | solution.py:394
  251.0 5.1 %shard_map.93 = bf16[3,128,256]{2,1,0:T(8,128)(2,1)S(1)} custom-call(s32[3]{0:T(128)S(1)} %copy-done.4, f32[3,64,256]{2,1,0:T(8,128)S(1)} %add.47.refs_0_, f32[3,64,256]{2,1,0:T(8,128)S(1)} %collective-permute-done.67.refs_1_, f32[3,64,256]{2,1,0:T(8,128)S(1)} %collective-permute-done.68.refs_2_, f32[3,64,256]{2,1,0:T(8,128)S(1)} %collective-permute-done.69.refs_3_, ...), custom_call_target="tpu_custom_call" | custom-call | flops 1 | bytes 1 | tf_op jit(solution)/shard_map/pallas_call | solution.py:51
  260.7 10.6 %collective-permute-done.70.refs_1_ = bf16[2,128,1024]{2,1,0:T(8,128)(2,1)S(1)} collective-permute-done((bf16[2,128,1024]{2,1,0:T(8,128)(2,1)}, bf16[2,128,1024]{2,1,0:T(8,128)(2,1)S(1)}, u32[]{:S(2)}, u32[]{:S(2)}) %collective-permute-start.70) | collective-permute-done | bytes 524320 | tf_op jit(solution)/shard_map/ppermute | solution.py:394
  271.2 10.8 %collective-permute-done.71.refs_2_ = bf16[2,128,1024]{2,1,0:T(8,128)(2,1)S(1)} collective-permute-done((bf16[2,128,1024]{2,1,0:T(8,128)(2,1)}, bf16[2,128,1024]{2,1,0:T(8,128)(2,1)S(1)}, u32[]{:S(2)}, u32[]{:S(2)}) %collective-permute-start.71) | collective-permute-done | bytes 524320 | tf_op jit(solution)/shard_map/ppermute | solution.py:394
  (179 shorter events, 141.5 us)
Async XLA Ops:
  15.2 15.1 %collective-permute-start.3 = (bf16[2,128,1024]{2,1,0:T(8,128)(2,1)}, bf16[2,128,1024]{2,1,0:T(8,128)(2,1)S(1)}, u32[]{:S(2)}, u32[]{:S(2)}) collective-permute-start(bf16[2,128,1024]{2,1,0:T(8,128)(2,1)} %get-tuple-element.190), channel_id=1, source_target_pairs={{0,4},{4,0},{8,12},{12,8},{1,5},{5,1},{9,13},{13,9},{2,6},{6,2},{1... | collective-permute-start | bytes 1572872 | tf_op jit(solution)/shard_map/ppermute | solution.py:394
  16.4 24.0 %collective-permute-start.4 = (bf16[2,128,1024]{2,1,0:T(8,128)(2,1)}, bf16[2,128,1024]{2,1,0:T(8,128)(2,1)S(1)}, u32[]{:S(2)}, u32[]{:S(2)}) collective-permute-start(bf16[2,128,1024]{2,1,0:T(8,128)(2,1)} %get-tuple-element.191), channel_id=1, source_target_pairs={{0,8},{4,12},{8,0},{12,4},{1,9},{5,13},{9,1},{13,5},{2,10},{6,14},... | collective-permute-start | bytes 1572872 | tf_op jit(solution)/shard_map/ppermute | solution.py:394
  17.2 23.1 %collective-permute-start.5 = (bf16[2,128,1024]{2,1,0:T(8,128)(2,1)}, bf16[2,128,1024]{2,1,0:T(8,128)(2,1)S(1)}, u32[]{:S(2)}, u32[]{:S(2)}) collective-permute-start(bf16[2,128,1024]{2,1,0:T(8,128)(2,1)} %get-tuple-element.192), channel_id=1, source_target_pairs={{0,12},{4,8},{8,4},{12,0},{1,13},{5,9},{9,5},{13,1},{2,14},{6,10},... | collective-permute-start | bytes 1572872 | tf_op jit(solution)/shard_map/ppermute | solution.py:394
  18.7 21.7 %collective-permute-start.6 = (bf16[3,128,256]{2,1,0:T(8,128)(2,1)S(1)}, bf16[3,128,256]{2,1,0:T(8,128)(2,1)S(1)}, u32[]{:S(2)}, u32[]{:S(2)}) collective-permute-start(bf16[3,128,256]{2,1,0:T(8,128)(2,1)S(1)} %collective-permute-done.refs_5_), channel_id=1, source_target_pairs={{0,16},{16,0},{1,17},{17,1},{2,18},{18,2},{3,19},{19,3},{4,20},{20... | collective-permute-start | bytes 589832 | tf_op jit(solution)/shard_map/ppermute | solution.py:407
  18.7 21.7 %collective-permute-start.7 = (bf16[3,128,256]{2,1,0:T(8,128)(2,1)S(1)}, bf16[3,128,256]{2,1,0:T(8,128)(2,1)S(1)}, u32[]{:S(2)}, u32[]{:S(2)}) collective-permute-start(bf16[3,128,256]{2,1,0:T(8,128)(2,1)S(1)} %collective-permute-done.1.refs_7_), channel_id=1, source_target_pairs={{0,16},{16,0},{1,17},{17,1},{2,18},{18,2},{3,19},{19,3},{4,20},{20... | collective-permute-start | bytes 589832 | tf_op jit(solution)/shard_map/ppermute | solution.py:407
  44.3 27.5 %collective-permute-start.12 = (bf16[2,128,1024]{2,1,0:T(8,128)(2,1)S(1)}, bf16[2,128,1024]{2,1,0:T(8,128)(2,1)S(1)}, u32[]{:S(2)}, u32[]{:S(2)}) collective-permute-start(bf16[2,128,1024]{2,1,0:T(8,128)(2,1)S(1)} %get-tuple-element.214), channel_id=1, source_target_pairs={{0,4},{4,0},{8,12},{12,8},{1,5},{5,1},{9,13},{13,9},{2,6},{6,2},{1... | collective-permute-start | bytes 1572872 | tf_op jit(solution)/shard_map/ppermute | solution.py:394
  44.9 26.9 %collective-permute-start.13 = (bf16[2,128,1024]{2,1,0:T(8,128)(2,1)S(1)}, bf16[2,128,1024]{2,1,0:T(8,128)(2,1)S(1)}, u32[]{:S(2)}, u32[]{:S(2)}) collective-permute-start(bf16[2,128,1024]{2,1,0:T(8,128)(2,1)S(1)} %get-tuple-element.215), channel_id=1, source_target_pairs={{0,8},{4,12},{8,0},{12,4},{1,9},{5,13},{9,1},{13,5},{2,10},{6,14},... | collective-permute-start | bytes 1572872 | tf_op jit(solution)/shard_map/ppermute | solution.py:394
  46.0 25.8 %collective-permute-start.14 = (bf16[2,128,1024]{2,1,0:T(8,128)(2,1)S(1)}, bf16[2,128,1024]{2,1,0:T(8,128)(2,1)S(1)}, u32[]{:S(2)}, u32[]{:S(2)}) collective-permute-start(bf16[2,128,1024]{2,1,0:T(8,128)(2,1)S(1)} %get-tuple-element.216), channel_id=1, source_target_pairs={{0,12},{4,8},{8,4},{12,0},{1,13},{5,9},{9,5},{13,1},{2,14},{6,10},... | collective-permute-start | bytes 1572872 | tf_op jit(solution)/shard_map/ppermute | solution.py:394
  54.4 15.6 %collective-permute-start.11 = (bf16[2,256,256]{2,1,0:T(8,128)(2,1)S(1)}, bf16[2,256,256]{2,1,0:T(8,128)(2,1)S(1)}, u32[]{:S(2)}, u32[]{:S(2)}) collective-permute-start(bf16[2,256,256]{2,1,0:T(8,128)(2,1)S(1)} %add_convert_fusion.2), channel_id=1, source_target_pairs={{0,2},{1,3},{2,0},{3,1},{4,6},{5,7},{6,4},{7,5},{8,10},{9,11},{10,... | collective-permute-start | bytes 786440 | tf_op jit(solution)/shard_map/ppermute | solution.py:394
  76.4 16.2 %collective-permute-start.17 = (bf16[1,2,256,256]{3,2,1,0:T(8,128)(2,1)S(1)}, bf16[1,2,256,256]{3,2,1,0:T(8,128)(2,1)S(1)}, u32[]{:S(2)}, u32[]{:S(2)}) collective-permute-start(bf16[1,2,256,256]{3,2,1,0:T(8,128)(2,1)S(1)} %get-tuple-element.227.refs_4_), channel_id=1, source_target_pairs={{0,1},{1,0},{2,3},{3,2},{4,5},{5,4},{6,7},{7,6},{8,9},{9,8},{10,11... | collective-permute-start | bytes 786440 | tf_op jit(solution)/shard_map/ppermute | solution.py:394
  81.4 27.5 %collective-permute-start.21 = (bf16[2,128,1024]{2,1,0:T(8,128)(2,1)S(1)}, bf16[2,128,1024]{2,1,0:T(8,128)(2,1)S(1)}, u32[]{:S(2)}, u32[]{:S(2)}) collective-permute-start(bf16[2,128,1024]{2,1,0:T(8,128)(2,1)S(1)} %get-tuple-element.239), channel_id=1, source_target_pairs={{0,4},{4,0},{8,12},{12,8},{1,5},{5,1},{9,13},{13,9},{2,6},{6,2},{1... | collective-permute-start | bytes 1572872 | tf_op jit(solution)/shard_map/ppermute | solution.py:394
  82.3 26.5 %collective-permute-start.22 = (bf16[2,128,1024]{2,1,0:T(8,128)(2,1)S(1)}, bf16[2,128,1024]{2,1,0:T(8,128)(2,1)S(1)}, u32[]{:S(2)}, u32[]{:S(2)}) collective-permute-start(bf16[2,128,1024]{2,1,0:T(8,128)(2,1)S(1)} %get-tuple-element.240), channel_id=1, source_target_pairs={{0,8},{4,12},{8,0},{12,4},{1,9},{5,13},{9,1},{13,5},{2,10},{6,14},... | collective-permute-start | bytes 1572872 | tf_op jit(solution)/shard_map/ppermute | solution.py:394
  85.6 23.3 %collective-permute-start.23 = (bf16[2,128,1024]{2,1,0:T(8,128)(2,1)S(1)}, bf16[2,128,1024]{2,1,0:T(8,128)(2,1)S(1)}, u32[]{:S(2)}, u32[]{:S(2)}) collective-permute-start(bf16[2,128,1024]{2,1,0:T(8,128)(2,1)S(1)} %get-tuple-element.241), channel_id=1, source_target_pairs={{0,12},{4,8},{8,4},{12,0},{1,13},{5,9},{9,5},{13,1},{2,14},{6,10},... | collective-permute-start | bytes 1572872 | tf_op jit(solution)/shard_map/ppermute | solution.py:394
  117.6 16.0 %collective-permute-start.25 = (bf16[1,2,256,256]{3,2,1,0:T(8,128)(2,1)S(1)}, bf16[1,2,256,256]{3,2,1,0:T(8,128)(2,1)S(1)}, u32[]{:S(2)}, u32[]{:S(2)}) collective-permute-start(bf16[1,2,256,256]{3,2,1,0:T(8,128)(2,1)S(1)} %get-tuple-element.250.refs_4_), channel_id=1, source_target_pairs={{0,1},{1,0},{2,3},{3,2},{4,5},{5,4},{6,7},{7,6},{8,9},{9,8},{10,11... | collective-permute-start | bytes 786440 | tf_op jit(solution)/shard_map/ppermute | solution.py:394
  117.7 19.3 %collective-permute-start.27 = (bf16[1,2,256,256]{3,2,1,0:T(8,128)(2,1)S(1)}, bf16[1,2,256,256]{3,2,1,0:T(8,128)(2,1)S(1)}, u32[]{:S(2)}, u32[]{:S(2)}) collective-permute-start(bf16[1,2,256,256]{3,2,1,0:T(8,128)(2,1)S(1)} %get-tuple-element.254.refs_0_), channel_id=1, source_target_pairs={{0,1},{1,0},{2,3},{3,2},{4,5},{5,4},{6,7},{7,6},{8,9},{9,8},{10,11... | collective-permute-start | bytes 786440 | tf_op jit(solution)/shard_map/ppermute | solution.py:394
  119.7 20.3 %collective-permute-start.29 = (bf16[1,2,256,256]{3,2,1,0:T(8,128)(2,1)S(1)}, bf16[1,2,256,256]{3,2,1,0:T(8,128)(2,1)S(1)}, u32[]{:S(2)}, u32[]{:S(2)}) collective-permute-start(bf16[1,2,256,256]{3,2,1,0:T(8,128)(2,1)S(1)} %get-tuple-element.250.refs_4_), channel_id=1, source_target_pairs={{1,2},{2,1},{5,6},{6,5},{9,10},{10,9},{13,14},{14,13},{17,18},{18,... | collective-permute-start | bytes 786440 | tf_op jit(solution)/shard_map/ppermute | solution.py:473
  123.0 32.7 %collective-permute-start.34 = (f32[1,4,128,256]{3,2,1,0:T(8,128)S(1)}, f32[1,4,128,256]{3,2,1,0:T(8,128)S(1)}, u32[]{:S(2)}, u32[]{:S(2)}) collective-permute-start(f32[1,4,128,256]{3,2,1,0:T(8,128)S(1)} %slice.72), channel_id=1, source_target_pairs={{0,16},{16,0},{1,17},{17,1},{2,18},{18,2},{3,19},{19,3},{4,20},{20... | collective-permute-start | bytes 1572872 | tf_op jit(solution)/shard_map/ppermute | solution.py:407
  155.7 16.4 %collective-permute-start.37 = (bf16[1,2,256,256]{3,2,1,0:T(8,128)(2,1)S(1)}, bf16[1,2,256,256]{3,2,1,0:T(8,128)(2,1)S(1)}, u32[]{:S(2)}, u32[]{:S(2)}) collective-permute-start(bf16[1,2,256,256]{3,2,1,0:T(8,128)(2,1)S(1)} %get-tuple-element.281.refs_4_), channel_id=1, source_target_pairs={{0,1},{1,0},{2,3},{3,2},{4,5},{5,4},{6,7},{7,6},{8,9},{9,8},{10,11... | collective-permute-start | bytes 786440 | tf_op jit(solution)/shard_map/ppermute | solution.py:394
  210.9 28.6 %collective-permute-start.60 = (bf16[2,128,1024]{2,1,0:T(8,128)(2,1)S(1)}, bf16[2,128,1024]{2,1,0:T(8,128)(2,1)S(1)}, u32[]{:S(2)}, u32[]{:S(2)}) collective-permute-start(bf16[2,128,1024]{2,1,0:T(8,128)(2,1)S(1)} %get-tuple-element.327), channel_id=1, source_target_pairs={{0,4},{4,0},{8,12},{12,8},{1,5},{5,1},{9,13},{13,9},{2,6},{6,2},{1... | collective-permute-start | bytes 1572872 | tf_op jit(solution)/shard_map/ppermute | solution.py:394
  212.4 28.2 %collective-permute-start.61 = (bf16[2,128,1024]{2,1,0:T(8,128)(2,1)S(1)}, bf16[2,128,1024]{2,1,0:T(8,128)(2,1)S(1)}, u32[]{:S(2)}, u32[]{:S(2)}) collective-permute-start(bf16[2,128,1024]{2,1,0:T(8,128)(2,1)S(1)} %get-tuple-element.328), channel_id=1, source_target_pairs={{0,8},{4,12},{8,0},{12,4},{1,9},{5,13},{9,1},{13,5},{2,10},{6,14},... | collective-permute-start | bytes 1572872 | tf_op jit(solution)/shard_map/ppermute | solution.py:394
  215.2 28.0 %collective-permute-start.62 = (bf16[2,128,1024]{2,1,0:T(8,128)(2,1)S(1)}, bf16[2,128,1024]{2,1,0:T(8,128)(2,1)S(1)}, u32[]{:S(2)}, u32[]{:S(2)}) collective-permute-start(bf16[2,128,1024]{2,1,0:T(8,128)(2,1)S(1)} %get-tuple-element.329), channel_id=1, source_target_pairs={{0,12},{4,8},{8,4},{12,0},{1,13},{5,9},{9,5},{13,1},{2,14},{6,10},... | collective-permute-start | bytes 1572872 | tf_op jit(solution)/shard_map/ppermute | solution.py:394
  221.9 15.4 %collective-permute-start.56 = (bf16[1,2,256,256]{3,2,1,0:T(8,128)(2,1)S(1)}, bf16[1,2,256,256]{3,2,1,0:T(8,128)(2,1)S(1)}, u32[]{:S(2)}, u32[]{:S(2)}) collective-permute-start(bf16[1,2,256,256]{3,2,1,0:T(8,128)(2,1)S(1)} %get-tuple-element.321.refs_0_), channel_id=1, source_target_pairs={{0,2},{1,3},{2,0},{3,1},{4,6},{5,7},{6,4},{7,5},{8,10},{9,11},{10,... | collective-permute-start | bytes 786440 | tf_op jit(solution)/shard_map/ppermute | solution.py:394
  256.3 25.7 %collective-permute-start.71 = (bf16[2,128,1024]{2,1,0:T(8,128)(2,1)}, bf16[2,128,1024]{2,1,0:T(8,128)(2,1)S(1)}, u32[]{:S(2)}, u32[]{:S(2)}) collective-permute-start(bf16[2,128,1024]{2,1,0:T(8,128)(2,1)} %get-tuple-element.348), channel_id=1, source_target_pairs={{0,8},{4,12},{8,0},{12,4},{1,9},{5,13},{9,1},{13,5},{2,10},{6,14},... | collective-permute-start | bytes 1572872 | tf_op jit(solution)/shard_map/ppermute | solution.py:394
  257.7 24.3 %collective-permute-start.72 = (bf16[2,128,1024]{2,1,0:T(8,128)(2,1)S(1)}, bf16[2,128,1024]{2,1,0:T(8,128)(2,1)S(1)}, u32[]{:S(2)}, u32[]{:S(2)}) collective-permute-start(bf16[2,128,1024]{2,1,0:T(8,128)(2,1)S(1)} %get-tuple-element.349), channel_id=1, source_target_pairs={{0,12},{4,8},{8,4},{12,0},{1,13},{5,9},{9,5},{13,1},{2,14},{6,10},... | collective-permute-start | bytes 1572872 | tf_op jit(solution)/shard_map/ppermute | solution.py:394
  (57 other events, 629.2 us)

commit v6 on v5

--- a/solution.py
+++ b/solution.py
@@ -86,7 +86,6 @@
         ],
         [((kc, rows, width), BF16, (1, rows, width), lambda i, p: (i, 0, 0))] * n,
         [],
-        vmem=60 * 1024 * 1024 if k0 == 0 else VMEM_LIMIT,
     )
 
 

time: 284 us -> 284 us (level)
  transfers between devices with their start and end apart: 74 -> 74, of which waited for: 39 -> 39; matrix products, arithmetic and copies ran while one was open for 1% -> 1% of each run, Pallas kernels for 10% -> 9%
where the time goes in v6:
time: 284 us
  waiting for transfers between devices  164 us (58%)
  starting transfers between devices  73.3 us (26%)
  Pallas kernels  39.6 us (14%)
  local copies, waits for them, and re-layouts  4.75 us (2%)
    ppermute x63, waiting for transfers between devices, swap(): return lax.ppermute(x, axis, [(i, i ^ m) for i in range(shape[axis])])  159 us
    ppermute x63, starting transfers between devices, swap(): return lax.ppermute(x, axis, [(i, i ^ m) for i in range(shape[axis])])  68.5 us
    pallas_call x20, Pallas kernels, call(): pl.pallas_call(body, grid_spec=pltpu.PrefetchScalarGridSpec(num_scalar_pr...  39.6 us
  transfers between devices with their start and end apart: 74, of which 39 were waited for; matrix products, arithmetic and copies ran while one was open for 1% of the time, Pallas kernels for 9%

profile of v6, /device:TPU:0, one launch (start us, length us, event | category | flops | bytes accessed | tf_op | source)
XLA Modules:
  0.0 283.8 jit_solution(9928013567371293115)
XLA Ops:
  1.6 3.0 %collective-permute-start = (bf16[3,128,256]{2,1,0:T(8,128)(2,1)S(1)}, bf16[3,128,256]{2,1,0:T(8,128)(2,1)S(1)}, u32[]{:S(2)}, u32[]{:S(2)}) collective-permute-start(bf16[3,128,256]{2,1,0:T(8,128)(2,1)S(1)} %constant_dynamic-slice_fusion), channel_id=1, source_target_pairs={{0,4},{4,0},{8,12},{12,8},{1,5},{5,1},{9,13},{13,9},{2,6},{6,2},{1... | collective-permute-start | bytes 589832 | tf_op jit(solution)/shard_map/ppermute | solution.py:393
  10.3 4.8 %collective-permute-done.1.refs_7_ = bf16[3,128,256]{2,1,0:T(8,128)(2,1)S(1)} collective-permute-done((bf16[3,128,256]{2,1,0:T(8,128)(2,1)S(1)}, bf16[3,128,256]{2,1,0:T(8,128)(2,1)S(1)}, u32[]{:S(2)}, u32[]{:S(2)}) %collective-permute-start.1) | collective-permute-done | bytes 196640 | tf_op jit(solution)/shard_map/ppermute | solution.py:393
  19.2 10.9 %collective-permute-done.3.refs_1_ = bf16[2,128,1024]{2,1,0:T(8,128)(2,1)S(1)} collective-permute-done((bf16[2,128,1024]{2,1,0:T(8,128)(2,1)S(1)}, bf16[2,128,1024]{2,1,0:T(8,128)(2,1)S(1)}, u32[]{:S(2)}, u32[]{:S(2)}) %collective-permute-start.3) | collective-permute-done | bytes 524320 | tf_op jit(solution)/shard_map/ppermute | solution.py:393
  30.9 9.2 %collective-permute-done.4.refs_2_ = bf16[2,128,1024]{2,1,0:T(8,128)(2,1)S(1)} collective-permute-done((bf16[2,128,1024]{2,1,0:T(8,128)(2,1)S(1)}, bf16[2,128,1024]{2,1,0:T(8,128)(2,1)S(1)}, u32[]{:S(2)}, u32[]{:S(2)}) %collective-permute-start.4) | collective-permute-done | bytes 524320 | tf_op jit(solution)/shard_map/ppermute | solution.py:393
  48.0 6.0 %collective-permute-done.9 = bf16[2,256,256]{2,1,0:T(8,128)(2,1)S(1)} collective-permute-done((bf16[2,256,256]{2,1,0:T(8,128)(2,1)S(1)}, bf16[2,256,256]{2,1,0:T(8,128)(2,1)S(1)}, u32[]{:S(2)}, u32[]{:S(2)}) %collective-permute-start.9) | collective-permute-done | bytes 262176 | tf_op jit(solution)/shard_map/ppermute | solution.py:393
  56.9 12.9 %collective-permute-done.11.refs_2_ = bf16[2,256,256]{2,1,0:T(8,128)(2,1)S(1)} collective-permute-done((bf16[2,256,256]{2,1,0:T(8,128)(2,1)S(1)}, bf16[2,256,256]{2,1,0:T(8,128)(2,1)S(1)}, u32[]{:S(2)}, u32[]{:S(2)}) %collective-permute-start.11) | collective-permute-done | bytes 262176 | tf_op jit(solution)/shard_map/ppermute | solution.py:393
  76.3 4.9 %collective-permute-done.15.refs_6_ = bf16[1,2,256,256]{3,2,1,0:T(8,128)(2,1)S(1)} collective-permute-done((bf16[1,2,256,256]{3,2,1,0:T(8,128)(2,1)S(1)}, bf16[1,2,256,256]{3,2,1,0:T(8,128)(2,1)S(1)}, u32[]{:S(2)}, u32[]{:S(2)}) %collective-permute-start.15) | collective-permute-done | bytes 262176 | tf_op jit(solution)/shard_map/ppermute | solution.py:393
  86.8 5.6 %collective-permute-done.17.refs_5_ = bf16[1,2,256,256]{3,2,1,0:T(8,128)(2,1)S(1)} collective-permute-done((bf16[1,2,256,256]{3,2,1,0:T(8,128)(2,1)S(1)}, bf16[1,2,256,256]{3,2,1,0:T(8,128)(2,1)S(1)}, u32[]{:S(2)}, u32[]{:S(2)}) %collective-permute-start.17) | collective-permute-done | bytes 262176 | tf_op jit(solution)/shard_map/ppermute | solution.py:393
  92.5 3.3 %collective-permute-done.18.refs_7_ = bf16[1,2,256,256]{3,2,1,0:T(8,128)(2,1)S(1)} collective-permute-done((bf16[1,2,256,256]{3,2,1,0:T(8,128)(2,1)S(1)}, bf16[1,2,256,256]{3,2,1,0:T(8,128)(2,1)S(1)}, u32[]{:S(2)}, u32[]{:S(2)}) %collective-permute-start.18) | collective-permute-done | bytes 262176 | tf_op jit(solution)/shard_map/ppermute | solution.py:393
  97.4 4.1 %collective-permute-done.19.refs_1_ = bf16[2,256,256]{2,1,0:T(8,128)(2,1)S(1)} collective-permute-done((bf16[2,256,256]{2,1,0:T(8,128)(2,1)S(1)}, bf16[2,256,256]{2,1,0:T(8,128)(2,1)S(1)}, u32[]{:S(2)}, u32[]{:S(2)}) %collective-permute-start.19) | collective-permute-done | bytes 262176 | tf_op jit(solution)/shard_map/ppermute | solution.py:393
  103.2 3.6 %collective-permute-done.20.refs_2_ = bf16[2,256,256]{2,1,0:T(8,128)(2,1)S(1)} collective-permute-done((bf16[2,256,256]{2,1,0:T(8,128)(2,1)S(1)}, bf16[2,256,256]{2,1,0:T(8,128)(2,1)S(1)}, u32[]{:S(2)}, u32[]{:S(2)}) %collective-permute-start.20) | collective-permute-done | bytes 262176 | tf_op jit(solution)/shard_map/ppermute | solution.py:393
  108.6 4.4 %collective-permute-done.24.refs_2_ = bf16[1,2,256,256]{3,2,1,0:T(8,128)(2,1)S(1)} collective-permute-done((bf16[1,2,256,256]{3,2,1,0:T(8,128)(2,1)S(1)}, bf16[1,2,256,256]{3,2,1,0:T(8,128)(2,1)S(1)}, u32[]{:S(2)}, u32[]{:S(2)}) %collective-permute-start.24) | collective-permute-done | bytes 262176 | tf_op jit(solution)/shard_map/ppermute | solution.py:393
  125.6 7.9 %collective-permute-done.25.refs_5_ = bf16[1,2,256,256]{3,2,1,0:T(8,128)(2,1)S(1)} collective-permute-done((bf16[1,2,256,256]{3,2,1,0:T(8,128)(2,1)S(1)}, bf16[1,2,256,256]{3,2,1,0:T(8,128)(2,1)S(1)}, u32[]{:S(2)}, u32[]{:S(2)}) %collective-permute-start.25) | collective-permute-done | bytes 262176 | tf_op jit(solution)/shard_map/ppermute | solution.py:393
  133.5 3.3 %collective-permute-done.27.refs_1_ = bf16[1,2,256,256]{3,2,1,0:T(8,128)(2,1)S(1)} collective-permute-done((bf16[1,2,256,256]{3,2,1,0:T(8,128)(2,1)S(1)}, bf16[1,2,256,256]{3,2,1,0:T(8,128)(2,1)S(1)}, u32[]{:S(2)}, u32[]{:S(2)}) %collective-permute-start.27) | collective-permute-done | bytes 262176 | tf_op jit(solution)/shard_map/ppermute | solution.py:393
  140.3 8.1 %collective-permute-done.31.refs_2_ = bf16[2,256,256]{2,1,0:T(8,128)(2,1)S(1)} collective-permute-done((bf16[2,256,256]{2,1,0:T(8,128)(2,1)S(1)}, bf16[2,256,256]{2,1,0:T(8,128)(2,1)S(1)}, u32[]{:S(2)}, u32[]{:S(2)}) %collective-permute-start.31) | collective-permute-done | bytes 262176 | tf_op jit(solution)/shard_map/ppermute | solution.py:393
  161.8 3.1 %collective-permute-done.35.refs_7_ = bf16[1,2,256,256]{3,2,1,0:T(8,128)(2,1)S(1)} collective-permute-done((bf16[1,2,256,256]{3,2,1,0:T(8,128)(2,1)S(1)}, bf16[1,2,256,256]{3,2,1,0:T(8,128)(2,1)S(1)}, u32[]{:S(2)}, u32[]{:S(2)}) %collective-permute-start.35) | collective-permute-done | bytes 262176 | tf_op jit(solution)/shard_map/ppermute | solution.py:472
  182.9 3.3 %collective-permute-done.42.refs_2_ = bf16[1,2,256,256]{3,2,1,0:T(8,128)(2,1)S(1)} collective-permute-done((bf16[1,2,256,256]{3,2,1,0:T(8,128)(2,1)S(1)}, bf16[1,2,256,256]{3,2,1,0:T(8,128)(2,1)S(1)}, u32[]{:S(2)}, u32[]{:S(2)}) %collective-permute-start.42) | collective-permute-done | bytes 262176 | tf_op jit(solution)/shard_map/ppermute | solution.py:393
  191.3 3.1 %collective-permute-done.49.refs_3_ = bf16[1,2,256,256]{3,2,1,0:T(8,128)(2,1)S(1)} collective-permute-done((bf16[1,2,256,256]{3,2,1,0:T(8,128)(2,1)S(1)}, bf16[1,2,256,256]{3,2,1,0:T(8,128)(2,1)S(1)}, u32[]{:S(2)}, u32[]{:S(2)}) %collective-permute-start.49) | collective-permute-done | bytes 262176 | tf_op jit(solution)/shard_map/ppermute | solution.py:393
  217.1 3.2 %collective-permute-done.58 = f32[3,64,256]{2,1,0:T(8,128)S(1)} collective-permute-done((f32[3,64,256]{2,1,0:T(8,128)S(1)}, f32[3,64,256]{2,1,0:T(8,128)S(1)}, u32[]{:S(2)}, u32[]{:S(2)}) %collective-permute-start.58) | collective-permute-done | bytes 196640 | tf_op jit(solution)/shard_map/ppermute | solution.py:393
  222.8 4.8 %collective-permute-done.63 = f32[3,64,256]{2,1,0:T(8,128)S(1)} collective-permute-done((f32[3,64,256]{2,1,0:T(8,128)S(1)}, f32[3,64,256]{2,1,0:T(8,128)S(1)}, u32[]{:S(2)}, u32[]{:S(2)}) %collective-permute-start.63) | collective-permute-done | bytes 196640 | tf_op jit(solution)/shard_map/ppermute | solution.py:393
  229.4 7.7 %collective-permute-done.56.refs_2_ = bf16[1,2,256,256]{3,2,1,0:T(8,128)(2,1)S(1)} collective-permute-done((bf16[1,2,256,256]{3,2,1,0:T(8,128)(2,1)S(1)}, bf16[1,2,256,256]{3,2,1,0:T(8,128)(2,1)S(1)}, u32[]{:S(2)}, u32[]{:S(2)}) %collective-permute-start.56) | collective-permute-done | bytes 262176 | tf_op jit(solution)/shard_map/ppermute | solution.py:393
  250.8 5.2 %shard_map.93 = bf16[3,128,256]{2,1,0:T(8,128)(2,1)S(1)} custom-call(s32[3]{0:T(128)S(1)} %pad_add_fusion.place_ref, f32[3,64,256]{2,1,0:T(8,128)S(1)} %add.47.refs_0_, f32[3,64,256]{2,1,0:T(8,128)S(1)} %collective-permute-done.67.refs_1_, f32[3,64,256]{2,1,0:T(8,128)S(1)} %collective-permute-done.68.refs_2_, ...), custom_call_target="tpu_custom_call" | custom-call | flops 1 | bytes 1 | tf_op jit(solution)/shard_map/pallas_call | solution.py:51
  260.5 10.6 %collective-permute-done.70.refs_1_ = bf16[2,128,1024]{2,1,0:T(8,128)(2,1)S(1)} collective-permute-done((bf16[2,128,1024]{2,1,0:T(8,128)(2,1)}, bf16[2,128,1024]{2,1,0:T(8,128)(2,1)S(1)}, u32[]{:S(2)}, u32[]{:S(2)}) %collective-permute-start.70) | collective-permute-done | bytes 524320 | tf_op jit(solution)/shard_map/ppermute | solution.py:393
  271.1 10.8 %collective-permute-done.71.refs_2_ = bf16[2,128,1024]{2,1,0:T(8,128)(2,1)S(1)} collective-permute-done((bf16[2,128,1024]{2,1,0:T(8,128)(2,1)}, bf16[2,128,1024]{2,1,0:T(8,128)(2,1)S(1)}, u32[]{:S(2)}, u32[]{:S(2)}) %collective-permute-start.71) | collective-permute-done | bytes 524320 | tf_op jit(solution)/shard_map/ppermute | solution.py:393
  (177 shorter events, 138.9 us)
Async XLA Ops:
  16.4 23.7 %collective-permute-start.4 = (bf16[2,128,1024]{2,1,0:T(8,128)(2,1)S(1)}, bf16[2,128,1024]{2,1,0:T(8,128)(2,1)S(1)}, u32[]{:S(2)}, u32[]{:S(2)}) collective-permute-start(bf16[2,128,1024]{2,1,0:T(8,128)(2,1)S(1)} %get-tuple-element.191), channel_id=1, source_target_pairs={{0,8},{4,12},{8,0},{12,4},{1,9},{5,13},{9,1},{13,5},{2,10},{6,14},... | collective-permute-start | bytes 1572872 | tf_op jit(solution)/shard_map/ppermute | solution.py:393
  17.2 22.9 %collective-permute-start.5 = (bf16[2,128,1024]{2,1,0:T(8,128)(2,1)S(1)}, bf16[2,128,1024]{2,1,0:T(8,128)(2,1)S(1)}, u32[]{:S(2)}, u32[]{:S(2)}) collective-permute-start(bf16[2,128,1024]{2,1,0:T(8,128)(2,1)S(1)} %get-tuple-element.192), channel_id=1, source_target_pairs={{0,12},{4,8},{8,4},{12,0},{1,13},{5,9},{9,5},{13,1},{2,14},{6,10},... | collective-permute-start | bytes 1572872 | tf_op jit(solution)/shard_map/ppermute | solution.py:393
  18.7 21.5 %collective-permute-start.6 = (bf16[3,128,256]{2,1,0:T(8,128)(2,1)S(1)}, bf16[3,128,256]{2,1,0:T(8,128)(2,1)S(1)}, u32[]{:S(2)}, u32[]{:S(2)}) collective-permute-start(bf16[3,128,256]{2,1,0:T(8,128)(2,1)S(1)} %collective-permute-done.refs_5_), channel_id=1, source_target_pairs={{0,16},{16,0},{1,17},{17,1},{2,18},{18,2},{3,19},{19,3},{4,20},{20... | collective-permute-start | bytes 589832 | tf_op jit(solution)/shard_map/ppermute | solution.py:406
  18.7 21.5 %collective-permute-start.7 = (bf16[3,128,256]{2,1,0:T(8,128)(2,1)S(1)}, bf16[3,128,256]{2,1,0:T(8,128)(2,1)S(1)}, u32[]{:S(2)}, u32[]{:S(2)}) collective-permute-start(bf16[3,128,256]{2,1,0:T(8,128)(2,1)S(1)} %collective-permute-done.1.refs_7_), channel_id=1, source_target_pairs={{0,16},{16,0},{1,17},{17,1},{2,18},{18,2},{3,19},{19,3},{4,20},{20... | collective-permute-start | bytes 589832 | tf_op jit(solution)/shard_map/ppermute | solution.py:406
  44.1 27.5 %collective-permute-start.12 = (bf16[2,128,1024]{2,1,0:T(8,128)(2,1)S(1)}, bf16[2,128,1024]{2,1,0:T(8,128)(2,1)S(1)}, u32[]{:S(2)}, u32[]{:S(2)}) collective-permute-start(bf16[2,128,1024]{2,1,0:T(8,128)(2,1)S(1)} %get-tuple-element.214), channel_id=1, source_target_pairs={{0,4},{4,0},{8,12},{12,8},{1,5},{5,1},{9,13},{13,9},{2,6},{6,2},{1... | collective-permute-start | bytes 1572872 | tf_op jit(solution)/shard_map/ppermute | solution.py:393
  44.7 26.9 %collective-permute-start.13 = (bf16[2,128,1024]{2,1,0:T(8,128)(2,1)S(1)}, bf16[2,128,1024]{2,1,0:T(8,128)(2,1)S(1)}, u32[]{:S(2)}, u32[]{:S(2)}) collective-permute-start(bf16[2,128,1024]{2,1,0:T(8,128)(2,1)S(1)} %get-tuple-element.215), channel_id=1, source_target_pairs={{0,8},{4,12},{8,0},{12,4},{1,9},{5,13},{9,1},{13,5},{2,10},{6,14},... | collective-permute-start | bytes 1572872 | tf_op jit(solution)/shard_map/ppermute | solution.py:393
  45.8 25.8 %collective-permute-start.14 = (bf16[2,128,1024]{2,1,0:T(8,128)(2,1)S(1)}, bf16[2,128,1024]{2,1,0:T(8,128)(2,1)S(1)}, u32[]{:S(2)}, u32[]{:S(2)}) collective-permute-start(bf16[2,128,1024]{2,1,0:T(8,128)(2,1)S(1)} %get-tuple-element.216), channel_id=1, source_target_pairs={{0,12},{4,8},{8,4},{12,0},{1,13},{5,9},{9,5},{13,1},{2,14},{6,10},... | collective-permute-start | bytes 1572872 | tf_op jit(solution)/shard_map/ppermute | solution.py:393
  54.2 15.6 %collective-permute-start.11 = (bf16[2,256,256]{2,1,0:T(8,128)(2,1)S(1)}, bf16[2,256,256]{2,1,0:T(8,128)(2,1)S(1)}, u32[]{:S(2)}, u32[]{:S(2)}) collective-permute-start(bf16[2,256,256]{2,1,0:T(8,128)(2,1)S(1)} %add_convert_fusion.2), channel_id=1, source_target_pairs={{0,2},{1,3},{2,0},{3,1},{4,6},{5,7},{6,4},{7,5},{8,10},{9,11},{10,... | collective-permute-start | bytes 786440 | tf_op jit(solution)/shard_map/ppermute | solution.py:393
  76.2 16.2 %collective-permute-start.17 = (bf16[1,2,256,256]{3,2,1,0:T(8,128)(2,1)S(1)}, bf16[1,2,256,256]{3,2,1,0:T(8,128)(2,1)S(1)}, u32[]{:S(2)}, u32[]{:S(2)}) collective-permute-start(bf16[1,2,256,256]{3,2,1,0:T(8,128)(2,1)S(1)} %get-tuple-element.227.refs_4_), channel_id=1, source_target_pairs={{0,1},{1,0},{2,3},{3,2},{4,5},{5,4},{6,7},{7,6},{8,9},{9,8},{10,11... | collective-permute-start | bytes 786440 | tf_op jit(solution)/shard_map/ppermute | solution.py:393
  81.2 27.5 %collective-permute-start.21 = (bf16[2,128,1024]{2,1,0:T(8,128)(2,1)S(1)}, bf16[2,128,1024]{2,1,0:T(8,128)(2,1)S(1)}, u32[]{:S(2)}, u32[]{:S(2)}) collective-permute-start(bf16[2,128,1024]{2,1,0:T(8,128)(2,1)S(1)} %get-tuple-element.239), channel_id=1, source_target_pairs={{0,4},{4,0},{8,12},{12,8},{1,5},{5,1},{9,13},{13,9},{2,6},{6,2},{1... | collective-permute-start | bytes 1572872 | tf_op jit(solution)/shard_map/ppermute | solution.py:393
  82.1 26.5 %collective-permute-start.22 = (bf16[2,128,1024]{2,1,0:T(8,128)(2,1)S(1)}, bf16[2,128,1024]{2,1,0:T(8,128)(2,1)S(1)}, u32[]{:S(2)}, u32[]{:S(2)}) collective-permute-start(bf16[2,128,1024]{2,1,0:T(8,128)(2,1)S(1)} %get-tuple-element.240), channel_id=1, source_target_pairs={{0,8},{4,12},{8,0},{12,4},{1,9},{5,13},{9,1},{13,5},{2,10},{6,14},... | collective-permute-start | bytes 1572872 | tf_op jit(solution)/shard_map/ppermute | solution.py:393
  85.4 23.3 %collective-permute-start.23 = (bf16[2,128,1024]{2,1,0:T(8,128)(2,1)S(1)}, bf16[2,128,1024]{2,1,0:T(8,128)(2,1)S(1)}, u32[]{:S(2)}, u32[]{:S(2)}) collective-permute-start(bf16[2,128,1024]{2,1,0:T(8,128)(2,1)S(1)} %get-tuple-element.241), channel_id=1, source_target_pairs={{0,12},{4,8},{8,4},{12,0},{1,13},{5,9},{9,5},{13,1},{2,14},{6,10},... | collective-permute-start | bytes 1572872 | tf_op jit(solution)/shard_map/ppermute | solution.py:393
  117.4 16.0 %collective-permute-start.25 = (bf16[1,2,256,256]{3,2,1,0:T(8,128)(2,1)S(1)}, bf16[1,2,256,256]{3,2,1,0:T(8,128)(2,1)S(1)}, u32[]{:S(2)}, u32[]{:S(2)}) collective-permute-start(bf16[1,2,256,256]{3,2,1,0:T(8,128)(2,1)S(1)} %get-tuple-element.250.refs_4_), channel_id=1, source_target_pairs={{0,1},{1,0},{2,3},{3,2},{4,5},{5,4},{6,7},{7,6},{8,9},{9,8},{10,11... | collective-permute-start | bytes 786440 | tf_op jit(solution)/shard_map/ppermute | solution.py:393
  117.5 19.3 %collective-permute-start.27 = (bf16[1,2,256,256]{3,2,1,0:T(8,128)(2,1)S(1)}, bf16[1,2,256,256]{3,2,1,0:T(8,128)(2,1)S(1)}, u32[]{:S(2)}, u32[]{:S(2)}) collective-permute-start(bf16[1,2,256,256]{3,2,1,0:T(8,128)(2,1)S(1)} %get-tuple-element.254.refs_0_), channel_id=1, source_target_pairs={{0,1},{1,0},{2,3},{3,2},{4,5},{5,4},{6,7},{7,6},{8,9},{9,8},{10,11... | collective-permute-start | bytes 786440 | tf_op jit(solution)/shard_map/ppermute | solution.py:393
  119.5 20.3 %collective-permute-start.29 = (bf16[1,2,256,256]{3,2,1,0:T(8,128)(2,1)S(1)}, bf16[1,2,256,256]{3,2,1,0:T(8,128)(2,1)S(1)}, u32[]{:S(2)}, u32[]{:S(2)}) collective-permute-start(bf16[1,2,256,256]{3,2,1,0:T(8,128)(2,1)S(1)} %get-tuple-element.250.refs_4_), channel_id=1, source_target_pairs={{1,2},{2,1},{5,6},{6,5},{9,10},{10,9},{13,14},{14,13},{17,18},{18,... | collective-permute-start | bytes 786440 | tf_op jit(solution)/shard_map/ppermute | solution.py:472
  122.7 32.7 %collective-permute-start.34 = (f32[1,4,128,256]{3,2,1,0:T(8,128)S(1)}, f32[1,4,128,256]{3,2,1,0:T(8,128)S(1)}, u32[]{:S(2)}, u32[]{:S(2)}) collective-permute-start(f32[1,4,128,256]{3,2,1,0:T(8,128)S(1)} %slice.72), channel_id=1, source_target_pairs={{0,16},{16,0},{1,17},{17,1},{2,18},{18,2},{3,19},{19,3},{4,20},{20... | collective-permute-start | bytes 1572872 | tf_op jit(solution)/shard_map/ppermute | solution.py:406
  155.4 16.4 %collective-permute-start.37 = (bf16[1,2,256,256]{3,2,1,0:T(8,128)(2,1)S(1)}, bf16[1,2,256,256]{3,2,1,0:T(8,128)(2,1)S(1)}, u32[]{:S(2)}, u32[]{:S(2)}) collective-permute-start(bf16[1,2,256,256]{3,2,1,0:T(8,128)(2,1)S(1)} %get-tuple-element.281.refs_4_), channel_id=1, source_target_pairs={{0,1},{1,0},{2,3},{3,2},{4,5},{5,4},{6,7},{7,6},{8,9},{9,8},{10,11... | collective-permute-start | bytes 786440 | tf_op jit(solution)/shard_map/ppermute | solution.py:393
  210.7 28.6 %collective-permute-start.60 = (bf16[2,128,1024]{2,1,0:T(8,128)(2,1)S(1)}, bf16[2,128,1024]{2,1,0:T(8,128)(2,1)S(1)}, u32[]{:S(2)}, u32[]{:S(2)}) collective-permute-start(bf16[2,128,1024]{2,1,0:T(8,128)(2,1)S(1)} %get-tuple-element.327), channel_id=1, source_target_pairs={{0,4},{4,0},{8,12},{12,8},{1,5},{5,1},{9,13},{13,9},{2,6},{6,2},{1... | collective-permute-start | bytes 1572872 | tf_op jit(solution)/shard_map/ppermute | solution.py:393
  212.2 28.2 %collective-permute-start.61 = (bf16[2,128,1024]{2,1,0:T(8,128)(2,1)S(1)}, bf16[2,128,1024]{2,1,0:T(8,128)(2,1)S(1)}, u32[]{:S(2)}, u32[]{:S(2)}) collective-permute-start(bf16[2,128,1024]{2,1,0:T(8,128)(2,1)S(1)} %get-tuple-element.328), channel_id=1, source_target_pairs={{0,8},{4,12},{8,0},{12,4},{1,9},{5,13},{9,1},{13,5},{2,10},{6,14},... | collective-permute-start | bytes 1572872 | tf_op jit(solution)/shard_map/ppermute | solution.py:393
  215.0 28.0 %collective-permute-start.62 = (bf16[2,128,1024]{2,1,0:T(8,128)(2,1)S(1)}, bf16[2,128,1024]{2,1,0:T(8,128)(2,1)S(1)}, u32[]{:S(2)}, u32[]{:S(2)}) collective-permute-start(bf16[2,128,1024]{2,1,0:T(8,128)(2,1)S(1)} %get-tuple-element.329), channel_id=1, source_target_pairs={{0,12},{4,8},{8,4},{12,0},{1,13},{5,9},{9,5},{13,1},{2,14},{6,10},... | collective-permute-start | bytes 1572872 | tf_op jit(solution)/shard_map/ppermute | solution.py:393
  221.7 15.4 %collective-permute-start.56 = (bf16[1,2,256,256]{3,2,1,0:T(8,128)(2,1)S(1)}, bf16[1,2,256,256]{3,2,1,0:T(8,128)(2,1)S(1)}, u32[]{:S(2)}, u32[]{:S(2)}) collective-permute-start(bf16[1,2,256,256]{3,2,1,0:T(8,128)(2,1)S(1)} %get-tuple-element.321.refs_0_), channel_id=1, source_target_pairs={{0,2},{1,3},{2,0},{3,1},{4,6},{5,7},{6,4},{7,5},{8,10},{9,11},{10,... | collective-permute-start | bytes 786440 | tf_op jit(solution)/shard_map/ppermute | solution.py:393
  256.1 15.0 %collective-permute-start.70 = (bf16[2,128,1024]{2,1,0:T(8,128)(2,1)}, bf16[2,128,1024]{2,1,0:T(8,128)(2,1)S(1)}, u32[]{:S(2)}, u32[]{:S(2)}) collective-permute-start(bf16[2,128,1024]{2,1,0:T(8,128)(2,1)} %get-tuple-element.347), channel_id=1, source_target_pairs={{0,4},{4,0},{8,12},{12,8},{1,5},{5,1},{9,13},{13,9},{2,6},{6,2},{1... | collective-permute-start | bytes 1572872 | tf_op jit(solution)/shard_map/ppermute | solution.py:393
  256.1 25.7 %collective-permute-start.71 = (bf16[2,128,1024]{2,1,0:T(8,128)(2,1)}, bf16[2,128,1024]{2,1,0:T(8,128)(2,1)S(1)}, u32[]{:S(2)}, u32[]{:S(2)}) collective-permute-start(bf16[2,128,1024]{2,1,0:T(8,128)(2,1)} %get-tuple-element.348), channel_id=1, source_target_pairs={{0,8},{4,12},{8,0},{12,4},{1,9},{5,13},{9,1},{13,5},{2,10},{6,14},... | collective-permute-start | bytes 1572872 | tf_op jit(solution)/shard_map/ppermute | solution.py:393
  257.6 24.3 %collective-permute-start.72 = (bf16[2,128,1024]{2,1,0:T(8,128)(2,1)S(1)}, bf16[2,128,1024]{2,1,0:T(8,128)(2,1)S(1)}, u32[]{:S(2)}, u32[]{:S(2)}) collective-permute-start(bf16[2,128,1024]{2,1,0:T(8,128)(2,1)S(1)} %get-tuple-element.349), channel_id=1, source_target_pairs={{0,12},{4,8},{8,4},{12,0},{1,13},{5,9},{9,5},{13,1},{2,14},{6,10},... | collective-permute-start | bytes 1572872 | tf_op jit(solution)/shard_map/ppermute | solution.py:393
  (56 other events, 621.1 us)
